TPU v7x, 32 devices: a whole 2x2x4 slice. The times are simulated.
32 devices in a mesh: group: 4 (over y, x), replica: 8 (over z, core).
Axes of the slice: x: 2, y: 2, z: 4, core: 2. Of those that a mesh axis runs over, the one named last changes fastest.
Arguments:
- tokens: bfloat16 [8, 512, 2048], P('replica', 'group'), may hold values from -6 to 6
- seq_lengths: int32 [8, 5], P('replica'), may hold values from 1 to 384, as said below
- attn_gain: bfloat16 [2048], P('group'), may hold values from 0.5 to 1.5
- w_query: bfloat16 [2048, 2048], P('group'), may hold values from -0.125 to 0.125
- w_key: bfloat16 [2048, 512], P('group'), may hold values from -0.125 to 0.125
- w_value: bfloat16 [2048, 512], P('group'), may hold values from -0.125 to 0.125
- w_out: bfloat16 [2048, 2048], P('group'), may hold values from -0.5 to 0.5
- mlp_gain: bfloat16 [2048], P('group'), may hold values from 0.5 to 1.5
- w_gate: bfloat16 [2048, 8192], P('group'), may hold values from -0.125 to 0.125
- w_up: bfloat16 [2048, 8192], P('group'), may hold values from -0.125 to 0.125
- w_down: bfloat16 [8192, 2048], P('group'), may hold values from -0.125 to 0.125
- cotangent: bfloat16 [8, 512, 2048], P('replica', 'group'), may hold values from -6 to 6
Outputs:
- output: bfloat16 [8, 512, 2048], P('replica', 'group')
- grad_tokens: bfloat16 [8, 512, 2048], P('replica', 'group')
- grad_attn_gain: float32 [2048], P('group')
- grad_query: float32 [2048, 2048], P('group')
- grad_key: float32 [2048, 512], P('group')
- grad_value: float32 [2048, 512], P('group')
- grad_out: float32 [2048, 2048], P('group')
- grad_mlp_gain: float32 [2048], P('group')
- grad_gate: float32 [2048, 8192], P('group')
- grad_up: float32 [2048, 8192], P('group')
- grad_down: float32 [8192, 2048], P('group')
Inputs may be any that keep to these rules, and one draw needn't show every extreme that they name: `seq_lengths`: each row holds a prompt length from 256 to 384 followed by 4 continuation lengths of one or more; a row sums to 512; in some row the prompt has exactly 384 tokens.
All inputs are finite; a program needn't handle non-finite values.
Results may differ from a plain program's by a relative error of at most 0.024.
Values may be sent and summed in bfloat16 or wider, within the bound.
No kernel may reach another device: no remote copies, remote signals or barrier semaphores. Data moves between devices by JAX's collectives and lax.ppermute only.
A program may use at most 384 MiB of HBM per device.

v0:
```python
import jax
import jax.numpy as jnp
from jax import lax
from jax.sharding import PartitionSpec as P

HQ = 32
HK = 8
HEAD = 64


EPS = 1e-05
BASE = 500000.0
MASKED = -1e30


def positions_of(lengths, total):
    ends = jnp.cumsum(lengths)
    starts = ends - lengths
    index = jnp.arange(total, dtype=jnp.int32)
    segment = jnp.sum((index[:, None] >= ends[None, :-1]).astype(jnp.int32), axis=1)
    member = segment[:, None] == jnp.arange(lengths.shape[0], dtype=jnp.int32)[None, :]
    start = jnp.sum(jnp.where(member, starts[None, :], 0), axis=1)
    place = jnp.where(segment == 0, index, lengths[0] + index - start)
    return (segment, place)


def allowed_of(seg_query, place_query, seg_key, place_key):
    same = (seg_key[None, :] == 0) | (seg_key[None, :] == seg_query[:, None])
    return same & (place_key[None, :] <= place_query[:, None])


def rope_tables(place, size):
    half = size // 2
    freq = BASE ** (-(2.0 * jnp.arange(half, dtype=jnp.float32)) / size)
    angle = place.astype(jnp.float32)[:, None] * freq[None, :]
    return (jnp.cos(angle)[:, None, :], jnp.sin(angle)[:, None, :])


def rotate(value, cosine, sine):
    half = value.shape[-1] // 2
    first, second = (value[..., :half], value[..., half:])
    return jnp.concatenate(
        [first * cosine - second * sine, second * cosine + first * sine], axis=-1
    )


def rotate_back(grad, cosine, sine):
    half = grad.shape[-1] // 2
    first, second = (grad[..., :half], grad[..., half:])
    return jnp.concatenate(
        [first * cosine + second * sine, second * cosine - first * sine], axis=-1
    )


def matmul(left, right):
    return jnp.dot(left, right, preferred_element_type=jnp.float32)


def contract_last(left, right):
    return lax.dot_general(
        left, right, (((1,), (1,)), ((), ())), preferred_element_type=jnp.float32
    )


def contract_first(left, right):
    return lax.dot_general(
        left, right, (((0,), (0,)), ((), ())), preferred_element_type=jnp.float32
    )


def to_heads(value, total):
    return value.reshape(total, HK, HEAD).transpose(1, 0, 2)


def norm_back(grad_normed, unit, inverse, gain):
    scaled = grad_normed * gain
    return inverse * (scaled - unit * jnp.mean(scaled * unit, axis=1, keepdims=True))


def body(
    tokens,
    seq_lengths,
    attn_gain,
    w_query,
    w_key,
    w_value,
    w_out,
    mlp_gain,
    w_gate,
    w_up,
    w_down,
    cotangent,
):
    x = tokens[0].astype(jnp.float32)
    rows = x.shape[0]
    parts = lax.axis_size("group")
    total = rows * parts
    member_index = lax.axis_index("group")
    begin = member_index * rows
    groups = HQ // HK
    scale = HEAD ** (-0.5)
    segment, place = positions_of(seq_lengths[0], total)
    seg_mine = lax.dynamic_slice_in_dim(segment, begin, rows)
    place_mine = lax.dynamic_slice_in_dim(place, begin, rows)
    allowed_rows = jnp.tile(allowed_of(seg_mine, place_mine, segment, place), (groups, 1))
    cosine, sine = rope_tables(place_mine, HEAD)
    gain_one, query_full, key_full, value_full, out_full = (
        lax.all_gather(attn_gain, "group", axis=0, tiled=True),
        lax.all_gather(w_query, "group", axis=0, tiled=True),
        lax.all_gather(w_key, "group", axis=0, tiled=True),
        lax.all_gather(w_value, "group", axis=0, tiled=True),
        lax.all_gather(w_out, "group", axis=0, tiled=True),
    )
    gain_one = gain_one.astype(jnp.float32)
    inverse_one = lax.rsqrt(jnp.mean(x * x, axis=1, keepdims=True) + EPS)
    unit_one = x * inverse_one
    normed_one = (unit_one * gain_one).astype(jnp.bfloat16)
    query_pre = matmul(normed_one, query_full)
    key_pre = matmul(normed_one, key_full)
    value_mine = matmul(normed_one, value_full).astype(jnp.bfloat16)
    query = rotate(query_pre.reshape(rows, HQ, HEAD), cosine, sine).astype(jnp.bfloat16)
    key_mine = (
        rotate(key_pre.reshape(rows, HK, HEAD), cosine, sine)
        .astype(jnp.bfloat16)
        .reshape(rows, HK * HEAD)
    )
    keys_all, values_all = (
        lax.all_gather(key_mine, "group", axis=0, tiled=True),
        lax.all_gather(value_mine, "group", axis=0, tiled=True),
    )
    query_heads = (
        query.reshape(rows, HK, groups, HEAD).transpose(1, 2, 0, 3).reshape(HK, groups * rows, HEAD)
    )
    key_heads = to_heads(keys_all, total)
    value_heads = to_heads(values_all, total)

    def head_forward(args):
        q_head, k_head, v_head = args
        scores = jnp.where(allowed_rows, contract_last(q_head, k_head) * scale, MASKED)
        top = jnp.max(scores, axis=1, keepdims=True)
        expo = jnp.exp(scores - top)
        denom = jnp.sum(expo, axis=1, keepdims=True)
        probs = (expo / denom).astype(jnp.bfloat16)
        return (matmul(probs, v_head), top[:, 0] + jnp.log(denom[:, 0]))

    attended, logsum = lax.map(head_forward, (query_heads, key_heads, value_heads))
    attended = (
        attended.reshape(HK, groups, rows, HEAD)
        .transpose(2, 0, 1, 3)
        .reshape(rows, HQ * HEAD)
        .astype(jnp.bfloat16)
    )
    mid = x + matmul(attended, out_full)
    gain_two, gate_full, up_full, down_full = (
        lax.all_gather(mlp_gain, "group", axis=0, tiled=True),
        lax.all_gather(w_gate, "group", axis=0, tiled=True),
        lax.all_gather(w_up, "group", axis=0, tiled=True),
        lax.all_gather(w_down, "group", axis=0, tiled=True),
    )
    gain_two = gain_two.astype(jnp.float32)
    inverse_two = lax.rsqrt(jnp.mean(mid * mid, axis=1, keepdims=True) + EPS)
    unit_two = mid * inverse_two
    normed_two = (unit_two * gain_two).astype(jnp.bfloat16)
    gate = matmul(normed_two, gate_full)
    up = matmul(normed_two, up_full)
    sigma = jax.nn.sigmoid(gate)
    active = (gate * sigma * up).astype(jnp.bfloat16)
    result = mid + matmul(active, down_full)
    grad_y = cotangent[0].astype(jnp.float32)
    grad_m = grad_y.astype(jnp.bfloat16)
    grad_active = contract_last(grad_m, down_full)
    width = gate.shape[1]
    grad_gate_up = jnp.concatenate(
        [
            (grad_active * up * sigma * (1.0 + gate * (1.0 - sigma))).astype(jnp.bfloat16),
            (grad_active * gate * sigma).astype(jnp.bfloat16),
        ],
        axis=1,
    )
    grad_normed_two = contract_last(grad_gate_up[:, :width], gate_full) + contract_last(
        grad_gate_up[:, width:], up_full
    )
    down_share = w_down.shape[0]
    gate_share = w_gate.shape[0]
    down_begin = member_index * down_share
    gate_begin = member_index * gate_share
    pieces = (
        lax.all_gather(active, "group", axis=0, tiled=True),
        lax.all_gather(grad_m, "group", axis=0, tiled=True),
    )
    grad_down = contract_first(
        lax.dynamic_slice_in_dim(pieces[0], down_begin, down_share, 1), pieces[1]
    )
    pieces = (
        lax.all_gather(normed_two, "group", axis=0, tiled=True),
        lax.all_gather(grad_gate_up, "group", axis=0, tiled=True),
    )
    both_rows = contract_first(
        lax.dynamic_slice_in_dim(pieces[0], gate_begin, gate_share, 1), pieces[1]
    )
    grad_gate = both_rows[:, :width]
    grad_up = both_rows[:, width:]
    grad_gain_two = jnp.sum(grad_normed_two * unit_two, axis=0)
    grad_mid = grad_y + norm_back(grad_normed_two, unit_two, inverse_two, gain_two)
    grad_branch = grad_mid.astype(jnp.bfloat16)
    grad_out_local = contract_first(attended, grad_branch)
    grad_attended = contract_last(grad_branch, out_full).astype(jnp.bfloat16)
    grad_heads = (
        grad_attended.reshape(rows, HK, groups, HEAD)
        .transpose(1, 2, 0, 3)
        .reshape(HK, groups * rows, HEAD)
    )

    def head_backward(args):
        q_head, k_head, v_head, g_head, l_head = args
        scores = jnp.where(allowed_rows, contract_last(q_head, k_head) * scale, MASKED)
        probs = jnp.exp(scores - l_head[:, None])
        grad_p = contract_last(g_head, v_head)
        grad_s = (probs * (grad_p - jnp.sum(probs * grad_p, axis=1, keepdims=True))).astype(
            jnp.bfloat16
        )
        return (
            matmul(grad_s, k_head) * scale,
            contract_first(grad_s, q_head) * scale,
            contract_first(probs.astype(jnp.bfloat16), g_head),
        )

    grad_q, grad_k, grad_v = lax.map(
        head_backward, (query_heads, key_heads, value_heads, grad_heads, logsum)
    )
    grad_q = grad_q.reshape(HK, groups, rows, HEAD).transpose(2, 0, 1, 3).reshape(rows, HQ, HEAD)
    grad_k = grad_k.transpose(1, 0, 2).reshape(total, HK * HEAD)
    grad_v = grad_v.transpose(1, 0, 2).reshape(total, HK * HEAD)
    grad_k_mine, grad_v_mine = (
        lax.psum_scatter(
            grad_k.astype(jnp.bfloat16), "group", scatter_dimension=0, tiled=True
        ).astype(jnp.float32),
        lax.psum_scatter(
            grad_v.astype(jnp.bfloat16), "group", scatter_dimension=0, tiled=True
        ).astype(jnp.float32),
    )
    grad_query_pre = rotate_back(grad_q, cosine, sine).reshape(rows, HQ * HEAD).astype(jnp.bfloat16)
    grad_key_pre = (
        rotate_back(grad_k_mine.reshape(rows, HK, HEAD), cosine, sine)
        .reshape(rows, HK * HEAD)
        .astype(jnp.bfloat16)
    )
    grad_value_pre = grad_v_mine.astype(jnp.bfloat16)
    grad_normed_one = (
        contract_last(grad_query_pre, query_full)
        + contract_last(grad_key_pre, key_full)
        + contract_last(grad_value_pre, value_full)
    )
    grad_gain_one = jnp.sum(grad_normed_one * unit_one, axis=0)
    grad_x = grad_mid + norm_back(grad_normed_one, unit_one, inverse_one, gain_one)
    grad_query_local = contract_first(normed_one, grad_query_pre)
    grad_key_local = contract_first(normed_one, grad_key_pre)
    grad_value_local = contract_first(normed_one, grad_value_pre)
    gain_one_rows, query_rows, key_rows, value_rows, out_rows, gain_two_rows = (
        lax.psum_scatter(
            grad_gain_one.astype(jnp.bfloat16), "group", scatter_dimension=0, tiled=True
        ).astype(jnp.float32),
        lax.psum_scatter(
            grad_query_local.astype(jnp.bfloat16), "group", scatter_dimension=0, tiled=True
        ).astype(jnp.float32),
        lax.psum_scatter(
            grad_key_local.astype(jnp.bfloat16), "group", scatter_dimension=0, tiled=True
        ).astype(jnp.float32),
        lax.psum_scatter(
            grad_value_local.astype(jnp.bfloat16), "group", scatter_dimension=0, tiled=True
        ).astype(jnp.float32),
        lax.psum_scatter(
            grad_out_local.astype(jnp.bfloat16), "group", scatter_dimension=0, tiled=True
        ).astype(jnp.float32),
        lax.psum_scatter(
            grad_gain_two.astype(jnp.bfloat16), "group", scatter_dimension=0, tiled=True
        ).astype(jnp.float32),
    )
    (
        gain_one_rows,
        query_rows,
        key_rows,
        value_rows,
        out_rows,
        gain_two_rows,
        grad_gate,
        grad_up,
        grad_down,
    ) = (
        lax.psum(gain_one_rows.astype(jnp.bfloat16), "replica").astype(jnp.float32),
        lax.psum(query_rows.astype(jnp.bfloat16), "replica").astype(jnp.float32),
        lax.psum(key_rows.astype(jnp.bfloat16), "replica").astype(jnp.float32),
        lax.psum(value_rows.astype(jnp.bfloat16), "replica").astype(jnp.float32),
        lax.psum(out_rows.astype(jnp.bfloat16), "replica").astype(jnp.float32),
        lax.psum(gain_two_rows.astype(jnp.bfloat16), "replica").astype(jnp.float32),
        lax.psum(grad_gate.astype(jnp.bfloat16), "replica").astype(jnp.float32),
        lax.psum(grad_up.astype(jnp.bfloat16), "replica").astype(jnp.float32),
        lax.psum(grad_down.astype(jnp.bfloat16), "replica").astype(jnp.float32),
    )
    return (
        result.astype(jnp.bfloat16)[None],
        grad_x.astype(jnp.bfloat16)[None],
        gain_one_rows,
        query_rows,
        key_rows,
        value_rows,
        out_rows,
        gain_two_rows,
        grad_gate,
        grad_up,
        grad_down,
    )


def solution(mesh):
    return jax.shard_map(
        body,
        mesh=mesh,
        in_specs=(
            P("replica", "group", None),
            P("replica", None),
            P("group"),
            P("group", None),
            P("group", None),
            P("group", None),
            P("group", None),
            P("group"),
            P("group", None),
            P("group", None),
            P("group", None),
            P("replica", "group", None),
        ),
        out_specs=(
            P("replica", "group", None),
            P("replica", "group", None),
            P("group"),
            P("group", None),
            P("group", None),
            P("group", None),
            P("group", None),
            P("group"),
            P("group", None),
            P("group", None),
            P("group", None),
        ),
        check_vma=False,
    )
```

profile of v0, /device:TPU:1, one launch (start us, length us, event | category | flops | bytes accessed | tf_op | source)
XLA Modules:
  0.0 2577.9 jit_solution(18410053589851860739)
XLA Ops:
  27.7 19.6 all-gather.17.cloned.1.call-done
  60.4 25.5 all-gather.19.cloned.1.call-done
  96.7 78.7 %all-gather.15.cloned.1.call-done = bf16[2048,2048]{1,0:T(8,128)(2,1)} async-done(((bf16[512,2048]{1,0:T(8,128)(2,1)}), bf16[2048,2048]{1,0:T(8,128)(2,1)}) %all-gather.15.cloned.1.call-update) | async-done | bytes 8388624 | tf_op jit(solution)/shard_map/all_gather | solution.py:109
  175.4 12.3 copy.65
  195.7 18.0 while.30
  214.8 50.0 %all-gather.21.cloned.1.call-done = bf16[2048,2048]{1,0:T(8,128)(2,1)} async-done(((bf16[512,2048]{1,0:T(8,128)(2,1)}), bf16[2048,2048]{1,0:T(8,128)(2,1)}) %all-gather.21.cloned.1.call-update) | async-done | bytes 8388624 | tf_op jit(solution)/shard_map/all_gather | solution.py:112
  269.7 294.0 %all-gather.23.cloned.1.call-done = bf16[2048,8192]{1,0:T(8,128)(2,1)} async-done(((bf16[512,8192]{1,0:T(8,128)(2,1)}), bf16[2048,8192]{1,0:T(8,128)(2,1)}) %all-gather.23.cloned.1.call-update) | async-done | bytes 33554448 | tf_op jit(solution)/shard_map/all_gather | solution.py:156
  563.7 19.4 fusion.91
  583.1 279.5 %all-gather.25.cloned.1.call-done = bf16[2048,8192]{1,0:T(8,128)(2,1)} async-done(((bf16[512,8192]{1,0:T(8,128)(2,1)}), bf16[2048,8192]{1,0:T(8,128)(2,1)}) %all-gather.25.cloned.1.call-update) | async-done | bytes 33554448 | tf_op jit(solution)/shard_map/all_gather | solution.py:157
  862.6 19.3 fusion.92
  881.9 279.8 %all-gather.27.cloned.1.call-done = bf16[8192,2048]{1,0:T(8,128)(2,1)} async-done(((bf16[2048,2048]{1,0:T(8,128)(2,1)}), bf16[8192,2048]{1,0:T(8,128)(2,1)}) %all-gather.27.cloned.1.call-update) | async-done | bytes 33554448 | tf_op jit(solution)/shard_map/all_gather | solution.py:158
  1161.7 21.0 multiply_convert_fusion.1
  1182.7 16.3 fusion.93
  1199.0 16.6 multiply_reduce_fusion.1
  1227.5 66.5 %while.31 = (s32[]{:T(128)}, f32[8,512,64]{1,2,0:T(8,128)}, bf16[8,512,64]{1,2,0:T(8,128)(2,1)}, bf16[8,512,64]{1,2,0:T(8,128)(2,1)}, bf16[8,512,64]{2,1,0:T(8,1...) while((s32[]{:T(128)}, f32[8,512,64]{1,2,0:T(8,128)}, ...), condition=%wide.region_12.13_spmd.clone.clone, body=%wide.region_10.12_spmd.clone.sunk.clone | while | flops 170196480 | bytes 13974697 | solution.py:228
  1304.8 16.1 reduce-scatter.19.cloned.1.call-done
  1324.2 25.1 reduce-scatter.21.cloned.1.call-done
  1366.5 19.9 all-gather.35.cloned.1.call-done
  1386.5 89.5 %all-gather.33.cloned.1.call-done = bf16[512,8192]{1,0:T(8,128)(2,1)} async-done(((bf16[128,8192]{1,0:T(8,128)(2,1)}), bf16[512,8192]{1,0:T(8,128)(2,1)}) %all-gather.33.cloned.1.call-update) | async-done | bytes 8388624 | tf_op jit(solution)/shard_map/all_gather | solution.py:188
  1486.0 27.0 %all-gather.29.cloned.1.call-done = bf16[512,2048]{1,0:T(8,128)(2,1)} async-done(((bf16[128,2048]{1,0:T(8,128)(2,1)}), bf16[512,2048]{1,0:T(8,128)(2,1)}) %all-gather.29.cloned.1.call-update) | async-done | bytes 2097168 | tf_op jit(solution)/shard_map/all_gather | solution.py:195
  1513.0 159.9 %all-gather.31.cloned.1.call-done = bf16[512,16384]{1,0:T(8,128)(2,1)} async-done(((bf16[128,16384]{1,0:T(8,128)(2,1)}), bf16[512,16384]{1,0:T(8,128)(2,1)}) %all-gather.31.cloned.1.call-update) | async-done | bytes 16777232 | tf_op jit(solution)/shard_map/all_gather | solution.py:196
  1672.9 16.4 convolution_convert_fusion
  1689.2 11.8 fusion.89
  1711.5 38.3 %reduce-scatter.15.cloned.1.call-done = bf16[512,512]{1,0:T(8,128)(2,1)} async-done(((bf16[2048,512]{1,0:T(8,128)(2,1)}), bf16[512,512]{1,0:T(8,128)(2,1)}) %reduce-scatter.15.cloned.1.call-update) | async-done | bytes 524304 | tf_op jit(solution)/shard_map/reduce_scatter | solution.py:269
  1749.8 89.9 %reduce-scatter.11.cloned.1.call-done = bf16[512,2048]{1,0:T(8,128)(2,1)} async-done(((bf16[2048,2048]{1,0:T(8,128)(2,1)}), bf16[512,2048]{1,0:T(8,128)(2,1)}) %reduce-scatter.11.cloned.1.call-update) | async-done | bytes 2097168 | tf_op jit(solution)/shard_map/reduce_scatter | solution.py:263
  1839.7 90.2 %reduce-scatter.17.cloned.1.call-done = bf16[512,2048]{1,0:T(8,128)(2,1)} async-done(((bf16[2048,2048]{1,0:T(8,128)(2,1)}), bf16[512,2048]{1,0:T(8,128)(2,1)}) %reduce-scatter.17.cloned.1.call-update) | async-done | bytes 2097168 | tf_op jit(solution)/shard_map/reduce_scatter | solution.py:272
  1938.3 15.5 fusion.47
  1963.9 16.5 all-reduce.2
  1982.7 544.0 %all-reduce.7.cloned.1.call-done = (bf16[512,2048]{1,0:T(8,128)(2,1)}, bf16[512,512]{1,0:T(8,128)(2,1)}, bf16[512,512]{1,0:T(8,128)(2,1)}, bf16[512,2048]{1,0:T(...) async-done(((bf16[512,2048]{1,0:T(8,128)(2,1)}, bf16[512,512]{1,0:T(8,128)(2,1)}, bf16[512,512]{1,0:T(8,128)(2,1)}, ...) | async-done | bytes 30408720 | tf_op jit(solution)/shard_map/psum | solution.py:291
  2535.7 11.7 convert_element_type.250
  2547.4 11.7 convert_element_type.251
  2559.2 11.7 convert_element_type.253
  (298 shorter events, 233.9 us)
Async XLA Ops:
  7.2 40.2 %all-gather.17.cloned.1.call-start = ((), (), s32[]{:S(2)}) async-start(), calls=%async_computation.7 | async-start | bytes 2621440 | tf_op jit(solution)/shard_map/all_gather | solution.py:110
  7.9 78.0 %all-gather.19.cloned.1.call-start = ((), (), s32[]{:S(2)}) async-start(), calls=%async_computation.8 | async-start | bytes 2621440 | tf_op jit(solution)/shard_map/all_gather | solution.py:111
  8.7 166.7 %all-gather.15.cloned.1.call-start = ((), (), s32[]{:S(2)}) async-start(), calls=%async_computation.6 | async-start | bytes 10485760 | tf_op jit(solution)/shard_map/all_gather | solution.py:109
  9.4 255.3 %all-gather.21.cloned.1.call-start = ((), (), s32[]{:S(2)}) async-start(), calls=%async_computation.9 | async-start | bytes 10485760 | tf_op jit(solution)/shard_map/all_gather | solution.py:112
  10.0 553.7 %all-gather.23.cloned.1.call-start = ((), (), s32[]{:S(2)}) async-start(), calls=%async_computation.10 | async-start | bytes 41943040 | tf_op jit(solution)/shard_map/all_gather | solution.py:156
  10.6 852.1 %all-gather.25.cloned.1.call-start = ((), (), s32[]{:S(2)}) async-start(), calls=%async_computation.11 | async-start | bytes 41943040 | tf_op jit(solution)/shard_map/all_gather | solution.py:157
  11.1 8.6 copy-start.20
  11.2 8.8 copy-start.19
  11.2 16.0 copy-start
  11.2 1150.5 %all-gather.27.cloned.1.call-start = ((), (), s32[]{:S(2)}) async-start(), calls=%async_computation.12 | async-start | bytes 41943040 | tf_op jit(solution)/shard_map/all_gather | solution.py:158
  11.9 1308.9 %reduce-scatter.19.cloned.1.call-start = ((), (), s32[]{:S(2)}) async-start(), calls=%async_computation.21 | async-start | bytes 655360
  12.0 39.0 %copy-start.4 = (bf16[8,512,64]{1,2,0:T(8,128)(2,1)}, bf16[8,512,64]{1,2,0:T(8,128)(2,1)S(1)}, u32[]{:S(2)}) copy-start(bf16[8,512,64]{1,2,0:T(8,128)(2,1)S(1)} %fusion.90) | copy-start | bytes 1572868
  269.7 593.0 %copy-start.2 = (bf16[128,2048]{1,0:T(8,128)(2,1)}, bf16[128,2048]{1,0:T(8,128)(2,1)S(1)}, u32[]{:S(2)}) copy-start(bf16[128,2048]{1,0:T(8,128)(2,1)S(1)} %multiply_convert_fusion.4) | copy-start | bytes 1572868
  583.1 578.6 %copy-start.13 = (bf16[1,128,2048]{2,1,0:T(8,128)(2,1)S(1)}, bf16[1,128,2048]{2,1,0:T(8,128)(2,1)}, u32[]{:S(2)}) copy-start(bf16[1,128,2048]{2,1,0:T(8,128)(2,1)} %param.27) | copy-start | bytes 1572868
  1199.0 16.7 copy-start.14
  1235.8 5.1 copy-start.5
  1244.1 5.1 copy-start.5
  1252.4 5.1 copy-start.5
  1296.0 53.3 %reduce-scatter.21.cloned.1.call-start = ((), (), s32[]{:S(2)}) async-start(), calls=%async_computation.22 | async-start | bytes 655360
  1298.2 88.3 %all-gather.35.cloned.1.call-start = ((), (), s32[]{:S(2)}) async-start(), calls=%async_computation.20 | async-start | bytes 2621440 | tf_op jit(solution)/shard_map/all_gather | solution.py:189
  1298.8 177.2 %all-gather.33.cloned.1.call-start = ((), (), s32[]{:S(2)}) async-start(), calls=%async_computation.19 | async-start | bytes 10485760 | tf_op jit(solution)/shard_map/all_gather | solution.py:188
  1299.5 213.5 %all-gather.29.cloned.1.call-start = ((), (), s32[]{:S(2)}) async-start(), calls=%async_computation.17 | async-start | bytes 2621440 | tf_op jit(solution)/shard_map/all_gather | solution.py:195
  1300.1 372.8 %all-gather.31.cloned.1.call-start = ((), (), s32[]{:S(2)}) async-start(), calls=%async_computation.18 | async-start | bytes 20971520 | tf_op jit(solution)/shard_map/all_gather | solution.py:196
  1304.8 406.7 %reduce-scatter.13.cloned.1.call-start = ((), (), s32[]{:S(2)}) async-start(), calls=%async_computation.14 | async-start | bytes 2621440 | tf_op jit(solution)/shard_map/reduce_scatter | solution.py:266
  1324.2 425.6 %reduce-scatter.15.cloned.1.call-start = ((), (), s32[]{:S(2)}) async-start(), calls=%async_computation.15 | async-start | bytes 2621440 | tf_op jit(solution)/shard_map/reduce_scatter | solution.py:269
  1352.4 487.3 %reduce-scatter.11.cloned.1.call-start = ((), (), s32[]{:S(2)}) async-start(), calls=%async_computation.13 | async-start | bytes 10485760 | tf_op jit(solution)/shard_map/reduce_scatter | solution.py:263
  1360.7 569.2 %reduce-scatter.17.cloned.1.call-start = ((), (), s32[]{:S(2)}) async-start(), calls=%async_computation.16 | async-start | bytes 10485760 | tf_op jit(solution)/shard_map/reduce_scatter | solution.py:272
  1366.5 1160.2 %all-reduce.7.cloned.1.call-start = ((), (), s32[]{:S(2)}) async-start(), calls=%async_computation.23 | async-start | bytes 60817408 | tf_op jit(solution)/shard_map/psum | solution.py:291
  1931.8 6.5 copy-start.1
  1938.3 15.5 copy-start.3
  2526.6 5.4 copy-start.15
  2526.6 6.5 copy-start.11
  (22 other events, 56.7 us)
Sparse Core Ops, SparseCore 0:
  9.9 37.4 all-gather.16
  49.2 36.6 all-gather.18
  87.8 87.5 all-gather.14
  177.1 87.5 all-gather.20
  266.4 297.2 all-gather.22
  565.4 297.2 all-gather.24
  864.5 297.2 all-gather.26
  1296.2 24.6 reduce-scatter.18
  1324.5 24.7 reduce-scatter.20
  1351.0 35.4 all-gather.34
  1388.3 87.5 all-gather.32
  1477.6 35.3 all-gather.28
  1515.4 157.4 all-gather.30
  1676.2 35.1 reduce-scatter.12
  1714.6 35.1 reduce-scatter.14
  1753.3 86.3 reduce-scatter.10
  1843.5 86.3 reduce-scatter.16
  1933.2 593.3 all-reduce.6
where the time goes:
time: 2590 us; the launch traced here: 2580 us
  waiting for transfers between devices  2140 us (83%)
  matrix products  256 us (10%)
  other arithmetic  57 us (2%)
  blocking collectives  53.4 us (2%)
  local copies, waits for them, and re-layouts  50.7 us (2%)
    psum x1, waiting for transfers between devices, body(): lax.psum(query_rows.astype(jnp.bfloat16), 'replica').astype(jnp.float32)  544 us
    all_gather x1, waiting for transfers between devices, body(): lax.all_gather(w_gate, 'group', axis=0, tiled=True)  294 us
    all_gather x1, waiting for transfers between devices, body(): lax.all_gather(w_down, 'group', axis=0, tiled=True)  280 us
    all_gather x1, waiting for transfers between devices, body(): lax.all_gather(w_up, 'group', axis=0, tiled=True)  280 us
    all_gather x1, waiting for transfers between devices, body(): lax.all_gather(grad_gate_up, 'group', axis=0, tiled=True)  160 us
    dot_general x31, matrix products, contract_last(): lax.dot_general(left, right, (((1,), (1,)), ((), ())), preferred_element_...  102 us
    reduce_scatter x1, waiting for transfers between devices, body(): lax.psum_scatter(grad_out_local.astype(jnp.bfloat16), 'group', scatter_di...  90.2 us
    reduce_scatter x1, waiting for transfers between devices, body(): lax.psum_scatter(grad_query_local.astype(jnp.bfloat16), 'group', scatter_...  89.9 us
  transfers between devices with their start and end apart: 18, of which 18 were waited for; matrix products, arithmetic and copies ran while one was open for 7% of the time, Pallas kernels for 0%

commit v1 on v0

v1 whole, which is shorter than its diff:
```python
import jax
import jax.numpy as jnp
from jax import lax
from jax.sharding import Mesh
from jax.sharding import PartitionSpec as P

HQ = 32
HK = 8
HEAD = 64

EPS = 1e-05
BASE = 500000.0
MASKED = -1e30

BF = jnp.bfloat16
F32 = jnp.float32


def positions_of(lengths, index):
    ends = jnp.cumsum(lengths)
    starts = ends - lengths
    segment = jnp.sum((index[:, None] >= ends[None, :-1]).astype(jnp.int32), axis=1)
    member = segment[:, None] == jnp.arange(lengths.shape[0], dtype=jnp.int32)[None, :]
    start = jnp.sum(jnp.where(member, starts[None, :], 0), axis=1)
    place = jnp.where(segment == 0, index, lengths[0] + index - start)
    return (segment, place)


def allowed_of(segment, place):
    same = (segment[None, :] == 0) | (segment[None, :] == segment[:, None])
    return same & (place[None, :] <= place[:, None])


def rope_tables(place, size):
    half = size // 2
    freq = BASE ** (-(2.0 * jnp.arange(half, dtype=F32)) / size)
    angle = place.astype(F32)[:, None] * freq[None, :]
    return (jnp.cos(angle)[:, None, :], jnp.sin(angle)[:, None, :])


def rotate(value, cosine, sine):
    half = value.shape[-1] // 2
    first, second = (value[..., :half], value[..., half:])
    return jnp.concatenate(
        [first * cosine - second * sine, second * cosine + first * sine], axis=-1
    )


def rotate_back(grad, cosine, sine):
    half = grad.shape[-1] // 2
    first, second = (grad[..., :half], grad[..., half:])
    return jnp.concatenate(
        [first * cosine + second * sine, second * cosine - first * sine], axis=-1
    )


def matmul(left, right):
    return jnp.dot(left, right, preferred_element_type=F32)


def contract_last(left, right):
    return lax.dot_general(left, right, (((1,), (1,)), ((), ())), preferred_element_type=F32)


def contract_first(left, right):
    return lax.dot_general(left, right, (((0,), (0,)), ((), ())), preferred_element_type=F32)


def norm_back(grad_normed, unit, inverse, gain):
    scaled = grad_normed * gain
    return inverse * (scaled - unit * jnp.mean(scaled * unit, axis=1, keepdims=True))


def step_to(value, axis, step):
    size = lax.axis_size(axis)
    return lax.ppermute(value, axis, [(i, i ^ step) for i in range(size)])


def fetch(blocks):
    return [blocks[0]] + [step_to(b, "group", s) for s, b in enumerate(blocks) if s]


def gather_plane(mine):
    parts = lax.axis_size("group")
    got = fetch([mine] * parts)
    if lax.axis_size("core") == 1:
        return jnp.concatenate(got, axis=0)
    return jnp.concatenate(got + [step_to(g, "core", 1) for g in got], axis=0)


def scatter_plane(partial):
    parts = lax.axis_size("group")
    if lax.axis_size("core") == 2:
        half = partial.shape[0] // 2
        other = step_to(partial[half:].astype(BF), "core", 1)
        partial = partial[:half] + other.astype(F32)
    rows = partial.shape[0] // parts
    blocks = [partial[:rows]] + [
        partial[s * rows : (s + 1) * rows].astype(BF) for s in range(1, parts)
    ]
    got = fetch(blocks)
    total = got[0]
    for other in got[1:]:
        total = total + other.astype(F32)
    return total


def sum_rest(value):
    size = lax.axis_size("rest")
    if size != 4:
        return lax.psum(value, "rest")
    place = lax.axis_index("rest")
    inner = (place == 1) | (place == 2)
    value = value + lax.ppermute(value, "rest", [(0, 1), (3, 2)])
    value = value + lax.ppermute(value, "rest", [(1, 2), (2, 1)])
    outer = lax.ppermute(value, "rest", [(1, 0), (2, 3)])
    return jnp.where(inner, value, outer)


def both_cores(value):
    if lax.axis_size("core") == 1:
        return value[None]
    other = step_to(value, "core", 1)
    core = lax.axis_index("core")
    return jnp.stack([jnp.where(core == 0, value, other), jnp.where(core == 0, other, value)])


def body(
    tokens,
    seq_lengths,
    attn_gain,
    w_query,
    w_key,
    w_value,
    w_out,
    mlp_gain,
    w_gate,
    w_up,
    w_down,
    cotangent,
):
    parts = lax.axis_size("group")
    cores = lax.axis_size("core")
    g = lax.axis_index("group")
    c = lax.axis_index("core")
    rows, width = tokens.shape[1:]
    total = rows * parts
    team = parts * cores
    heads = HQ // HK
    scale = HEAD ** (-0.5)
    ff = w_gate.shape[1] // team
    share = w_gate.shape[0]
    qw = HQ * HEAD // team
    kw = HK * HEAD // team
    assert kw == HEAD

    def member(s):
        return (g ^ s) * cores + c

    def columns(weight, size, s):
        return lax.dynamic_slice_in_dim(weight, member(s) * size, size, 1)

    def in_order(got):
        out = jnp.zeros((parts,) + got[0].shape, got[0].dtype)
        for s, block in enumerate(got):
            out = lax.dynamic_update_slice_in_dim(out, block[None], g ^ s, 0)
        return out.reshape((parts * got[0].shape[0],) + got[0].shape[1:])

    x_mine = tokens[0]
    x_all = gather_plane(x_mine)
    gains = in_order(fetch([jnp.stack([attn_gain, mlp_gain], axis=1)] * parts))
    gain_one = gains[:, 0].astype(F32)
    gain_two = gains[:, 1].astype(F32)
    qkv_full = in_order(
        fetch(
            [
                jnp.concatenate(
                    [columns(w_query, qw, s), columns(w_key, kw, s), columns(w_value, kw, s)],
                    axis=1,
                )
                for s in range(parts)
            ]
        )
    )
    gate_full = in_order(fetch([columns(w_gate, ff, s) for s in range(parts)]))
    up_full = in_order(fetch([columns(w_up, ff, s) for s in range(parts)]))
    out_rows = lax.dynamic_slice_in_dim(w_out, c * qw, qw, 0)
    down_rows = lax.dynamic_slice_in_dim(w_down, c * ff, ff, 0)
    cot_all = gather_plane(cotangent[0])

    lengths = [seq_lengths[0]]
    if cores == 2:
        lengths.append(step_to(seq_lengths[0], "core", 1))
    index = jnp.concatenate(
        [(g ^ s) * rows + jnp.arange(rows, dtype=jnp.int32) for s in range(parts)]
    )
    marks = [positions_of(one, index) for one in lengths]
    allowed = [jnp.tile(allowed_of(*m), (heads, 1)) for m in marks]
    tables = [rope_tables(m[1], HEAD) for m in marks]

    x = x_all.astype(F32)
    inverse_all = lax.rsqrt(jnp.mean(x * x, axis=1, keepdims=True) + EPS)
    normed_one = (x * inverse_all * gain_one).astype(BF)
    qkv = matmul(normed_one, qkv_full)

    def stack_heads(value):
        return value.reshape(total, heads, HEAD).transpose(1, 0, 2).reshape(heads * total, HEAD)

    def lay_heads(value):
        return value.reshape(heads, total, HEAD).transpose(1, 0, 2).reshape(total, heads * HEAD)

    kept = []
    attended = []
    for j in range(cores):
        one = qkv[j * total : (j + 1) * total]
        query = rotate(one[:, :qw].reshape(total, heads, HEAD), *tables[j]).astype(BF)
        query = stack_heads(query.reshape(total, qw))
        key = rotate(one[:, qw : qw + kw].reshape(total, 1, HEAD), *tables[j]).astype(BF)[:, 0]
        value = one[:, qw + kw :].astype(BF)
        scores = jnp.where(allowed[j], contract_last(query, key) * scale, MASKED)
        top = jnp.max(scores, axis=1, keepdims=True)
        expo = jnp.exp(scores - top)
        probs = expo / jnp.sum(expo, axis=1, keepdims=True)
        attended.append(lay_heads(matmul(probs.astype(BF), value)).astype(BF))
        kept.append((query, key, value, probs))
    attended = jnp.concatenate(attended, axis=0)

    x_own = x_mine.astype(F32)
    mid = x_own + scatter_plane(matmul(attended, out_rows))
    inverse_two = lax.rsqrt(jnp.mean(mid * mid, axis=1, keepdims=True) + EPS)
    unit_two = mid * inverse_two
    normed_two = gather_plane((unit_two * gain_two).astype(BF))

    gate = matmul(normed_two, gate_full)
    up = matmul(normed_two, up_full)
    sigma = jax.nn.sigmoid(gate)
    active = (gate * sigma * up).astype(BF)
    grad_active = contract_last(cot_all, down_rows)
    grad_gate_pre = (grad_active * up * sigma * (1.0 + gate * (1.0 - sigma))).astype(BF)
    grad_up_pre = (grad_active * gate * sigma).astype(BF)
    grad_normed_two = scatter_plane(
        contract_last(grad_gate_pre, gate_full) + contract_last(grad_up_pre, up_full)
    )
    grad_down = contract_first(active, cot_all).astype(BF)
    grad_gate = contract_first(normed_two, grad_gate_pre).astype(BF)
    grad_up = contract_first(normed_two, grad_up_pre).astype(BF)
    result = mid + scatter_plane(matmul(active, down_rows))

    def turn(grad):
        return fetch(
            [lax.dynamic_slice_in_dim(grad, (g ^ s) * share, share, 0) for s in range(parts)]
        )

    def finish_columns(blocks, size):
        out = jnp.zeros((share, parts, cores, size), F32)
        for s, block in enumerate(blocks):
            pair = both_cores(sum_rest(block)).astype(F32).transpose(1, 0, 2)
            out = lax.dynamic_update_slice_in_dim(out, pair[:, None], g ^ s, 1)
        return out.reshape(share, parts * cores * size)

    def finish_rows(grad, pieces):
        size = grad.shape[0] // pieces
        got = [
            both_cores(sum_rest(grad[i * size : (i + 1) * size])).astype(F32)
            for i in range(pieces)
        ]
        return jnp.stack(got, axis=1).reshape(cores * grad.shape[0], grad.shape[1])

    grad_y = cotangent[0].astype(F32)
    grad_gain_two = jnp.sum(grad_normed_two * unit_two, axis=0)
    grad_mid = grad_y + norm_back(grad_normed_two, unit_two, inverse_two, gain_two)
    grad_branch = gather_plane(grad_mid.astype(BF))
    grad_attended = contract_last(grad_branch, out_rows).astype(BF)
    grad_out = contract_first(attended, grad_branch).astype(BF)

    grad_qkv = []
    for j in range(cores):
        query, key, value, probs = kept[j]
        g_head = stack_heads(grad_attended[j * total : (j + 1) * total])
        grad_p = contract_last(g_head, value)
        grad_s = (probs * (grad_p - jnp.sum(probs * grad_p, axis=1, keepdims=True))).astype(BF)
        grad_q = lay_heads(matmul(grad_s, key) * scale).reshape(total, heads, HEAD)
        grad_k = (contract_first(grad_s, query) * scale)[:, None]
        grad_v = contract_first(probs.astype(BF), g_head)
        grad_qkv.append(
            jnp.concatenate(
                [
                    rotate_back(grad_q, *tables[j]).reshape(total, qw),
                    rotate_back(grad_k, *tables[j]).reshape(total, kw),
                    grad_v,
                ],
                axis=1,
            ).astype(BF)
        )
    grad_qkv = jnp.concatenate(grad_qkv, axis=0)
    grad_normed_one = scatter_plane(contract_last(grad_qkv, qkv_full))
    inverse_one = inverse_all[:rows]
    unit_one = x_own * inverse_one
    grad_gain_one = jnp.sum(grad_normed_one * unit_one, axis=0)
    grad_x = grad_mid + norm_back(grad_normed_one, unit_one, inverse_one, gain_one)
    grad_weights = contract_first(normed_one, grad_qkv).astype(BF)

    grad_gains = lax.psum(
        jnp.stack([grad_gain_one, grad_gain_two]), ("group", "rest", "core")
    )
    grad_gains = lax.dynamic_slice_in_dim(grad_gains, g * share, share, 1)

    turned = turn(grad_weights)
    grad_qkv_rows = finish_columns(turned, qw + 2 * kw).reshape(share, team, qw + 2 * kw)
    return (
        result.astype(BF)[None],
        grad_x.astype(BF)[None],
        grad_gains[0],
        grad_qkv_rows[:, :, :qw].reshape(share, team * qw),
        grad_qkv_rows[:, :, qw : qw + kw].reshape(share, team * kw),
        grad_qkv_rows[:, :, qw + kw :].reshape(share, team * kw),
        finish_rows(grad_out, 1),
        grad_gains[1],
        finish_columns(turn(grad_gate), ff),
        finish_columns(turn(grad_up), ff),
        finish_rows(grad_down, 4),
    )


def solution(mesh):
    parts, replicas = mesh.devices.shape
    cores = 2 if HK % (2 * parts) == 0 and replicas % 2 == 0 else 1
    split = Mesh(
        mesh.devices.reshape(parts, replicas // cores, cores), ("group", "rest", "core")
    )
    replica = ("rest", "core")
    weights = (P("group"),) + (P("group", None),) * 4 + (P("group"),) + (P("group", None),) * 3
    split_tokens = P(replica, "group", None)
    return jax.shard_map(
        body,
        mesh=split,
        in_specs=(split_tokens, P(replica, None)) + weights + (split_tokens,),
        out_specs=(split_tokens, split_tokens) + weights,
        check_vma=False,
    )
```

time: 2590 us -> 1210 us (0.47)
  waiting for transfers between devices: 2140 us -> 507 us
  starting transfers between devices: 0.92 us -> 206 us
  matrix products: 256 us -> 91.6 us
  local copies, waits for them, and re-layouts: 50.7 us -> 215 us
  other arithmetic: 57 us -> 138 us
    all_gather x11 -> x0, waiting for transfers between devices: 1320 us -> none  [the longest x1 294 us: body(): lax.all_gather(w_gate, 'group', axis=0, tiled=True)]
    psum x1 -> x0, waiting for transfers between devices: 544 us -> none  [body(): lax.psum(query_rows.astype(jnp.bfloat16), 'replica').astype(jnp.float32)]
    ppermute x0 -> x134, waiting for transfers between devices: none -> 507 us  [the longest x83 173 us: step_to(): return lax.ppermute(value, axis, [(i, i ^ step) for i in range(size)])]
    reduce_scatter x4 -> x0, waiting for transfers between devices: 229 us -> none  [the longest x1 90.2 us: body(): lax.psum_scatter(grad_out_local.astype(jnp.bfloat16), 'group', scatter_di...]
    ppermute x0 -> x134, starting transfers between devices: none -> 206 us  [the longest x83 109 us: step_to(): return lax.ppermute(value, axis, [(i, i ^ step) for i in range(size)])]
    dot_general x31 -> x9, matrix products: 102 us -> 36.4 us  [contract_last(): lax.dot_general(left, right, (((1,), (1,)), ((), ())), preferred_element_...]
    dynamic_update_slice x8 -> x21, local copies, waits for them, and re-layouts: 0.49 us -> 55.4 us  [the longest x6 39.1 us: finish_columns(): out = lax.dynamic_update_slice_in_dim(out, pair[:, None], g ^ s, 1)]
    dot_general x23 -> x9, matrix products: 85.2 us -> 31.3 us  [matmul(): return jnp.dot(left, right, preferred_element_type=F32)]
  transfers between devices with their start and end apart: 18 -> 134, of which waited for: 18 -> 47; matrix products, arithmetic and copies ran while one was open for 7% -> 32% of each run, Pallas kernels for 0% -> 0%
where the time goes in v1:
time: 1210 us; the launch traced here: 1200 us
  waiting for transfers between devices  507 us (42%)
  local copies, waits for them, and re-layouts  215 us (18%)
  starting transfers between devices  206 us (17%)
  other arithmetic  138 us (11%)
  matrix products  91.6 us (8%)
  blocking collectives  40.7 us (3%)
    ppermute x83, waiting for transfers between devices, step_to(): return lax.ppermute(value, axis, [(i, i ^ step) for i in range(size)])  173 us
    ppermute x17, waiting for transfers between devices, sum_rest(): value = value + lax.ppermute(value, 'rest', [(0, 1), (3, 2)])  171 us
    ppermute x17, waiting for transfers between devices, sum_rest(): outer = lax.ppermute(value, 'rest', [(1, 0), (2, 3)])  162 us
    ppermute x83, starting transfers between devices, step_to(): return lax.ppermute(value, axis, [(i, i ^ step) for i in range(size)])  109 us
    ppermute x17, starting transfers between devices, sum_rest(): value = value + lax.ppermute(value, 'rest', [(0, 1), (3, 2)])  58.2 us
    psum x1, blocking collectives, body(): lax.psum(jnp.stack([grad_gain_one, grad_gain_two]), ('group', 'rest', 'co...  40.7 us
    reshape x2, local copies, waits for them, and re-layouts, finish_columns(): return out.reshape(share, parts * cores * size)  39.5 us
    dynamic_update_slice x6, local copies, waits for them, and re-layouts, finish_columns(): out = lax.dynamic_update_slice_in_dim(out, pair[:, None], g ^ s, 1)  39.1 us
  transfers between devices with their start and end apart: 134, of which 47 were waited for; matrix products, arithmetic and copies ran while one was open for 32% of the time, Pallas kernels for 0%

profile of v1, /device:TPU:1, one launch (start us, length us, event | category | flops | bytes accessed | tf_op | source)
XLA Modules:
  0.0 1202.0 jit_solution(10514595105014259838)
XLA Ops:
  82.4 12.5 %collective-permute-start.4 = (bf16[128,2048]{1,0:T(8,128)(2,1)}, bf16[128,2048]{1,0:T(8,128)(2,1)S(1)}, u32[]{:S(2)}, u32[]{:S(2)}) collective-permute-start(bf16[128,2048]{1,0:T(8,128)(2,1)} %collective-permute-done), channel_id=1, source_target_pairs={{0,1},{1,0},{2,3},{3,2},{4,5},{5,4},{6,7},{7,6},{8,9},{9,8},{10,11... | collective-permute-start | bytes 1572872 | tf_op jit(solution)/shard_map/ppermute | solution.py:76
  143.4 20.6 %collective-permute-done.25 = bf16[512,1024]{1,0:T(8,128)(2,1)S(1)} collective-permute-done((bf16[512,1024]{1,0:T(8,128)(2,1)S(1)}, bf16[512,1024]{1,0:T(8,128)(2,1)S(1)}, u32[]{:S(2)}, u32[]{:S(2)}) %collective-permute-start.25) | collective-permute-done | bytes 1048608 | tf_op jit(solution)/shard_map/ppermute | solution.py:76
  175.0 12.0 collective-permute-done.16
  191.5 17.2 %collective-permute-done.27 = bf16[512,1024]{1,0:T(8,128)(2,1)S(1)} collective-permute-done((bf16[512,1024]{1,0:T(8,128)(2,1)S(1)}, bf16[512,1024]{1,0:T(8,128)(2,1)S(1)}, u32[]{:S(2)}, u32[]{:S(2)}) %collective-permute-start.27) | collective-permute-done | bytes 1048608 | tf_op jit(solution)/shard_map/ppermute | solution.py:76
  222.0 9.2 collective-permute-done.20
  240.2 9.6 multiply_convert_fusion.3
  296.0 10.6 collective-permute-done.80
  311.9 19.9 %collective-permute-done.94 = bf16[512,1024]{0,1:T(8,128)(2,1)} collective-permute-done((bf16[512,1024]{0,1:T(8,128)(2,1)S(1)}, bf16[512,1024]{0,1:T(8,128)(2,1)}, u32[]{:S(2)}, u32[]{:S(2)}) %collective-permute-start.94) | collective-permute-done | bytes 1048608 | tf_op jit(solution)/shard_map/ppermute | solution.py:76
  345.3 9.1 collective-permute-done.103
  356.5 21.4 %collective-permute-done.108 = bf16[512,1024]{0,1:T(8,128)(2,1)S(1)} collective-permute-done((bf16[512,1024]{0,1:T(8,128)(2,1)S(1)}, bf16[512,1024]{0,1:T(8,128)(2,1)S(1)}, u32[]{:S(2)}, u32[]{:S(2)}) %collective-permute-start.108) | collective-permute-done | bytes 1048608 | tf_op jit(solution)/shard_map/ppermute | solution.py:76
  383.3 16.9 %collective-permute-done.122 = bf16[256,2048]{1,0:T(8,128)(2,1)S(1)} collective-permute-done((bf16[256,2048]{1,0:T(8,128)(2,1)S(1)}, bf16[256,2048]{1,0:T(8,128)(2,1)S(1)}, u32[]{:S(2)}, u32[]{:S(2)}) %collective-permute-start.122) | collective-permute-done | bytes 1048608 | tf_op jit(solution)/shard_map/ppermute | solution.py:114
  401.8 20.8 %collective-permute-done.126 = bf16[256,2048]{1,0:T(8,128)(2,1)S(1)} collective-permute-done((bf16[256,2048]{1,0:T(8,128)(2,1)S(1)}, bf16[256,2048]{1,0:T(8,128)(2,1)S(1)}, u32[]{:S(2)}, u32[]{:S(2)}) %collective-permute-start.126) | collective-permute-done | bytes 1048608 | tf_op jit(solution)/shard_map/ppermute | solution.py:114
  427.9 17.2 %collective-permute-done.130 = bf16[256,2048]{1,0:T(8,128)(2,1)S(1)} collective-permute-done((bf16[256,2048]{1,0:T(8,128)(2,1)S(1)}, bf16[256,2048]{1,0:T(8,128)(2,1)S(1)}, u32[]{:S(2)}, u32[]{:S(2)}) %collective-permute-start.130) | collective-permute-done | bytes 1048608 | tf_op jit(solution)/shard_map/ppermute | solution.py:114
  475.7 14.5 %collective-permute-done.90 = bf16[512,1024]{0,1:T(8,128)(2,1)} collective-permute-done((bf16[512,1024]{0,1:T(8,128)(2,1)}, bf16[512,1024]{0,1:T(8,128)(2,1)}, u32[]{:S(2)}, u32[]{:S(2)}) %collective-permute-start.90) | collective-permute-done | bytes 1048608 | tf_op jit(solution)/shard_map/ppermute | solution.py:114
  490.9 21.7 %collective-permute-done.95 = bf16[512,1024]{0,1:T(8,128)(2,1)} collective-permute-done((bf16[512,1024]{0,1:T(8,128)(2,1)}, bf16[512,1024]{0,1:T(8,128)(2,1)}, u32[]{:S(2)}, u32[]{:S(2)}) %collective-permute-start.95) | collective-permute-done | bytes 1048608 | tf_op jit(solution)/shard_map/ppermute | solution.py:114
  523.4 11.7 collective-permute-done.104
  536.7 20.8 %collective-permute-done.109 = bf16[512,1024]{0,1:T(8,128)(2,1)S(1)} collective-permute-done((bf16[512,1024]{0,1:T(8,128)(2,1)}, bf16[512,1024]{0,1:T(8,128)(2,1)S(1)}, u32[]{:S(2)}, u32[]{:S(2)}) %collective-permute-start.109) | collective-permute-done | bytes 1048608 | tf_op jit(solution)/shard_map/ppermute | solution.py:114
  559.4 20.5 %collective-permute-done.114 = bf16[512,1024]{0,1:T(8,128)(2,1)S(1)} collective-permute-done((bf16[512,1024]{0,1:T(8,128)(2,1)S(1)}, bf16[512,1024]{0,1:T(8,128)(2,1)S(1)}, u32[]{:S(2)}, u32[]{:S(2)}) %collective-permute-start.114) | collective-permute-done | bytes 1048608 | tf_op jit(solution)/shard_map/ppermute | solution.py:114
  611.7 31.5 %collective-permute-done.132 = bf16[256,2048]{1,0:T(8,128)(2,1)S(1)} collective-permute-done((bf16[256,2048]{1,0:T(8,128)(2,1)S(1)}, bf16[256,2048]{1,0:T(8,128)(2,1)S(1)}, u32[]{:S(2)}, u32[]{:S(2)}) %collective-permute-start.132) | collective-permute-done | bytes 1048608 | tf_op jit(solution)/shard_map/ppermute | solution.py:116
  644.7 21.0 %collective-permute-done.128 = bf16[256,2048]{1,0:T(8,128)(2,1)S(1)} collective-permute-done((bf16[256,2048]{1,0:T(8,128)(2,1)S(1)}, bf16[256,2048]{1,0:T(8,128)(2,1)S(1)}, u32[]{:S(2)}, u32[]{:S(2)}) %collective-permute-start.128) | collective-permute-done | bytes 1048608 | tf_op jit(solution)/shard_map/ppermute | solution.py:116
  669.2 19.0 %collective-permute-done.124 = bf16[256,2048]{1,0:T(8,128)(2,1)S(1)} collective-permute-done((bf16[256,2048]{1,0:T(8,128)(2,1)S(1)}, bf16[256,2048]{1,0:T(8,128)(2,1)S(1)}, u32[]{:S(2)}, u32[]{:S(2)}) %collective-permute-start.124) | collective-permute-done | bytes 1048608 | tf_op jit(solution)/shard_map/ppermute | solution.py:116
  689.8 20.9 %collective-permute-done.120 = bf16[256,2048]{1,0:T(8,128)(2,1)S(1)} collective-permute-done((bf16[256,2048]{1,0:T(8,128)(2,1)S(1)}, bf16[256,2048]{1,0:T(8,128)(2,1)S(1)}, u32[]{:S(2)}, u32[]{:S(2)}) %collective-permute-start.120) | collective-permute-done | bytes 1048608 | tf_op jit(solution)/shard_map/ppermute | solution.py:116
  713.7 19.4 %collective-permute-done.101 = bf16[512,1024]{0,1:T(8,128)(2,1)S(1)} collective-permute-done((bf16[512,1024]{0,1:T(8,128)(2,1)S(1)}, bf16[512,1024]{0,1:T(8,128)(2,1)S(1)}, u32[]{:S(2)}, u32[]{:S(2)}) %collective-permute-start.101) | collective-permute-done | bytes 1048608 | tf_op jit(solution)/shard_map/ppermute | solution.py:116
  788.6 12.6 %collective-permute-start.57 = (bf16[512,384]{0,1:T(8,128)(2,1)S(1)}, bf16[512,384]{0,1:T(8,128)(2,1)S(1)}, u32[]{:S(2)}, u32[]{:S(2)}) collective-permute-start(bf16[512,384]{0,1:T(8,128)(2,1)S(1)} %get-tuple-element.146), channel_id=1, source_target_pairs={{0,2},{6,4},{1,3},{7,5},{8,10},{14,12},{9,11},{15,13},{16,18},{22,... | collective-permute-start | bytes 1179656 | tf_op jit(solution)/shard_map/ppermute | solution.py:114
  822.4 11.7 bitcast_convert_fusion
  865.7 14.3 %collective-permute-done.111 = bf16[512,1024]{0,1:T(8,128)(2,1)S(1)} collective-permute-done((bf16[512,1024]{0,1:T(8,128)(2,1)S(1)}, bf16[512,1024]{0,1:T(8,128)(2,1)S(1)}, u32[]{:S(2)}, u32[]{:S(2)}) %collective-permute-start.111) | collective-permute-done | bytes 1048608 | tf_op jit(solution)/shard_map/ppermute | solution.py:116
  889.6 12.9 %collective-permute-done.116 = bf16[512,1024]{0,1:T(8,128)(2,1)S(1)} collective-permute-done((bf16[512,1024]{0,1:T(8,128)(2,1)S(1)}, bf16[512,1024]{0,1:T(8,128)(2,1)S(1)}, u32[]{:S(2)}, u32[]{:S(2)}) %collective-permute-start.116) | collective-permute-done | bytes 1048608 | tf_op jit(solution)/shard_map/ppermute | solution.py:116
  957.8 25.4 %copy.93 = f32[512,4,2,1024]{3,2,1,0:T(2,128)} copy(f32[512,4,2,1024]{0,3,2,1:T(8,128)} %bitcast_dynamic-update-slice_fusion.4) | data formatting | bytes 33554432 | tf_op jit(solution)/shard_map/dynamic_update_slice | solution.py:258
  1000.7 22.1 %reshape.969 = f32[512,8192]{1,0:T(8,128)} reshape(f32[512,4,2,1024]{3,2,1,0:T(2,128)} %constant_dynamic-update-slice_fusion.32) | data formatting | bytes 33554432 | tf_op jit(solution)/shard_map/reshape | solution.py:259
  1038.6 17.4 %copy.99 = f32[512,8192]{1,0:T(8,128)} copy(f32[512,8192]{0,1:T(8,128)} %bitcast.120) | data formatting | bytes 33554432 | tf_op jit(solution)/shard_map/reshape | solution.py:259
  1062.9 13.5 %collective-permute-done.69 = bf16[512,384]{0,1:T(8,128)(2,1)} collective-permute-done((bf16[512,384]{0,1:T(8,128)(2,1)}, bf16[512,384]{0,1:T(8,128)(2,1)}, u32[]{:S(2)}, u32[]{:S(2)}) %collective-permute-start.69) | collective-permute-done | bytes 393248 | tf_op jit(solution)/shard_map/ppermute | solution.py:116
  1151.9 40.7 %psum.7 = f32[2,2048]{1,0:T(2,128)S(1)} all-reduce(f32[2,2048]{1,0:T(2,128)S(1)} %pad_maximum_fusion.15), channel_id=1, replica_groups=mesh['group'=4,'rest'=4,'core'=2] {'group','rest','core'}, use_global_device_ids=true, to_apply=%region_18.19 | all-reduce | flops 4096 | bytes 32768 | tf_op jit(solution)/shard_map/psum | solution.py:303
  (741 shorter events, 629.3 us)
Async XLA Ops:
  0.7 68.0 %collective-permute-start = (bf16[128,2048]{1,0:T(8,128)(2,1)}, bf16[128,2048]{1,0:T(8,128)(2,1)}, u32[]{:S(2)}, u32[]{:S(2)}) collective-permute-start(bf16[128,2048]{1,0:T(8,128)(2,1)} %bitcast.324), channel_id=1, source_target_pairs={{0,8},{8,0},{16,24},{24,16},{1,9},{9,1},{17,25},{25,17},{2,10},{10... | collective-permute-start | bytes 1572872 | tf_op jit(solution)/shard_map/ppermute | solution.py:76
  2.8 69.0 %collective-permute-start.1 = (bf16[128,2048]{1,0:T(8,128)(2,1)}, bf16[128,2048]{1,0:T(8,128)(2,1)}, u32[]{:S(2)}, u32[]{:S(2)}) collective-permute-start(bf16[128,2048]{1,0:T(8,128)(2,1)} %bitcast.325), channel_id=1, source_target_pairs={{0,16},{8,24},{16,0},{24,8},{1,17},{9,25},{17,1},{25,9},{2,18},{10... | collective-permute-start | bytes 1572872 | tf_op jit(solution)/shard_map/ppermute | solution.py:76
  4.0 70.3 %collective-permute-start.2 = (bf16[128,2048]{1,0:T(8,128)(2,1)}, bf16[128,2048]{1,0:T(8,128)(2,1)}, u32[]{:S(2)}, u32[]{:S(2)}) collective-permute-start(bf16[128,2048]{1,0:T(8,128)(2,1)} %bitcast.326), channel_id=1, source_target_pairs={{0,24},{8,16},{16,8},{24,0},{1,25},{9,17},{17,9},{25,1},{2,26},{10... | collective-permute-start | bytes 1572872 | tf_op jit(solution)/shard_map/ppermute | solution.py:76
  118.6 70.8 %collective-permute-start.26 = (bf16[512,1024]{1,0:T(8,128)(2,1)S(1)}, bf16[512,1024]{1,0:T(8,128)(2,1)S(1)}, u32[]{:S(2)}, u32[]{:S(2)}) collective-permute-start(bf16[512,1024]{1,0:T(8,128)(2,1)S(1)} %copy-done.53), channel_id=1, source_target_pairs={{0,16},{8,24},{16,0},{24,8},{1,17},{9,25},{17,1},{25,9},{2,18},{10... | collective-permute-start | bytes 3145736 | tf_op jit(solution)/shard_map/ppermute | solution.py:76
  132.4 54.6 %collective-permute-start.16 = (bf16[128,2048]{1,0:T(8,128)(2,1)S(1)}, bf16[128,2048]{1,0:T(8,128)(2,1)S(1)}, u32[]{:S(2)}, u32[]{:S(2)}) collective-permute-start(bf16[128,2048]{1,0:T(8,128)(2,1)S(1)} %get-tuple-element.138), channel_id=1, source_target_pairs={{0,16},{8,24},{16,0},{24,8},{1,17},{9,25},{17,1},{25,9},{2,18},{10... | collective-permute-start | bytes 1572872 | tf_op jit(solution)/shard_map/ppermute | solution.py:76
  310.5 67.3 %collective-permute-start.108 = (bf16[512,1024]{0,1:T(8,128)(2,1)S(1)}, bf16[512,1024]{0,1:T(8,128)(2,1)S(1)}, u32[]{:S(2)}, u32[]{:S(2)}) collective-permute-start(bf16[512,1024]{0,1:T(8,128)(2,1)S(1)} %get-tuple-element.94), channel_id=1, source_target_pairs={{0,16},{8,24},{16,0},{24,8},{1,17},{9,25},{17,1},{25,9},{2,18},{10... | collective-permute-start | bytes 3145736 | tf_op jit(solution)/shard_map/ppermute | solution.py:76
  311.1 68.1 %collective-permute-start.113 = (bf16[512,1024]{0,1:T(8,128)(2,1)S(1)}, bf16[512,1024]{0,1:T(8,128)(2,1)S(1)}, u32[]{:S(2)}, u32[]{:S(2)}) collective-permute-start(bf16[512,1024]{0,1:T(8,128)(2,1)S(1)} %get-tuple-element.93), channel_id=1, source_target_pairs={{0,24},{8,16},{16,8},{24,0},{1,25},{9,17},{17,9},{25,1},{2,26},{10... | collective-permute-start | bytes 3145736 | tf_op jit(solution)/shard_map/ppermute | solution.py:76
  341.2 108.9 %collective-permute-start.42 = (bf16[512,2048]{1,0:T(8,128)(2,1)S(1)}, bf16[512,2048]{1,0:T(8,128)(2,1)S(1)}, u32[]{:S(2)}, u32[]{:S(2)}) collective-permute-start(bf16[512,2048]{1,0:T(8,128)(2,1)S(1)} %slice.446), channel_id=1, source_target_pairs={{0,1},{1,0},{2,3},{3,2},{4,5},{5,4},{6,7},{7,6},{8,9},{9,8},{10,11... | collective-permute-start | bytes 6291464 | tf_op jit(solution)/shard_map/ppermute | solution.py:76
  354.4 99.3 %collective-permute-start.31 = (bf16[512,2048]{1,0:T(8,128)(2,1)S(1)}, bf16[512,2048]{1,0:T(8,128)(2,1)S(1)}, u32[]{:S(2)}, u32[]{:S(2)}) collective-permute-start(bf16[512,2048]{1,0:T(8,128)(2,1)S(1)} %slice.447), channel_id=1, source_target_pairs={{0,1},{1,0},{2,3},{3,2},{4,5},{5,4},{6,7},{7,6},{8,9},{9,8},{10,11... | collective-permute-start | bytes 6291464 | tf_op jit(solution)/shard_map/ppermute | solution.py:76
  380.6 64.5 %collective-permute-start.130 = (bf16[256,2048]{1,0:T(8,128)(2,1)S(1)}, bf16[256,2048]{1,0:T(8,128)(2,1)S(1)}, u32[]{:S(2)}, u32[]{:S(2)}) collective-permute-start(bf16[256,2048]{1,0:T(8,128)(2,1)S(1)} %copy-done.58), channel_id=1, source_target_pairs={{0,2},{6,4},{1,3},{7,5},{8,10},{14,12},{9,11},{15,13},{16,18},{22,... | collective-permute-start | bytes 3145736 | tf_op jit(solution)/shard_map/ppermute | solution.py:114
  400.1 57.2 %collective-permute-start.81 = (bf16[512,1024]{0,1:T(8,128)(2,1)}, bf16[512,1024]{0,1:T(8,128)(2,1)}, u32[]{:S(2)}, u32[]{:S(2)}) collective-permute-start(bf16[512,1024]{0,1:T(8,128)(2,1)} %add.540), channel_id=1, source_target_pairs={{2,4},{4,2},{3,5},{5,3},{10,12},{12,10},{11,13},{13,11},{18,20},{2... | collective-permute-start | bytes 3145736 | tf_op jit(solution)/shard_map/ppermute | solution.py:115
  450.2 62.4 %collective-permute-start.95 = (bf16[512,1024]{0,1:T(8,128)(2,1)}, bf16[512,1024]{0,1:T(8,128)(2,1)}, u32[]{:S(2)}, u32[]{:S(2)}) collective-permute-start(bf16[512,1024]{0,1:T(8,128)(2,1)} %collective-permute-done.94), channel_id=1, source_target_pairs={{0,2},{6,4},{1,3},{7,5},{8,10},{14,12},{9,11},{15,13},{16,18},{22,... | collective-permute-start | bytes 3145736 | tf_op jit(solution)/shard_map/ppermute | solution.py:114
  455.1 58.4 %collective-permute-start.100 = (bf16[512,1024]{0,1:T(8,128)(2,1)}, bf16[512,1024]{0,1:T(8,128)(2,1)}, u32[]{:S(2)}, u32[]{:S(2)}) collective-permute-start(bf16[512,1024]{0,1:T(8,128)(2,1)} %add.548), channel_id=1, source_target_pairs={{2,4},{4,2},{3,5},{5,3},{10,12},{12,10},{11,13},{13,11},{18,20},{2... | collective-permute-start | bytes 3145736 | tf_op jit(solution)/shard_map/ppermute | solution.py:115
  457.4 77.7 %collective-permute-start.104 = (bf16[512,1024]{0,1:T(8,128)(2,1)}, bf16[512,1024]{0,1:T(8,128)(2,1)S(1)}, u32[]{:S(2)}, u32[]{:S(2)}) collective-permute-start(bf16[512,1024]{0,1:T(8,128)(2,1)} %copy-done.29), channel_id=1, source_target_pairs={{0,2},{6,4},{1,3},{7,5},{8,10},{14,12},{9,11},{15,13},{16,18},{22,... | collective-permute-start | bytes 3145736 | tf_op jit(solution)/shard_map/ppermute | solution.py:114
  467.7 89.9 %collective-permute-start.109 = (bf16[512,1024]{0,1:T(8,128)(2,1)}, bf16[512,1024]{0,1:T(8,128)(2,1)S(1)}, u32[]{:S(2)}, u32[]{:S(2)}) collective-permute-start(bf16[512,1024]{0,1:T(8,128)(2,1)} %copy-done.32), channel_id=1, source_target_pairs={{0,2},{6,4},{1,3},{7,5},{8,10},{14,12},{9,11},{15,13},{16,18},{22,... | collective-permute-start | bytes 3145736 | tf_op jit(solution)/shard_map/ppermute | solution.py:114
  490.1 89.8 %collective-permute-start.131 = (bf16[256,2048]{1,0:T(8,128)(2,1)S(1)}, bf16[256,2048]{1,0:T(8,128)(2,1)S(1)}, u32[]{:S(2)}, u32[]{:S(2)}) collective-permute-start(bf16[256,2048]{1,0:T(8,128)(2,1)S(1)} %get-tuple-element.88), channel_id=1, source_target_pairs={{2,4},{4,2},{3,5},{5,3},{10,12},{12,10},{11,13},{13,11},{18,20},{2... | collective-permute-start | bytes 3145736 | tf_op jit(solution)/shard_map/ppermute | solution.py:115
  512.6 70.2 %collective-permute-start.127 = (bf16[256,2048]{1,0:T(8,128)(2,1)S(1)}, bf16[256,2048]{1,0:T(8,128)(2,1)S(1)}, u32[]{:S(2)}, u32[]{:S(2)}) collective-permute-start(bf16[256,2048]{1,0:T(8,128)(2,1)S(1)} %get-tuple-element.87), channel_id=1, source_target_pairs={{2,4},{4,2},{3,5},{5,3},{10,12},{12,10},{11,13},{13,11},{18,20},{2... | collective-permute-start | bytes 3145736 | tf_op jit(solution)/shard_map/ppermute | solution.py:115
  513.5 66.4 %collective-permute-start.114 = (bf16[512,1024]{0,1:T(8,128)(2,1)S(1)}, bf16[512,1024]{0,1:T(8,128)(2,1)S(1)}, u32[]{:S(2)}, u32[]{:S(2)}) collective-permute-start(bf16[512,1024]{0,1:T(8,128)(2,1)S(1)} %copy-done.35), channel_id=1, source_target_pairs={{0,2},{6,4},{1,3},{7,5},{8,10},{14,12},{9,11},{15,13},{16,18},{22,... | collective-permute-start | bytes 3145736 | tf_op jit(solution)/shard_map/ppermute | solution.py:114
  535.1 61.8 %collective-permute-start.123 = (bf16[256,2048]{1,0:T(8,128)(2,1)S(1)}, bf16[256,2048]{1,0:T(8,128)(2,1)}, u32[]{:S(2)}, u32[]{:S(2)}) collective-permute-start(bf16[256,2048]{1,0:T(8,128)(2,1)S(1)} %get-tuple-element.86), channel_id=1, source_target_pairs={{2,4},{4,2},{3,5},{5,3},{10,12},{12,10},{11,13},{13,11},{18,20},{2... | collective-permute-start | bytes 3145736 | tf_op jit(solution)/shard_map/ppermute | solution.py:115
  596.9 70.3 %collective-permute-start.82 = (bf16[512,1024]{0,1:T(8,128)(2,1)S(1)}, bf16[512,1024]{0,1:T(8,128)(2,1)S(1)}, u32[]{:S(2)}, u32[]{:S(2)}) collective-permute-start(bf16[512,1024]{0,1:T(8,128)(2,1)S(1)} %add.541), channel_id=1, source_target_pairs={{2,0},{4,6},{3,1},{5,7},{10,8},{12,14},{11,9},{13,15},{18,16},{20,... | collective-permute-start | bytes 3145736 | tf_op jit(solution)/shard_map/ppermute | solution.py:116
  599.8 68.1 %collective-permute-start.86 = (bf16[512,1024]{0,1:T(8,128)(2,1)S(1)}, bf16[512,1024]{0,1:T(8,128)(2,1)S(1)}, u32[]{:S(2)}, u32[]{:S(2)}) collective-permute-start(bf16[512,1024]{0,1:T(8,128)(2,1)S(1)} %add.542), channel_id=1, source_target_pairs={{2,4},{4,2},{3,5},{5,3},{10,12},{12,10},{11,13},{13,11},{18,20},{2... | collective-permute-start | bytes 3145736 | tf_op jit(solution)/shard_map/ppermute | solution.py:115
  602.2 86.8 %collective-permute-start.91 = (bf16[512,1024]{0,1:T(8,128)(2,1)S(1)}, bf16[512,1024]{0,1:T(8,128)(2,1)S(1)}, u32[]{:S(2)}, u32[]{:S(2)}) collective-permute-start(bf16[512,1024]{0,1:T(8,128)(2,1)S(1)} %add.544), channel_id=1, source_target_pairs={{2,4},{4,2},{3,5},{5,3},{10,12},{12,10},{11,13},{13,11},{18,20},{2... | collective-permute-start | bytes 3145736 | tf_op jit(solution)/shard_map/ppermute | solution.py:115
  607.5 58.2 %collective-permute-start.128 = (bf16[256,2048]{1,0:T(8,128)(2,1)S(1)}, bf16[256,2048]{1,0:T(8,128)(2,1)S(1)}, u32[]{:S(2)}, u32[]{:S(2)}) collective-permute-start(bf16[256,2048]{1,0:T(8,128)(2,1)S(1)} %add.561), channel_id=1, source_target_pairs={{2,0},{4,6},{3,1},{5,7},{10,8},{12,14},{11,9},{13,15},{18,16},{20,... | collective-permute-start | bytes 3145736 | tf_op jit(solution)/shard_map/ppermute | solution.py:116
  667.9 65.2 %collective-permute-start.101 = (bf16[512,1024]{0,1:T(8,128)(2,1)S(1)}, bf16[512,1024]{0,1:T(8,128)(2,1)S(1)}, u32[]{:S(2)}, u32[]{:S(2)}) collective-permute-start(bf16[512,1024]{0,1:T(8,128)(2,1)S(1)} %add.549), channel_id=1, source_target_pairs={{2,0},{4,6},{3,1},{5,7},{10,8},{12,14},{11,9},{13,15},{18,16},{20,... | collective-permute-start | bytes 3145736 | tf_op jit(solution)/shard_map/ppermute | solution.py:116
  745.5 89.3 %collective-permute-start.87 = (bf16[512,1024]{0,1:T(8,128)(2,1)}, bf16[512,1024]{0,1:T(8,128)(2,1)}, u32[]{:S(2)}, u32[]{:S(2)}) collective-permute-start(bf16[512,1024]{0,1:T(8,128)(2,1)} %add.543), channel_id=1, source_target_pairs={{2,0},{4,6},{3,1},{5,7},{10,8},{12,14},{11,9},{13,15},{18,16},{20,... | collective-permute-start | bytes 3145736 | tf_op jit(solution)/shard_map/ppermute | solution.py:116
  747.2 89.0 %collective-permute-start.92 = (bf16[512,1024]{0,1:T(8,128)(2,1)}, bf16[512,1024]{0,1:T(8,128)(2,1)}, u32[]{:S(2)}, u32[]{:S(2)}) collective-permute-start(bf16[512,1024]{0,1:T(8,128)(2,1)} %add.545), channel_id=1, source_target_pairs={{2,0},{4,6},{3,1},{5,7},{10,8},{12,14},{11,9},{13,15},{18,16},{20,... | collective-permute-start | bytes 3145736 | tf_op jit(solution)/shard_map/ppermute | solution.py:116
  847.7 54.8 %collective-permute-start.116 = (bf16[512,1024]{0,1:T(8,128)(2,1)S(1)}, bf16[512,1024]{0,1:T(8,128)(2,1)S(1)}, u32[]{:S(2)}, u32[]{:S(2)}) collective-permute-start(bf16[512,1024]{0,1:T(8,128)(2,1)S(1)} %add.555), channel_id=1, source_target_pairs={{2,0},{4,6},{3,1},{5,7},{10,8},{12,14},{11,9},{13,15},{18,16},{20,... | collective-permute-start | bytes 3145736 | tf_op jit(solution)/shard_map/ppermute | solution.py:116
  943.2 250.0 %collective-permute-start.34 = (bf16[128,2048]{1,0:T(8,128)(2,1)}, bf16[128,2048]{1,0:T(8,128)(2,1)}, u32[]{:S(2)}, u32[]{:S(2)}) collective-permute-start(bf16[128,2048]{1,0:T(8,128)(2,1)} %get-tuple-element.134), channel_id=1, source_target_pairs={{0,24},{8,16},{16,8},{24,0},{1,25},{9,17},{17,9},{25,1},{2,26},{10... | collective-permute-start | bytes 1572872 | tf_op jit(solution)/shard_map/ppermute | solution.py:76
  946.2 156.9 %collective-permute-start.53 = (bf16[512,2048]{1,0:T(8,128)(2,1)}, bf16[512,2048]{1,0:T(8,128)(2,1)}, u32[]{:S(2)}, u32[]{:S(2)}) collective-permute-start(bf16[512,2048]{1,0:T(8,128)(2,1)} %slice.445), channel_id=1, source_target_pairs={{0,1},{1,0},{2,3},{3,2},{4,5},{5,4},{6,7},{7,6},{8,9},{9,8},{10,11... | collective-permute-start | bytes 6291464 | tf_op jit(solution)/shard_map/ppermute | solution.py:76
  951.8 71.0 %collective-permute-start.107 = (bf16[512,1024]{0,1:T(8,128)(2,1)}, bf16[512,1024]{0,1:T(8,128)(2,1)}, u32[]{:S(2)}, u32[]{:S(2)}) collective-permute-start(bf16[512,1024]{0,1:T(8,128)(2,1)} %broadcast_select_fusion.2), channel_id=1, source_target_pairs={{0,1},{1,0},{2,3},{3,2},{4,5},{5,4},{6,7},{7,6},{8,9},{9,8},{10,11... | collective-permute-start | bytes 3145736 | tf_op jit(solution)/shard_map/ppermute | solution.py:76
  955.0 73.7 %collective-permute-start.112 = (bf16[512,1024]{0,1:T(8,128)(2,1)}, bf16[512,1024]{0,1:T(8,128)(2,1)}, u32[]{:S(2)}, u32[]{:S(2)}) collective-permute-start(bf16[512,1024]{0,1:T(8,128)(2,1)} %broadcast_select_fusion.1), channel_id=1, source_target_pairs={{0,1},{1,0},{2,3},{3,2},{4,5},{5,4},{6,7},{7,6},{8,9},{9,8},{10,11... | collective-permute-start | bytes 3145736 | tf_op jit(solution)/shard_map/ppermute | solution.py:76
  1022.8 76.4 %collective-permute-start.77 = (bf16[256,2048]{1,0:T(8,128)(2,1)S(1)}, bf16[256,2048]{1,0:T(8,128)(2,1)}, u32[]{:S(2)}, u32[]{:S(2)}) collective-permute-start(bf16[256,2048]{1,0:T(8,128)(2,1)S(1)} %add.538), channel_id=1, source_target_pairs={{2,4},{4,2},{3,5},{5,3},{10,12},{12,10},{11,13},{13,11},{18,20},{2... | collective-permute-start | bytes 3145736 | tf_op jit(solution)/shard_map/ppermute | solution.py:115
  (215 other events, 6879.7 us)

commit v2 on v1

v2 whole, which is shorter than its diff:
```python
import jax
import jax.numpy as jnp
from jax import lax
from jax.experimental import pallas as pl
from jax.experimental.pallas import tpu as pltpu
from jax.sharding import Mesh
from jax.sharding import PartitionSpec as P

HQ = 32
HK = 8
HEAD = 64

EPS = 1e-05
BASE = 500000.0
MASKED = -1e30

BF = jnp.bfloat16
F32 = jnp.float32


def positions_of(lengths, index):
    ends = jnp.cumsum(lengths)
    starts = ends - lengths
    segment = jnp.sum((index[:, None] >= ends[None, :-1]).astype(jnp.int32), axis=1)
    member = segment[:, None] == jnp.arange(lengths.shape[0], dtype=jnp.int32)[None, :]
    start = jnp.sum(jnp.where(member, starts[None, :], 0), axis=1)
    place = jnp.where(segment == 0, index, lengths[0] + index - start)
    return (segment, place)


def matmul(left, right):
    return jnp.dot(left, right, preferred_element_type=F32)


def contract_last(left, right):
    return lax.dot_general(left, right, (((1,), (1,)), ((), ())), preferred_element_type=F32)


def contract_first(left, right):
    return lax.dot_general(left, right, (((0,), (0,)), ((), ())), preferred_element_type=F32)


def norm_back(grad_normed, unit, inverse, gain):
    scaled = grad_normed * gain
    return inverse * (scaled - unit * jnp.mean(scaled * unit, axis=1, keepdims=True))


def after(value, *others):
    return lax.optimization_barrier((value,) + others)[0]


def after(value, *others):
    return lax.optimization_barrier((value,) + others)[0]


def step_to(value, axis, step):
    size = lax.axis_size(axis)
    return lax.ppermute(value, axis, [(i, i ^ step) for i in range(size)])


def exchange(blocks):
    return lax.all_to_all(blocks, "group", 0, 0, tiled=True)


def spread(mine):
    parts = lax.axis_size("group")
    blocks = exchange(jnp.broadcast_to(mine[None], (parts,) + mine.shape))
    return blocks.reshape((parts * mine.shape[0],) + mine.shape[1:])


def from_core(value):
    return step_to(value, "core", 1)


def with_core(got):
    if lax.axis_size("core") == 1:
        return got
    return jnp.concatenate([got, from_core(got)], axis=0)


def scatter_send(partial):
    parts = lax.axis_size("group")
    if lax.axis_size("core") == 2:
        half = partial.shape[0] // 2
        partial = partial[:half] + from_core(partial[half:].astype(BF)).astype(F32)
    rows = partial.shape[0] // parts
    return partial.astype(BF).reshape((parts, rows) + partial.shape[1:])


def scatter_sum(blocks):
    return jnp.sum(exchange(blocks).astype(F32), axis=0)


def rotated(value, cosine, sine, back):
    wide = value.shape[1]
    half = HEAD // 2
    lane = lax.broadcasted_iota(jnp.int32, value.shape, 1)
    low = lane % HEAD < half
    other = jnp.where(
        low, pltpu.roll(value, wide - half, 1), pltpu.roll(value, half, 1)
    )
    sign = jnp.where(low, -1.0, 1.0)
    if back:
        sign = -sign
    return value * cosine + other * sign * sine


def visible(place_query, segment_query, place_key, segment_key):
    same = (segment_key == 0) | (segment_key == segment_query)
    return same & (place_key <= place_query)


def forward_kernel(qkv_ref, cos_ref, sin_ref, column_ref, row_ref, o_ref, kept_ref, lse_ref):
    heads = HQ // HK
    wide = heads * HEAD
    scale = HEAD ** (-0.5)
    cosine, sine = cos_ref[...], sin_ref[...]
    tiles = wide // cosine.shape[1]
    query = rotated(
        qkv_ref[:, :wide],
        jnp.concatenate([cosine] * tiles, axis=1),
        jnp.concatenate([sine] * tiles, axis=1),
        False,
    )
    query = query.astype(BF)
    pair = qkv_ref[:, wide:]
    lane = lax.broadcasted_iota(jnp.int32, pair.shape, 1)
    pair = jnp.where(lane < HEAD, rotated(pair, cosine, sine, False), pair).astype(BF)
    kept_ref[:, :wide] = query
    kept_ref[:, wide:] = pair
    key, value = pair[:, :HEAD], pair[:, HEAD:]
    allowed = visible(column_ref[:, 0:1], column_ref[:, 1:2], row_ref[0:1, :], row_ref[1:2, :])
    found = []
    for h in range(heads):
        one = query[:, h * HEAD : (h + 1) * HEAD]
        scores = jnp.where(allowed, contract_last(one, key) * scale, MASKED)
        top = jnp.max(scores, axis=1, keepdims=True)
        expo = jnp.exp(scores - top)
        denom = jnp.sum(expo, axis=1, keepdims=True)
        probs = (expo / denom).astype(BF)
        o_ref[:, h * HEAD : (h + 1) * HEAD] = matmul(probs, value).astype(BF)
        found.append(top + jnp.log(denom))
    place = lax.broadcasted_iota(jnp.int32, lse_ref.shape, 1)
    total = jnp.zeros(lse_ref.shape, F32)
    for h in range(heads):
        total = jnp.where(place == h, found[h], total)
    lse_ref[...] = total


def backward_kernel(
    kept_ref, lse_ref, grad_ref, cos_ref, sin_ref, column_ref, row_ref, out_ref, hold_ref
):
    heads = HQ // HK
    wide = heads * HEAD
    scale = HEAD ** (-0.5)
    key = kept_ref[:, wide : wide + HEAD]
    value = kept_ref[:, wide + HEAD :]
    allowed = visible(column_ref[:, 0:1], column_ref[:, 1:2], row_ref[0:1, :], row_ref[1:2, :])
    total = key.shape[0]
    grad_k = jnp.zeros((total, HEAD), F32)
    grad_v = jnp.zeros((total, HEAD), F32)
    for h in range(heads):
        one = kept_ref[:, h * HEAD : (h + 1) * HEAD]
        grad = grad_ref[:, h * HEAD : (h + 1) * HEAD]
        scores = jnp.where(allowed, contract_last(one, key) * scale, MASKED)
        probs = jnp.exp(scores - lse_ref[:, h : h + 1])
        grad_p = contract_last(grad, value)
        grad_s = probs * (grad_p - jnp.sum(probs * grad_p, axis=1, keepdims=True))
        grad_s = grad_s.astype(BF)
        hold_ref[:, h * HEAD : (h + 1) * HEAD] = matmul(grad_s, key) * scale
        grad_k = grad_k + contract_first(grad_s, one)
        grad_v = grad_v + contract_first(probs.astype(BF), grad)
    hold_ref[:, wide : wide + HEAD] = grad_k * scale
    hold_ref[:, wide + HEAD :] = grad_v
    cosine, sine = cos_ref[...], sin_ref[...]
    tiles = wide // cosine.shape[1]
    out_ref[:, :wide] = rotated(
        hold_ref[:, :wide],
        jnp.concatenate([cosine] * tiles, axis=1),
        jnp.concatenate([sine] * tiles, axis=1),
        True,
    ).astype(BF)
    pair = hold_ref[:, wide:]
    lane = lax.broadcasted_iota(jnp.int32, pair.shape, 1)
    pair = jnp.where(lane < HEAD, rotated(pair, cosine, sine, True), pair)
    out_ref[:, wide:] = pair.astype(BF)


def by_group(kernel, total, groups, inputs, outputs, scratch=()):
    def spec(shape):
        if len(shape) == 3:
            return pl.BlockSpec((None,) + shape[1:], lambda i: (i, 0, 0))
        return pl.BlockSpec((total, shape[1]), lambda i: (i, 0))

    return pl.pallas_call(
        kernel,
        grid=(groups,),
        in_specs=[spec(one.shape) for one in inputs],
        out_specs=[spec(one.shape) for one in outputs],
        out_shape=list(outputs),
        scratch_shapes=list(scratch),
        compiler_params=pltpu.CompilerParams(vmem_limit_bytes=40 * 2**20),
        cost_estimate=pl.CostEstimate(flops=0, bytes_accessed=1, transcendentals=0),
    )(*inputs)


class Clock:
    def __init__(self):
        self.token = jnp.zeros((8, 128), F32)

    def tick(self, *values):
        flat, tree = jax.tree.flatten(values)
        out = lax.optimization_barrier((self.token, *flat))
        self.token = out[0]
        values = jax.tree.unflatten(tree, out[1:])
        return values[0] if len(values) == 1 else values

    def now(self, value):
        return after(value, self.token)


class Line:
    def __init__(self, clock, shape):
        self.clock = clock
        self.shape = shape
        place = lax.axis_index("rest")
        self.inner = (place == 1) | (place == 2)
        self.sums = {}
        self.flight = {}

    def piece(self, array, block):
        rows, wide = self.shape
        if array.ndim == 3:
            return array[block[0]]
        row, column = block
        return array[row * rows : (row + 1) * rows, column * wide : (column + 1) * wide]

    def slot(self, entering, *values):
        last = self.flight
        came, moved, values = self.clock.tick(last.get("came"), last.get("moved"), values)
        flight = {}
        send = None
        if last.get("across"):
            name, part = last["across"]
            full = (part.astype(F32) + moved.astype(F32)).astype(BF)
            flight["out"] = (name, full)
            send = full
        if entering is not None:
            name, array, block = entering
            array = self.clock.now(array)
            flight["enter"] = (name, array, block)
            piece = self.piece(array, block)
            send = piece if send is None else jnp.where(self.inner, send, piece)
        if last.get("enter"):
            name, array, block = last["enter"]
            part = (self.piece(array, block).astype(F32) + came.astype(F32)).astype(BF)
            flight["across"] = (name, part)
            flight["moved"] = lax.ppermute(part, "rest", [(1, 2), (2, 1)])
        if send is not None:
            flight["came"] = lax.ppermute(send, "rest", [(0, 1), (1, 0), (2, 3), (3, 2)])
        if last.get("out"):
            name, full = last["out"]
            self.sums[name] = jnp.where(self.inner, full, came)
        self.flight = flight
        return values[0] if len(values) == 1 else values

    def stack(self, name, count):
        return jnp.stack([self.sums[name, k] for k in range(count)])


def place(shape, mine, other, rows, wide, blocks):
    core = lax.axis_index("core")
    table = jnp.asarray(
        [[list(there) + list(here(k)) for k in range(2)] for there, here in blocks], jnp.int32
    )
    table = jnp.stack([table[:, 0], table[:, 1]])
    table = jnp.where(core == 0, table, table[::-1])
    count = len(blocks)
    table = table.reshape(-1)
    size = table.shape[0] // (2 * count)

    def entry(w, k, j, field):
        return w[(k * count + j) * size + field]

    def source(k, j, w, own):
        j = jnp.where(k == own, j, count - 1 if own == 0 else 0)
        return tuple(entry(w, k, j, field) for field in range(3))

    def kernel(table_ref, mine_ref, other_ref, out_ref):
        @pl.when(pl.program_id(0) == 0)
        def _():
            out_ref[...] = mine_ref[...].astype(F32)

        @pl.when(pl.program_id(0) == 1)
        def _():
            out_ref[...] = other_ref[...].astype(F32)

    return pl.pallas_call(
        kernel,
        grid_spec=pltpu.PrefetchScalarGridSpec(
            num_scalar_prefetch=1,
            grid=(2, count),
            in_specs=[
                pl.BlockSpec((None, rows, wide), lambda k, j, w: source(k, j, w, 0)),
                pl.BlockSpec((None, rows, wide), lambda k, j, w: source(k, j, w, 1)),
            ],
            out_specs=pl.BlockSpec(
                (rows, wide), lambda k, j, w: (entry(w, k, j, 3), entry(w, k, j, 4))
            ),
        ),
        out_shape=jax.ShapeDtypeStruct(shape, F32),
        compiler_params=pltpu.CompilerParams(vmem_limit_bytes=16 * 2**20),
        cost_estimate=pl.CostEstimate(
            flops=0, bytes_accessed=12 * count * rows * wide, transcendentals=0
        ),
    )(table, mine, other)


def body(
    tokens,
    seq_lengths,
    attn_gain,
    w_query,
    w_key,
    w_value,
    w_out,
    mlp_gain,
    w_gate,
    w_up,
    w_down,
    cotangent,
):
    parts = lax.axis_size("group")
    cores = lax.axis_size("core")
    g = lax.axis_index("group")
    c = lax.axis_index("core")
    rows, width = tokens.shape[1:]
    total = rows * parts
    team = parts * cores
    heads = HQ // HK
    scale = HEAD ** (-0.5)
    ff = w_gate.shape[1] // team
    share = w_gate.shape[0]
    qw = HQ * HEAD // team
    kw = HK * HEAD // team
    assert kw == HEAD

    def columns(weight, size, rows=slice(None)):
        return jnp.stack(
            [
                lax.dynamic_slice_in_dim(weight[rows], (k * cores + c) * size, size, 1)
                for k in range(parts)
            ]
        )

    def fetch(blocks):
        return [
            step_to(lax.dynamic_index_in_dim(blocks, g ^ s, 0, keepdims=False), "group", s)
            for s in range(1, parts)
        ]

    def in_order(own, got):
        out = jnp.zeros((parts,) + own.shape, own.dtype)
        for s, block in enumerate([own] + got):
            out = lax.dynamic_update_slice_in_dim(out, block[None], g ^ s, 0)
        return out.reshape((parts * own.shape[0],) + own.shape[1:])

    def own_columns(weight, size):
        return lax.dynamic_slice_in_dim(weight, (g * cores + c) * size, size, 1)

    clock = Clock()
    x_mine = tokens[0]
    extra = 2 * share // width if 2 * share > width else 1
    gains = jnp.concatenate([attn_gain, mlp_gain])
    gains = jnp.pad(gains, (0, 16 * width - gains.shape[0])).reshape(16, width)
    x_got = spread(jnp.concatenate([x_mine, gains], axis=0))
    x_got = x_got.reshape(parts, rows + 16, width)
    gains = x_got[:, rows].reshape(parts, width)[:, : 2 * share]
    gain_one = gains[:, :share].reshape(-1).astype(F32)
    gain_two = gains[:, share:].reshape(-1).astype(F32)
    x_got = x_got[:, :rows].reshape(parts * rows, width)
    qkv_send = jnp.concatenate(
        [columns(w_query, qw), columns(w_key, kw), columns(w_value, kw)], axis=2
    )
    qkv_got = fetch(qkv_send)
    qkv_own = lax.dynamic_index_in_dim(qkv_send, g, 0, keepdims=False)

    paired = lax.axis_size("rest") == 4
    even = lax.axis_index("rest") % 2 == 0
    halves = [slice(0, share // 4 * 3), slice(share // 4 * 3, share)]
    sends = []
    for half in halves:
        gate_send = columns(w_gate, ff, half)
        up_send = columns(w_up, ff, half)
        sends.append([jnp.where(even, gate_send, up_send)] if paired else [gate_send, up_send])
    lengths = [seq_lengths[0]]
    if cores == 2:
        lengths.append(from_core(seq_lengths[0]))
    index = jnp.arange(total, dtype=jnp.int32)
    marks = [positions_of(one, index) for one in lengths]
    half = HEAD // 2
    freq = BASE ** (-(2.0 * jnp.arange(half, dtype=F32)) / HEAD)
    place_all = jnp.concatenate([one[1] for one in marks]).astype(F32)
    angle = place_all[:, None] * jnp.tile(freq, 128 // half)[None, :]
    cosine, sine = jnp.cos(angle), jnp.sin(angle)
    marks_row = jnp.stack([jnp.stack([one[1], one[0]]) for one in marks])
    marks_column = marks_row.transpose(0, 2, 1)
    x_got, qkv_got, sends, cosine, sine, marks_row, marks_column = clock.tick(
        x_got, qkv_got, sends, cosine, sine, marks_row, marks_column
    )

    out_rows = lax.dynamic_slice_in_dim(w_out, c * qw, qw, 0)
    down_rows = lax.dynamic_slice_in_dim(w_down, c * ff, ff, 0)
    first_got = [[fetch(one) for one in sends[0]]]
    second_got = []
    qkv_full = in_order(qkv_own, qkv_got)
    x_all = with_core(x_got)

    def swap(got):
        return step_to(jnp.stack(got[0]), "rest", 1)

    def fill(out, got, row):
        for s in range(1, parts):
            out = lax.dynamic_update_slice(out, got[s - 1][None], (g ^ s, row, 0))
        return out

    def begin(own):
        return lax.dynamic_update_slice_in_dim(
            jnp.zeros((parts, share, ff), BF), own[None], g, 0
        )

    def ordered(first, second):
        if not paired:
            return first, second
        return jnp.where(even, first, second), jnp.where(even, second, first)

    x = x_all.astype(F32)
    inverse_all = lax.rsqrt(jnp.mean(x * x, axis=1, keepdims=True) + EPS)
    normed_one = (x * inverse_all * gain_one).astype(BF)
    qkv = matmul(normed_one, qkv_full)
    attended, kept, logsum = by_group(
        forward_kernel,
        total,
        cores,
        [qkv, cosine, sine, marks_column, marks_row],
        [
            jax.ShapeDtypeStruct((cores * total, qw), BF),
            jax.ShapeDtypeStruct((cores * total, qw + 2 * kw), BF),
            jax.ShapeDtypeStruct((cores * total, 128), F32),
        ],
    )
    x_own = x_mine.astype(F32)
    send = scatter_send(matmul(attended, out_rows))
    send, first_got, kept, attended, logsum = clock.tick(
        send, first_got, kept, attended, logsum
    )

    if paired:
        second_got.append(swap(first_got[0]))
    first_got.append([fetch(clock.now(one)) for one in sends[1]])
    own = [own_columns(w_gate, ff), own_columns(w_up, ff)]
    if paired:
        own = ordered(*own)
    first_full = fill(begin(clock.now(own[0])), first_got[0][0], 0)
    second_full = begin(clock.now(own[1]))
    mid = x_own + scatter_sum(send)
    mid, first_got, first_full, second_full = clock.tick(
        mid, first_got, first_full, second_full
    )

    inverse_two = lax.rsqrt(jnp.mean(mid * mid, axis=1, keepdims=True) + EPS)
    unit_two = mid * inverse_two
    if paired:
        second_got.append(swap(first_got[1]))
    normed_two = spread((unit_two * gain_two).astype(BF))
    cot_all = spread(clock.now(cotangent[0]))
    split = share // 4 * 3
    first_full = fill(first_full, first_got[1][0], split)
    others = second_got if paired else [got[1] for got in first_got]
    second_full = fill(second_full, others[0], 0)
    normed_two, second_got, unit_two, inverse_two, first_full, second_full = clock.tick(
        normed_two, second_got, unit_two, inverse_two, first_full, second_full
    )
    normed_two = with_core(normed_two)
    cot_all = with_core(cot_all)
    others = second_got if paired else [got[1] for got in first_got]
    second_full = fill(second_full, others[1], split)
    first_full = first_full.reshape(share * parts, ff)
    second_full = second_full.reshape(share * parts, ff)
    gate, up = ordered(matmul(normed_two, first_full), matmul(normed_two, second_full))
    sigma = jax.nn.sigmoid(gate)
    active = (gate * sigma * up).astype(BF)
    grad_down = contract_first(active, cot_all).astype(BF)
    on_line = paired and cores == 2
    line = Line(clock, (share, ff))
    outs = {}

    def slot(entering, *values):
        if on_line:
            return line.slot(entering, *values)
        return clock.tick(*values) if values else None

    active, cot_all, grad_down = slot(
        (("down", 0), grad_down, (0, 0)), active, cot_all, grad_down
    )
    grad_active = contract_last(cot_all, down_rows)
    grad_gate_pre = (grad_active * up * sigma * (1.0 + gate * (1.0 - sigma))).astype(BF)
    grad_up_pre = (grad_active * gate * sigma).astype(BF)
    grad_gate_pre, grad_up_pre = slot(
        (("down", 1), grad_down, (0, 1)), grad_gate_pre, grad_up_pre
    )
    first_pre, second_pre = ordered(grad_gate_pre, grad_up_pre)
    send = scatter_send(
        contract_last(first_pre, first_full) + contract_last(second_pre, second_full)
    )
    send = slot((("down", 2), grad_down, (1, 0)), send)
    grad_normed_two = scatter_sum(send)
    grad_gate = contract_first(normed_two, clock.now(grad_gate_pre)).astype(BF)
    grad_gate = slot((("down", 3), grad_down, (1, 1)), grad_gate)
    grad_up = contract_first(normed_two, clock.now(grad_up_pre)).astype(BF)
    grad_up, grad_normed_two = slot((("gate", 0), grad_gate, (0, 0)), grad_up, grad_normed_two)
    grad_y = cotangent[0].astype(F32)
    grad_gain_two = jnp.sum(grad_normed_two * unit_two, axis=0)
    grad_mid = grad_y + norm_back(grad_normed_two, unit_two, inverse_two, gain_two)
    grad_branch = spread(grad_mid.astype(BF))
    send = scatter_send(matmul(clock.now(active), down_rows))
    grad_mid, grad_gain_two, send = slot(
        (("gate", 1), grad_gate, (1, 0)), grad_mid, grad_gain_two, send
    )
    grad_branch = slot((("gate", 2), grad_gate, (2, 0)), grad_branch)
    result = mid + scatter_sum(clock.now(send))
    grad_branch = with_core(grad_branch)
    grad_attended = contract_last(grad_branch, out_rows).astype(BF)
    grad_out = contract_first(attended, grad_branch).astype(BF)

    def both(mine):
        mine = clock.now(mine)
        return mine, from_core(mine)

    (grad_qkv,) = by_group(
        backward_kernel,
        total,
        cores,
        [kept, logsum, grad_attended, cosine, sine, marks_column, marks_row],
        [jax.ShapeDtypeStruct((cores * total, qw + 2 * kw), BF)],
        [pltpu.VMEM((total, qw + 2 * kw), F32)],
    )
    grad_qkv, grad_out, result = slot(
        (("gate", 3), grad_gate, (3, 0)), grad_qkv, grad_out, result
    )
    grad_weights = contract_first(normed_one, grad_qkv).astype(BF)
    send = scatter_send(contract_last(grad_qkv, qkv_full))
    grad_weights, send = slot((("up", 0), grad_up, (0, 0)), grad_weights, send)
    grad_normed_one = scatter_sum(send)
    if on_line:
        outs["down"] = place(
            (ff * 2, width),
            *both(line.stack("down", 4)),
            share,
            ff,
            [
                ((a * 2 + b, 0, 0), lambda k, a=a, b=b: (k * 2 + a, b))
                for a in range(2)
                for b in range(2)
            ],
        )
        grad_out = jnp.concatenate([grad_out[:, :ff], grad_out[:, ff:]], axis=0)
    outs = slot((("up", 1), grad_up, (1, 0)), outs)
    grad_normed_one, outs = slot((("up", 2), grad_up, (2, 0)), grad_normed_one, outs)
    turned = exchange(clock.now(grad_weights).reshape(parts, share, qw + 2 * kw))
    inverse_one = lax.rsqrt(jnp.mean(x_own * x_own, axis=1, keepdims=True) + EPS)
    unit_one = x_own * inverse_one
    grad_gain_one = jnp.sum(grad_normed_one * unit_one, axis=0)
    grad_x = grad_mid + norm_back(grad_normed_one, unit_one, inverse_one, gain_one)
    grad_gains = jnp.stack([grad_gain_one, grad_gain_two]).reshape(2, parts, share)
    grad_gains = jnp.sum(exchange(grad_gains.transpose(1, 0, 2)), axis=0)
    turned, grad_x = slot((("up", 3), grad_up, (3, 0)), turned, grad_x)
    turned_q = turned[:, :, :qw].transpose(1, 0, 2).reshape(share, parts * qw)
    turned_kv = turned[:, :, qw:].transpose(1, 0, 2).reshape(share, parts * 2 * kw)
    grad_gains, turned_q, turned_kv = slot(
        (("rows", 0), grad_out, (0, 0)), grad_gains, turned_q, turned_kv
    )
    if on_line:
        turned_kv = jnp.concatenate(
            [
                turned_kv,
                jnp.pad(
                    grad_gains.astype(BF), ((0, share - 2), (0, ff - parts * 2 * kw - share))
                ),
            ],
            axis=1,
        )

        def turn(name):
            return exchange(line.stack(name, parts))

        def place_columns(turned):
            return place(
                (share, ff * team),
                *both(turned),
                share,
                ff,
                [((j, 0, 0), lambda k, j=j: (0, j * 2 + k)) for j in range(parts)],
            )

        gate_turned = turn("gate")
        turned_kv = slot((("heads", 0), turned_q, (0, 0)), turned_kv)
        gate_turned = slot((("heads", 1), turned_kv, (0, 0)), gate_turned)
        outs["gate"] = place_columns(gate_turned)
        up_turned = turn("up")
        outs, up_turned = slot(None, outs, up_turned)
        outs["up"] = place_columns(up_turned)
        outs["out"] = place(
            (qw * 2, width),
            *both(line.stack("rows", 1)),
            qw,
            ff,
            [((0, b, 0), lambda k, b=b: (k, b)) for b in range(2)],
        )
        outs = slot(None, outs)
        slot(None)
        mine, other = both(line.stack("heads", 2))
        grad_gains = sum(
            one[1, :2, parts * 2 * kw : parts * 2 * kw + share].astype(F32) for one in (mine, other)
        )
        outs["query"] = place(
            (share, qw * team),
            mine,
            other,
            share,
            qw,
            [((0, 0, j), lambda k, j=j: (0, j * 2 + k)) for j in range(parts)],
        )
        narrow = [
            one[1, :, : parts * 2 * kw].reshape(share, parts, 2 * kw) for one in (mine, other)
        ]
        narrow = jnp.stack(
            [jnp.where(c == 0, *narrow), jnp.where(c == 0, *narrow[::-1])], axis=2
        ).astype(F32)
        outs["key"] = narrow[..., :kw].reshape(share, team * kw)
        outs["value"] = narrow[..., kw:].reshape(share, team * kw)
    else:
        def whole(value):
            value = lax.psum(value, "rest")[None]
            if cores == 2:
                other = from_core(value)
                value = jnp.concatenate(
                    [jnp.where(c == 0, value, other), jnp.where(c == 0, other, value)]
                )
            return value.astype(F32)

        def beside(value):
            return value.transpose(2, 1, 0, 3).reshape(share, -1)

        grad_gains = lax.psum(grad_gains, ("rest", "core"))
        outs["down"] = whole(grad_down).reshape(cores * ff, width)
        outs["out"] = whole(grad_out).reshape(cores * qw, width)
        for name, grad in (("gate", grad_gate), ("up", grad_up)):
            outs[name] = beside(whole(exchange(grad.reshape(parts, share, ff))))
        turned = whole(turned)
        outs["query"] = beside(turned[..., :qw])
        outs["key"] = beside(turned[..., qw : qw + kw])
        outs["value"] = beside(turned[..., qw + kw :])
    return (
        result.astype(BF)[None],
        grad_x.astype(BF)[None],
        grad_gains[0],
        outs["query"],
        outs["key"],
        outs["value"],
        outs["out"],
        grad_gains[1],
        outs["gate"],
        outs["up"],
        outs["down"],
    )


def solution(mesh):
    parts, replicas = mesh.devices.shape
    cores = 2 if HK % (2 * parts) == 0 and replicas % 2 == 0 else 1
    split = Mesh(
        mesh.devices.reshape(parts, replicas // cores, cores), ("group", "rest", "core")
    )
    replica = ("rest", "core")
    weights = (P("group"),) + (P("group", None),) * 4 + (P("group"),) + (P("group", None),) * 3
    split_tokens = P(replica, "group", None)
    return jax.shard_map(
        body,
        mesh=split,
        in_specs=(split_tokens, P(replica, None)) + weights + (split_tokens,),
        out_specs=(split_tokens, split_tokens) + weights,
        check_vma=False,
    )
```

time: 1210 us -> 921 us (0.76)
  waiting for transfers between devices: 507 us -> 310 us
  local copies, waits for them, and re-layouts: 215 us -> 104 us
  Pallas kernels: 0 us -> 68.7 us
  starting transfers between devices: 206 us -> 149 us
  other arithmetic: 138 us -> 184 us
  blocking collectives: 40.7 us -> 0 us
    ppermute x51 -> x32, waiting for transfers between devices: 333 us -> 199 us  [the longest x17 199 us: slot(): lax.ppermute(send, 'rest', [(0, 1), (1, 0), (2, 3), (3, 2)])]
    ppermute x83 -> x25, waiting for transfers between devices: 173 us -> 44 us  [step_to(): return lax.ppermute(value, axis, [(i, i ^ step) for i in range(size)])]
    ppermute x83 -> x25, starting transfers between devices: 109 us -> 35.8 us  [step_to(): return lax.ppermute(value, axis, [(i, i ^ step) for i in range(size)])]
    pallas_call x0 -> x7, Pallas kernels: none -> 68.7 us  [the longest x5 46.9 us: place(): pl.pallas_call(kernel, grid_spec=pltpu.PrefetchScalarGridSpec(num_scalar_...]
    all_to_all x0 -> x12, waiting for transfers between devices: none -> 67.3 us  [exchange(): return lax.all_to_all(blocks, 'group', 0, 0, tiled=True)]
    all_to_all x0 -> x12, starting transfers between devices: none -> 54.3 us  [exchange(): return lax.all_to_all(blocks, 'group', 0, 0, tiled=True)]
    convert_element_type x6 -> x25, other arithmetic: 4.98 us -> 56.9 us  [the longest x15 32.6 us: slot(): part = (self.piece(array, block).astype(F32) + came.astype(F32)).astype(BF)]
    psum x1 -> x0, blocking collectives: 40.7 us -> none  [body(): lax.psum(jnp.stack([grad_gain_one, grad_gain_two]), ('group', 'rest', 'co...]
  transfers between devices with their start and end apart: 134 -> 69, of which waited for: 47 -> 30; matrix products, arithmetic and copies ran while one was open for 32% -> 33% of each run, Pallas kernels for 0% -> 6%
where the time goes in v2:
time: 921 us; the launch traced here: 914 us
  waiting for transfers between devices  310 us (34%)
  other arithmetic  184 us (20%)
  starting transfers between devices  149 us (16%)
  local copies, waits for them, and re-layouts  104 us (11%)
  matrix products  95.5 us (10%)
  Pallas kernels  68.7 us (7%)
    ppermute x17, waiting for transfers between devices, slot(): lax.ppermute(send, 'rest', [(0, 1), (1, 0), (2, 3), (3, 2)])  199 us
    all_to_all x12, waiting for transfers between devices, exchange(): return lax.all_to_all(blocks, 'group', 0, 0, tiled=True)  67.3 us
    all_to_all x12, starting transfers between devices, exchange(): return lax.all_to_all(blocks, 'group', 0, 0, tiled=True)  54.3 us
    another operation x19, other arithmetic, stack(): return jnp.stack([self.sums[name, k] for k in range(count)])  48.8 us
    pallas_call x5, Pallas kernels, place(): pl.pallas_call(kernel, grid_spec=pltpu.PrefetchScalarGridSpec(num_scalar_...  46.9 us
    ppermute x25, waiting for transfers between devices, step_to(): return lax.ppermute(value, axis, [(i, i ^ step) for i in range(size)])  44 us
    select_n x13, other arithmetic, slot(): send = piece if send is None else jnp.where(self.inner, send, piece)  35.9 us
    ppermute x25, starting transfers between devices, step_to(): return lax.ppermute(value, axis, [(i, i ^ step) for i in range(size)])  35.8 us
  transfers between devices with their start and end apart: 69, of which 30 were waited for; matrix products, arithmetic and copies ran while one was open for 33% of the time, Pallas kernels for 6%

profile of v2, /device:TPU:1, one launch (start us, length us, event | category | flops | bytes accessed | tf_op | source)
XLA Modules:
  0.0 913.5 jit_solution(13385749486810892275)
XLA Ops:
  46.2 8.7 all-to-all-done
  73.1 9.9 %shard_map.248 = (bf16[1024,256]{1,0:T(8,128)(2,1)S(1)}, bf16[1024,384]{1,0:T(8,128)(2,1)S(1)}, f32[1024,128]{1,0:T(8,128)S(1)}) custom-call(f32[1024,384]{1,0:T(8,128)S(1)} %fusion.41.qkv_ref, f32[1024,128]{1,0:T(8,128)S(1)} %copy-done.1, f32[1024,128]{1,0:T(8,128)S(1)} %get-tuple-element.163.sin_ref, s32[2,512,2]{2,1,0:T(8,128)S(1)} %copy.55.column_ref, ...), custom_call_target="tpu_custom_call" | custom-call | bytes 1 | tf_op jit(solution)/shard_map/pallas_call | solution.py:195
  100.3 9.0 collective-permute-done.6
  109.9 17.1 %collective-permute-done.8 = bf16[384,1024]{1,0:T(8,128)(2,1)} collective-permute-done((bf16[384,1024]{1,0:T(8,128)(2,1)S(1)}, bf16[384,1024]{1,0:T(8,128)(2,1)}, u32[]{:S(2)}, u32[]{:S(2)}) %collective-permute-start.8) | collective-permute-done | bytes 786464 | tf_op jit(solution)/shard_map/ppermute | solution.py:58
  158.8 8.3 collective-permute-done.10
  188.7 10.2 %all-to-all-done.2 = bf16[4,128,2048]{2,1,0:T(8,128)(2,1)} async-done(((bf16[4,128,2048]{2,1,0:T(8,128)(2,1)}), bf16[4,128,2048]{2,1,0:T(8,128)(2,1)}, u32[]{:S(2)}, u32[]{:S(2)}) %all-to-all-start.2) | async-done | bytes 2097184 | tf_op jit(solution)/shard_map/all_to_all | solution.py:62
  212.2 18.8 %all-to-all-done.3 = bf16[4,128,2048]{2,1,0:T(8,128)(2,1)} async-done(((bf16[4,128,2048]{2,1,0:T(8,128)(2,1)}), bf16[4,128,2048]{2,1,0:T(8,128)(2,1)}, u32[]{:S(2)}, u32[]{:S(2)}) %all-to-all-start.3) | async-done | bytes 2097184 | tf_op jit(solution)/shard_map/all_to_all | solution.py:62
  240.9 7.8 fusion.47
  248.8 11.2 %multiply_convert_fusion.2 = (bf16[1024,1024]{1,0:T(8,128)(2,1)S(1)}, f32[1024,1024]{1,0:T(8,128)}, f32[1024,1024]{1,0:T(8,128)}) fusion(f32[1024,1024]{1,0:T(8,128)S(1)} %fusion.47, pred[]{:T(512)S(6)} %eq.74, bf16[1024,2048]{1,0:T(8,128)(2,1)S(1)} %constant_dynamic-update-slice_fusion.6, bf16[2048,1024]{1,0:T(8,128)(2,1)} %bitcast.72), kind=kOutput, calls=%fused_computation.27 | convolution fusion | flops 4303355904 | bytes 23068672 | tf_op jit(solution)/shard_map/dot_general | solution.py:32
  270.9 10.6 %multiply_convert_fusion = (bf16[1024,1024]{1,0:T(8,128)(2,1)S(1)}, bf16[1024,1024]{1,0:T(8,128)(2,1)}) fusion(f32[1024,1024]{1,0:T(8,128)} %get-tuple-element.354, f32[1024,1024]{1,0:T(8,128)} %get-tuple-element.417, f32[1024,1024]{1,0:T(8,128)} %copy-done.90, pred[]{:T(512)S(6)} %eq.74, bf16[1024,2048]{1,0:T(8,128)(2,1)S(1)} %pad_maximum_fusion.1, ...), kind=kOutput, calls=%fused_computation.25 | convolution fusion | flops 4309647360 | bytes 25165828 | tf_op jit(solution)/shard_map/dot_general | solution.py:36
  281.5 12.9 %collective-permute-done.16 = bf16[512,1024]{1,0:T(8,128)(2,1)S(1)} collective-permute-done((bf16[512,1024]{1,0:T(8,128)(2,1)S(1)}, bf16[512,1024]{1,0:T(8,128)(2,1)S(1)}, u32[]{:S(2)}, u32[]{:S(2)}) %collective-permute-start.16) | collective-permute-done | bytes 1048608 | tf_op jit(solution)/shard_map/ppermute | solution.py:260
  294.4 10.3 %fusion.11 = f32[1024,2048]{1,0:T(8,128)} fusion(bf16[2048,1024]{1,0:T(8,128)(2,1)} %bitcast.72, bf16[1024,1024]{1,0:T(8,128)(2,1)S(1)} %get-tuple-element.210, bf16[1024,1024]{1,0:T(8,128)(2,1)} %get-tuple-element.205, pred[]{:T(512)S(6)} %eq.74), kind=kOutput, calls=%fused_computation.73 | convolution fusion | flops 4296015872 | bytes 16777216 | tf_op jit(solution)/shard_map/dot_general | solution.py:36
  304.7 9.2 %convolution_add_fusion = f32[1024,2048]{1,0:T(8,128)S(1)} fusion(f32[1024,2048]{1,0:T(8,128)} %fusion.11, bf16[2048,1024]{1,0:T(8,128)(2,1)} %bitcast.71, bf16[1024,1024]{1,0:T(8,128)(2,1)S(1)} %copy-done.89, bf16[1024,1024]{1,0:T(8,128)(2,1)} %copy-done.87, pred[]{:T(512)S(6)} %eq.74), kind=kOutput, calls=%fused_computation.30 | convolution fusion | flops 4298113024 | bytes 25165824 | tf_op jit(solution)/shard_map/dot_general | solution.py:36
  329.0 18.3 %collective-permute-done.17 = bf16[512,1024]{1,0:T(8,128)(2,1)} collective-permute-done((bf16[512,1024]{1,0:T(8,128)(2,1)}, bf16[512,1024]{1,0:T(8,128)(2,1)}, u32[]{:S(2)}, u32[]{:S(2)}) %collective-permute-start.17) | collective-permute-done | bytes 1048608 | tf_op jit(solution)/shard_map/ppermute | solution.py:260
  362.2 9.6 %convolution_convert_fusion.1 = bf16[2048,1024]{1,0:T(8,128)(2,1)} fusion(bf16[1024,2048]{1,0:T(8,128)(2,1)} %copy-done.64, bf16[1024,1024]{1,0:T(8,128)(2,1)} %get-tuple-element.205), kind=kOutput, calls=%fused_computation.32 | convolution fusion | flops 4297064448 | bytes 10485760 | tf_op jit(solution)/shard_map/dot_general | solution.py:40
  371.8 7.8 collective-permute-done.20
  397.0 12.4 %collective-permute-done.22 = bf16[512,1024]{1,0:T(8,128)(2,1)} collective-permute-done((bf16[512,1024]{1,0:T(8,128)(2,1)}, bf16[512,1024]{1,0:T(8,128)(2,1)}, u32[]{:S(2)}, u32[]{:S(2)}) %collective-permute-start.22) | collective-permute-done | bytes 1048608 | tf_op jit(solution)/shard_map/ppermute | solution.py:260
  445.6 9.1 collective-permute-done.24
  464.9 19.4 %collective-permute-done.27 = bf16[512,1024]{1,0:T(8,128)(2,1)} collective-permute-done((bf16[512,1024]{1,0:T(8,128)(2,1)}, bf16[512,1024]{1,0:T(8,128)(2,1)}, u32[]{:S(2)}, u32[]{:S(2)}) %collective-permute-start.27) | collective-permute-done | bytes 1048608 | tf_op jit(solution)/shard_map/ppermute | solution.py:260
  524.1 11.9 %shard_map.249 = bf16[1024,384]{1,0:T(8,128)(2,1)S(1)} custom-call(bf16[1024,384]{1,0:T(8,128)(2,1)S(1)} %copy-done.4, f32[1024,128]{1,0:T(8,128)S(1)} %copy-done.8, bf16[1024,256]{1,0:T(8,128)(2,1)S(1)} %convolution_convert_fusion.5.grad_ref, f32[1024,128]{1,0:T(8,128)S(1)} %copy-done.2, f32[1024,128]{1,0:T(8,128)S(1)} %get-tuple-element.163.sin_ref, ...), custom_call_target="tpu_custom_call" | custom-call | bytes 1 | tf_op jit(solution)/shard_map/pallas_call | solution.py:195
  567.1 15.2 %collective-permute-done.32 = bf16[512,1024]{1,0:T(8,128)(2,1)S(1)} collective-permute-done((bf16[512,1024]{1,0:T(8,128)(2,1)S(1)}, bf16[512,1024]{1,0:T(8,128)(2,1)S(1)}, u32[]{:S(2)}, u32[]{:S(2)}) %collective-permute-start.32) | collective-permute-done | bytes 1048608 | tf_op jit(solution)/shard_map/ppermute | solution.py:260
  594.5 11.9 %shard_map.250 = f32[2048,2048]{1,0:T(8,128)} custom-call(s32[40]{0:T(128)S(1)} %reshape.323.table_ref, bf16[4,512,1024]{2,1,0:T(8,128)(2,1)} %pad_maximum_fusion.2.mine_ref, bf16[4,512,1024]{2,1,0:T(8,128)(2,1)} %collective-permute-done.37.other_ref), custom_call_target="tpu_custom_call" | custom-call | bytes 25165824 | tf_op jit(solution)/shard_map/pallas_call | solution.py:298
  633.3 11.5 %collective-permute-done.38 = bf16[512,1024]{1,0:T(8,128)(2,1)} collective-permute-done((bf16[512,1024]{1,0:T(8,128)(2,1)}, bf16[512,1024]{1,0:T(8,128)(2,1)}, u32[]{:S(2)}, u32[]{:S(2)}) %collective-permute-start.38) | collective-permute-done | bytes 1048608 | tf_op jit(solution)/shard_map/ppermute | solution.py:260
  662.6 15.5 %collective-permute-done.40 = bf16[512,1024]{1,0:T(8,128)(2,1)} collective-permute-done((bf16[512,1024]{1,0:T(8,128)(2,1)S(1)}, bf16[512,1024]{1,0:T(8,128)(2,1)}, u32[]{:S(2)}, u32[]{:S(2)}) %collective-permute-start.40) | collective-permute-done | bytes 1048608 | tf_op jit(solution)/shard_map/ppermute | solution.py:260
  717.0 17.5 %collective-permute-done.44 = bf16[512,1024]{1,0:T(8,128)(2,1)S(1)} collective-permute-done((bf16[512,1024]{1,0:T(8,128)(2,1)S(1)}, bf16[512,1024]{1,0:T(8,128)(2,1)S(1)}, u32[]{:S(2)}, u32[]{:S(2)}) %collective-permute-start.44) | collective-permute-done | bytes 1048608 | tf_op jit(solution)/shard_map/ppermute | solution.py:260
  751.1 8.5 collective-permute-done.46
  789.0 11.6 %shard_map.251 = f32[512,8192]{1,0:T(8,128)} custom-call(s32[40]{0:T(128)S(1)} %reshape.327.table_ref, bf16[4,512,1024]{2,1,0:T(8,128)(2,1)} %all-to-all-done.10.mine_ref, bf16[4,512,1024]{2,1,0:T(8,128)(2,1)} %collective-permute-done.50.other_ref), custom_call_target="tpu_custom_call" | custom-call | bytes 25165824 | tf_op jit(solution)/shard_map/pallas_call | solution.py:298
  800.7 12.7 %collective-permute-done.48 = bf16[512,1024]{1,0:T(8,128)(2,1)S(1)} collective-permute-done((bf16[512,1024]{1,0:T(8,128)(2,1)}, bf16[512,1024]{1,0:T(8,128)(2,1)S(1)}, u32[]{:S(2)}, u32[]{:S(2)}) %collective-permute-start.48) | collective-permute-done | bytes 1048608 | tf_op jit(solution)/shard_map/ppermute | solution.py:260
  813.3 14.8 %all-to-all-done.11.mine_ref = bf16[4,512,1024]{2,1,0:T(8,128)(2,1)} async-done(((bf16[4,512,1024]{2,1,0:T(8,128)(2,1)}), bf16[4,512,1024]{2,1,0:T(8,128)(2,1)}, u32[]{:S(2)}, u32[]{:S(2)}) %all-to-all-start.11) | async-done | bytes 4194336 | tf_op jit(solution)/shard_map/all_to_all | solution.py:62
  844.1 11.6 %shard_map.253 = f32[512,8192]{1,0:T(8,128)} custom-call(s32[40]{0:T(128)S(1)} %reshape.327.table_ref, bf16[4,512,1024]{2,1,0:T(8,128)(2,1)} %all-to-all-done.11.mine_ref, bf16[4,512,1024]{2,1,0:T(8,128)(2,1)} %collective-permute-done.54.other_ref), custom_call_target="tpu_custom_call" | custom-call | bytes 25165824 | tf_op jit(solution)/shard_map/pallas_call | solution.py:298
  855.8 7.5 collective-permute-done.51
  866.7 21.9 %collective-permute-done.55 = bf16[512,1024]{1,0:T(8,128)(2,1)S(1)} collective-permute-done((bf16[512,1024]{1,0:T(8,128)(2,1)S(1)}, bf16[512,1024]{1,0:T(8,128)(2,1)S(1)}, u32[]{:S(2)}, u32[]{:S(2)}) %collective-permute-start.55) | collective-permute-done | bytes 1048608 | tf_op jit(solution)/shard_map/ppermute | solution.py:260
  (493 shorter events, 518.4 us)
Async XLA Ops:
  7.8 50.2 %collective-permute-start = (bf16[512,384]{1,0:T(8,128)(2,1)}, bf16[512,384]{1,0:T(8,128)(2,1)S(1)}, u32[]{:S(2)}, u32[]{:S(2)}) collective-permute-start(bf16[512,384]{1,0:T(8,128)(2,1)} %get-tuple-element.391), channel_id=1, source_target_pairs={{0,8},{8,0},{16,24},{24,16},{1,9},{9,1},{17,25},{25,17},{2,10},{10... | collective-permute-start | bytes 1179656 | tf_op jit(solution)/shard_map/ppermute | solution.py:58
  9.9 48.1 %collective-permute-start.1 = (bf16[512,384]{1,0:T(8,128)(2,1)}, bf16[512,384]{1,0:T(8,128)(2,1)S(1)}, u32[]{:S(2)}, u32[]{:S(2)}) collective-permute-start(bf16[512,384]{1,0:T(8,128)(2,1)} %get-tuple-element.390), channel_id=1, source_target_pairs={{0,16},{8,24},{16,0},{24,8},{1,17},{9,25},{17,1},{25,9},{2,18},{10... | collective-permute-start | bytes 1179656 | tf_op jit(solution)/shard_map/ppermute | solution.py:58
  11.1 46.9 %collective-permute-start.2 = (bf16[512,384]{1,0:T(8,128)(2,1)}, bf16[512,384]{1,0:T(8,128)(2,1)}, u32[]{:S(2)}, u32[]{:S(2)}) collective-permute-start(bf16[512,384]{1,0:T(8,128)(2,1)} %get-tuple-element.389), channel_id=1, source_target_pairs={{0,24},{8,16},{16,8},{24,0},{1,25},{9,17},{17,9},{25,1},{2,26},{10... | collective-permute-start | bytes 1179656 | tf_op jit(solution)/shard_map/ppermute | solution.py:58
  11.1 31.0 %collective-permute-start.3 = (s32[5]{0:T(128)S(1)}, s32[5]{0:T(128)S(1)}, u32[]{:S(2)}, u32[]{:S(2)}) collective-permute-start(s32[5]{0:T(128)S(1)} %bitcast.291), channel_id=1, source_target_pairs={{0,1},{1,0},{2,3},{3,2},{4,5},{5,4},{6,7},{7,6},{8,9},{9,8},{10,11... | collective-permute-start | bytes 68 | tf_op jit(solution)/shard_map/ppermute | solution.py:58
  14.2 40.7 %all-to-all-start = ((bf16[4,144,2048]{2,1,0:T(8,128)(2,1)}), bf16[4,144,2048]{2,1,0:T(8,128)(2,1)}, u32[]{:S(2)}, u32[]{:S(2)}) async-start(bf16[4,144,2048]{2,1,0:T(8,128)(2,1)} %broadcast_in_dim.53), calls=%async_computation | async-start | bytes 4718592 | tf_op jit(solution)/shard_map/all_to_all | solution.py:62
  92.0 35.1 %collective-permute-start.8 = (bf16[384,1024]{1,0:T(8,128)(2,1)S(1)}, bf16[384,1024]{1,0:T(8,128)(2,1)}, u32[]{:S(2)}, u32[]{:S(2)}) collective-permute-start(bf16[384,1024]{1,0:T(8,128)(2,1)S(1)} %get-tuple-element.371), channel_id=1, source_target_pairs={{0,24},{8,16},{16,8},{24,0},{1,25},{9,17},{17,9},{25,1},{2,26},{10... | collective-permute-start | bytes 2359304 | tf_op jit(solution)/shard_map/ppermute | solution.py:58
  127.1 28.8 %all-to-all-start.1 = ((bf16[4,128,2048]{2,1,0:T(8,128)(2,1)}), bf16[4,128,2048]{2,1,0:T(8,128)(2,1)}, u32[]{:S(2)}, u32[]{:S(2)}) async-start(bf16[4,128,2048]{2,1,0:T(8,128)(2,1)} %bitcast.249), calls=%async_computation.1 | async-start | bytes 4194304 | tf_op jit(solution)/shard_map/all_to_all | solution.py:62
  134.9 51.7 %collective-permute-start.12 = (bf16[3,384,1024]{2,1,0:T(8,128)(2,1)}, bf16[3,384,1024]{2,1,0:T(8,128)(2,1)}, u32[]{:S(2)}, u32[]{:S(2)}) collective-permute-start(bf16[3,384,1024]{2,1,0:T(8,128)(2,1)} %pad_maximum_fusion.5), channel_id=1, source_target_pairs={{0,2},{2,0},{4,6},{6,4},{1,3},{3,1},{5,7},{7,5},{8,10},{10,8},{12,... | collective-permute-start | bytes 7077896 | tf_op jit(solution)/shard_map/ppermute | solution.py:58
  137.1 30.1 %collective-permute-start.10 = (bf16[128,1024]{1,0:T(8,128)(2,1)}, bf16[128,1024]{1,0:T(8,128)(2,1)S(1)}, u32[]{:S(2)}, u32[]{:S(2)}) collective-permute-start(bf16[128,1024]{1,0:T(8,128)(2,1)} %get-tuple-element.395), channel_id=1, source_target_pairs={{0,16},{8,24},{16,0},{24,8},{1,17},{9,25},{17,1},{25,9},{2,18},{10... | collective-permute-start | bytes 786440 | tf_op jit(solution)/shard_map/ppermute | solution.py:58
  138.5 28.6 %collective-permute-start.11 = (bf16[128,1024]{1,0:T(8,128)(2,1)}, bf16[128,1024]{1,0:T(8,128)(2,1)}, u32[]{:S(2)}, u32[]{:S(2)}) collective-permute-start(bf16[128,1024]{1,0:T(8,128)(2,1)} %get-tuple-element.394), channel_id=1, source_target_pairs={{0,24},{8,16},{16,8},{24,0},{1,25},{9,17},{17,9},{25,1},{2,26},{10... | collective-permute-start | bytes 786440 | tf_op jit(solution)/shard_map/ppermute | solution.py:58
  139.7 27.5 %collective-permute-start.9 = (bf16[128,1024]{1,0:T(8,128)(2,1)}, bf16[128,1024]{1,0:T(8,128)(2,1)}, u32[]{:S(2)}, u32[]{:S(2)}) collective-permute-start(bf16[128,1024]{1,0:T(8,128)(2,1)} %get-tuple-element.396), channel_id=1, source_target_pairs={{0,8},{8,0},{16,24},{24,16},{1,9},{9,1},{17,25},{25,17},{2,10},{10... | collective-permute-start | bytes 786440 | tf_op jit(solution)/shard_map/ppermute | solution.py:58
  170.1 28.8 %all-to-all-start.2 = ((bf16[4,128,2048]{2,1,0:T(8,128)(2,1)}), bf16[4,128,2048]{2,1,0:T(8,128)(2,1)}, u32[]{:S(2)}, u32[]{:S(2)}) async-start(bf16[4,128,2048]{2,1,0:T(8,128)(2,1)} %broadcast_in_dim.119), calls=%async_computation.2 | async-start | bytes 4194304 | tf_op jit(solution)/shard_map/all_to_all | solution.py:62
  176.5 34.2 %collective-permute-start.13 = (bf16[3,128,1024]{2,1,0:T(8,128)(2,1)}, bf16[3,128,1024]{2,1,0:T(8,128)(2,1)}, u32[]{:S(2)}, u32[]{:S(2)}) collective-permute-start(bf16[3,128,1024]{2,1,0:T(8,128)(2,1)} %pad_maximum_fusion.8), channel_id=1, source_target_pairs={{0,2},{2,0},{4,6},{6,4},{1,3},{3,1},{5,7},{7,5},{8,10},{10,8},{12,... | collective-permute-start | bytes 2359304 | tf_op jit(solution)/shard_map/ppermute | solution.py:58
  201.5 29.5 %all-to-all-start.3 = ((bf16[4,128,2048]{2,1,0:T(8,128)(2,1)}), bf16[4,128,2048]{2,1,0:T(8,128)(2,1)}, u32[]{:S(2)}, u32[]{:S(2)}) async-start(bf16[4,128,2048]{2,1,0:T(8,128)(2,1)} %broadcast_in_dim.120), calls=%async_computation.3 | async-start | bytes 4194304 | tf_op jit(solution)/shard_map/all_to_all | solution.py:62
  210.7 28.5 %collective-permute-start.14 = (bf16[512,2048]{1,0:T(8,128)(2,1)}, bf16[512,2048]{1,0:T(8,128)(2,1)}, u32[]{:S(2)}, u32[]{:S(2)}) collective-permute-start(bf16[512,2048]{1,0:T(8,128)(2,1)} %bitcast.66), channel_id=1, source_target_pairs={{0,1},{1,0},{2,3},{3,2},{4,5},{5,4},{6,7},{7,6},{8,9},{9,8},{10,11... | collective-permute-start | bytes 6291464 | tf_op jit(solution)/shard_map/ppermute | solution.py:58
  231.0 28.9 %collective-permute-start.15 = (bf16[512,2048]{1,0:T(8,128)(2,1)}, bf16[512,2048]{1,0:T(8,128)(2,1)S(1)}, u32[]{:S(2)}, u32[]{:S(2)}) collective-permute-start(bf16[512,2048]{1,0:T(8,128)(2,1)} %bitcast.74), channel_id=1, source_target_pairs={{0,1},{1,0},{2,3},{3,2},{4,5},{5,4},{6,7},{7,6},{8,9},{9,8},{10,11... | collective-permute-start | bytes 6291464 | tf_op jit(solution)/shard_map/ppermute | solution.py:58
  321.1 26.2 %collective-permute-start.17 = (bf16[512,1024]{1,0:T(8,128)(2,1)}, bf16[512,1024]{1,0:T(8,128)(2,1)}, u32[]{:S(2)}, u32[]{:S(2)}) collective-permute-start(bf16[512,1024]{1,0:T(8,128)(2,1)} %slice.237), channel_id=1, source_target_pairs={{0,2},{2,0},{4,6},{6,4},{1,3},{3,1},{5,7},{7,5},{8,10},{10,8},{12,... | collective-permute-start | bytes 3145736 | tf_op jit(solution)/shard_map/ppermute | solution.py:260
  357.5 37.3 %all-to-all-start.4 = ((bf16[4,128,2048]{2,1,0:T(8,128)(2,1)}), bf16[4,128,2048]{2,1,0:T(8,128)(2,1)}, u32[]{:S(2)}, u32[]{:S(2)}) async-start(bf16[4,128,2048]{2,1,0:T(8,128)(2,1)} %bitcast.251), calls=%async_computation.4 | async-start | bytes 4194304 | tf_op jit(solution)/shard_map/all_to_all | solution.py:62
  436.1 28.8 %all-to-all-start.5 = ((bf16[4,128,2048]{2,1,0:T(8,128)(2,1)}), bf16[4,128,2048]{2,1,0:T(8,128)(2,1)}, u32[]{:S(2)}, u32[]{:S(2)}) async-start(bf16[4,128,2048]{2,1,0:T(8,128)(2,1)} %broadcast_in_dim.121), calls=%async_computation.5 | async-start | bytes 4194304 | tf_op jit(solution)/shard_map/all_to_all | solution.py:62
  484.3 36.5 %collective-permute-start.31 = (bf16[512,2048]{1,0:T(8,128)(2,1)}, bf16[512,2048]{1,0:T(8,128)(2,1)}, u32[]{:S(2)}, u32[]{:S(2)}) collective-permute-start(bf16[512,2048]{1,0:T(8,128)(2,1)} %bitcast.78), channel_id=1, source_target_pairs={{0,1},{1,0},{2,3},{3,2},{4,5},{5,4},{6,7},{7,6},{8,9},{9,8},{10,11... | collective-permute-start | bytes 6291464 | tf_op jit(solution)/shard_map/ppermute | solution.py:58
  488.1 29.6 %all-to-all-start.6 = ((bf16[4,128,2048]{2,1,0:T(8,128)(2,1)}), bf16[4,128,2048]{2,1,0:T(8,128)(2,1)}, u32[]{:S(2)}, u32[]{:S(2)}) async-start(bf16[4,128,2048]{2,1,0:T(8,128)(2,1)} %bitcast.250), calls=%async_computation.6 | async-start | bytes 4194304 | tf_op jit(solution)/shard_map/all_to_all | solution.py:62
  502.3 36.0 %collective-permute-start.30 = (bf16[512,1024]{1,0:T(8,128)(2,1)}, bf16[512,1024]{1,0:T(8,128)(2,1)}, u32[]{:S(2)}, u32[]{:S(2)}) collective-permute-start(bf16[512,1024]{1,0:T(8,128)(2,1)} %add_convert_fusion.19), channel_id=1, source_target_pairs={{2,4},{4,2},{3,5},{5,3},{10,12},{12,10},{11,13},{13,11},{18,20},{2... | collective-permute-start | bytes 3145736 | tf_op jit(solution)/shard_map/ppermute | solution.py:258
  507.1 31.2 %collective-permute-start.29 = (bf16[512,1024]{1,0:T(8,128)(2,1)}, bf16[512,1024]{1,0:T(8,128)(2,1)}, u32[]{:S(2)}, u32[]{:S(2)}) collective-permute-start(bf16[512,1024]{1,0:T(8,128)(2,1)} %broadcast_select_fusion.10), channel_id=1, source_target_pairs={{0,2},{2,0},{4,6},{6,4},{1,3},{3,1},{5,7},{7,5},{8,10},{10,8},{12,... | collective-permute-start | bytes 3145736 | tf_op jit(solution)/shard_map/ppermute | solution.py:260
  555.5 26.8 %collective-permute-start.32 = (bf16[512,1024]{1,0:T(8,128)(2,1)S(1)}, bf16[512,1024]{1,0:T(8,128)(2,1)S(1)}, u32[]{:S(2)}, u32[]{:S(2)}) collective-permute-start(bf16[512,1024]{1,0:T(8,128)(2,1)S(1)} %broadcast_select_fusion.9), channel_id=1, source_target_pairs={{0,2},{2,0},{4,6},{6,4},{1,3},{3,1},{5,7},{7,5},{8,10},{10,8},{12,... | collective-permute-start | bytes 3145736 | tf_op jit(solution)/shard_map/ppermute | solution.py:260
  588.1 25.4 %collective-permute-start.35 = (bf16[512,1024]{1,0:T(8,128)(2,1)}, bf16[512,1024]{1,0:T(8,128)(2,1)}, u32[]{:S(2)}, u32[]{:S(2)}) collective-permute-start(bf16[512,1024]{1,0:T(8,128)(2,1)} %broadcast_select_fusion.8), channel_id=1, source_target_pairs={{0,2},{2,0},{4,6},{6,4},{1,3},{3,1},{5,7},{7,5},{8,10},{10,8},{12,... | collective-permute-start | bytes 3145736 | tf_op jit(solution)/shard_map/ppermute | solution.py:260
  590.0 40.2 %all-to-all-start.7 = ((bf16[4,128,2048]{2,1,0:T(8,128)(2,1)}), bf16[4,128,2048]{2,1,0:T(8,128)(2,1)}, u32[]{:S(2)}, u32[]{:S(2)}) async-start(bf16[4,128,2048]{2,1,0:T(8,128)(2,1)} %bitcast.248), calls=%async_computation.7 | async-start | bytes 4194304 | tf_op jit(solution)/shard_map/all_to_all | solution.py:62
  619.6 25.2 %collective-permute-start.38 = (bf16[512,1024]{1,0:T(8,128)(2,1)}, bf16[512,1024]{1,0:T(8,128)(2,1)}, u32[]{:S(2)}, u32[]{:S(2)}) collective-permute-start(bf16[512,1024]{1,0:T(8,128)(2,1)} %broadcast_select_fusion.7), channel_id=1, source_target_pairs={{0,2},{2,0},{4,6},{6,4},{1,3},{3,1},{5,7},{7,5},{8,10},{10,8},{12,... | collective-permute-start | bytes 3145736 | tf_op jit(solution)/shard_map/ppermute | solution.py:260
  644.8 33.3 %all-to-all-start.8 = ((bf16[4,512,384]{2,1,0:T(8,128)(2,1)}), bf16[4,512,384]{2,1,0:T(8,128)(2,1)}, u32[]{:S(2)}, u32[]{:S(2)}) async-start(bf16[4,512,384]{2,1,0:T(8,128)(2,1)} %bitcast.260), calls=%async_computation.8 | async-start | bytes 3145728 | tf_op jit(solution)/shard_map/all_to_all | solution.py:62
  681.2 26.1 %collective-permute-start.43 = (bf16[512,1024]{1,0:T(8,128)(2,1)}, bf16[512,1024]{1,0:T(8,128)(2,1)}, u32[]{:S(2)}, u32[]{:S(2)}) collective-permute-start(bf16[512,1024]{1,0:T(8,128)(2,1)} %add_convert_fusion.9), channel_id=1, source_target_pairs={{2,4},{4,2},{3,5},{5,3},{10,12},{12,10},{11,13},{13,11},{18,20},{2... | collective-permute-start | bytes 3145736 | tf_op jit(solution)/shard_map/ppermute | solution.py:258
  699.4 51.7 %all-to-all-start.10 = ((bf16[4,512,1024]{2,1,0:T(8,128)(2,1)}), bf16[4,512,1024]{2,1,0:T(8,128)(2,1)}, u32[]{:S(2)}, u32[]{:S(2)}) async-start(bf16[4,512,1024]{2,1,0:T(8,128)(2,1)} %pad_maximum_fusion.3), calls=%async_computation.10 | async-start | bytes 8388608 | tf_op jit(solution)/shard_map/all_to_all | solution.py:62
  759.6 29.4 %collective-permute-start.50 = (bf16[4,512,1024]{2,1,0:T(8,128)(2,1)}, bf16[4,512,1024]{2,1,0:T(8,128)(2,1)}, u32[]{:S(2)}, u32[]{:S(2)}) collective-permute-start(bf16[4,512,1024]{2,1,0:T(8,128)(2,1)} %all-to-all-done.10.mine_ref), channel_id=1, source_target_pairs={{0,1},{1,0},{2,3},{3,2},{4,5},{5,4},{6,7},{7,6},{8,9},{9,8},{10,11... | collective-permute-start | bytes 12582920 | tf_op jit(solution)/shard_map/ppermute | solution.py:58
  775.5 52.6 %all-to-all-start.11 = ((bf16[4,512,1024]{2,1,0:T(8,128)(2,1)}), bf16[4,512,1024]{2,1,0:T(8,128)(2,1)}, u32[]{:S(2)}, u32[]{:S(2)}) async-start(bf16[4,512,1024]{2,1,0:T(8,128)(2,1)} %pad_maximum_fusion.4), calls=%async_computation.11 | async-start | bytes 8388608 | tf_op jit(solution)/shard_map/all_to_all | solution.py:62
  (130 other events, 1571.4 us)

commit v3 on v2

--- a/solution.py
+++ b/solution.py
@@ -238,34 +238,134 @@
     def slot(self, entering, *values):
         last = self.flight
         came, moved, values = self.clock.tick(last.get("came"), last.get("moved"), values)
-        flight = {}
-        send = None
-        if last.get("across"):
-            name, part = last["across"]
-            full = (part.astype(F32) + moved.astype(F32)).astype(BF)
-            flight["out"] = (name, full)
-            send = full
         if entering is not None:
             name, array, block = entering
-            array = self.clock.now(array)
-            flight["enter"] = (name, array, block)
-            piece = self.piece(array, block)
-            send = piece if send is None else jnp.where(self.inner, send, piece)
-        if last.get("enter"):
-            name, array, block = last["enter"]
-            part = (self.piece(array, block).astype(F32) + came.astype(F32)).astype(BF)
-            flight["across"] = (name, part)
+            entering = (name, self.clock.now(array), block)
+        part, send = self.combine(last, came, moved, entering)
+        across = last["enter"][0] if part is not None else None
+        flight = {"enter": entering, "across": across, "part": part}
+        if last.get("across"):
+            flight["out"] = (last["across"], send)
+        if part is not None:
             flight["moved"] = lax.ppermute(part, "rest", [(1, 2), (2, 1)])
         if send is not None:
             flight["came"] = lax.ppermute(send, "rest", [(0, 1), (1, 0), (2, 3), (3, 2)])
         if last.get("out"):
             name, full = last["out"]
-            self.sums[name] = jnp.where(self.inner, full, came)
+            self.sums[name] = (full, came)
         self.flight = flight
         return values[0] if len(values) == 1 else values
 
     def stack(self, name, count):
-        return jnp.stack([self.sums[name, k] for k in range(count)])
+        rows, wide = self.shape
+        steps = 2
+        tile = rows // steps
+        pairs = [self.sums[name, k] for k in range(count)]
+
+        def spec(k, used):
+            def at(j, i, w):
+                here = jnp.where(j == k, i, jnp.where(j < k, 0, steps - 1))
+                return (jnp.where(w[0] == used, here, 0), 0)
+
+            return pl.BlockSpec((tile, wide), at)
+
+        def kernel(where_ref, *refs):
+            for k in range(count):
+                for used in range(2):
+
+                    @pl.when((pl.program_id(0) == k) & (where_ref[0] == used))
+                    def _(k=k, used=used):
+                        refs[-1][...] = refs[2 * k + 1 - used][...]
+
+        return pl.pallas_call(
+            kernel,
+            grid_spec=pltpu.PrefetchScalarGridSpec(
+                num_scalar_prefetch=1,
+                grid=(count, steps),
+                in_specs=[spec(k, used) for k in range(count) for used in (1, 0)],
+                out_specs=pl.BlockSpec((None, tile, wide), lambda j, i, w: (j, i, 0)),
+            ),
+            out_shape=jax.ShapeDtypeStruct((count, rows, wide), BF),
+            compiler_params=pltpu.CompilerParams(vmem_limit_bytes=16 * 2**20),
+            cost_estimate=pl.CostEstimate(flops=0, bytes_accessed=1, transcendentals=0),
+        )(self.inner.astype(jnp.int32)[None], *[one for pair in pairs for one in pair])
+
+    def combine(self, stream, came, moved, entering):
+        rows, wide = self.shape
+        steps = 4
+        tile = rows // steps
+        last, across = stream.get("enter"), stream.get("across")
+
+        def spec(block, used):
+            def at(i, w):
+                here = jnp.where(w[0] == used, i, 0)
+                return block[:-2] + (block[-2] * steps + here, block[-1])
+
+            return pl.BlockSpec((None,) * (len(block) - 2) + (tile, wide), at)
+
+        inputs, names = [], []
+
+        def take(name, array, block, used):
+            inputs.append((array, spec(block, used)))
+            names.append(name)
+
+        if last is not None:
+            take("came", came, (0, 0), 1)
+            take("last", last[1], last[2], 1)
+        if across is not None:
+            take("part", stream["part"], (0, 0), 1)
+            take("moved", moved, (0, 0), 1)
+        if entering is not None:
+            take("next", entering[1], entering[2], 0)
+        given = []
+        if last is not None:
+            given.append("part")
+        if across is not None or entering is not None:
+            given.append("send")
+        if not given:
+            return None, None
+
+        def kernel(where_ref, *refs):
+            read = dict(zip(names, refs))
+            write = dict(zip(given, refs[len(names) :]))
+
+            @pl.when(where_ref[0] == 1)
+            def _():
+                if "last" in read:
+                    total = read["last"][...].astype(F32) + read["came"][...].astype(F32)
+                    write["part"][...] = total.astype(BF)
+                if "part" in read:
+                    total = read["part"][...].astype(F32) + read["moved"][...].astype(F32)
+                    write["send"][...] = total.astype(BF)
+
+            if "next" in read:
+
+                @pl.when(where_ref[0] == 0)
+                def _():
+                    write["send"][...] = read["next"][...]
+
+        results = pl.pallas_call(
+            kernel,
+            grid_spec=pltpu.PrefetchScalarGridSpec(
+                num_scalar_prefetch=1,
+                grid=(steps,),
+                in_specs=[one[1] for one in inputs],
+                out_specs=[
+                    pl.BlockSpec(
+                        (tile, wide),
+                        lambda i, w: (i, 0)
+                        if name == "send"
+                        else (jnp.where(w[0] == 1, i, 0), 0),
+                    )
+                    for name in given
+                ],
+            ),
+            out_shape=[jax.ShapeDtypeStruct((rows, wide), BF)] * len(given),
+            compiler_params=pltpu.CompilerParams(vmem_limit_bytes=16 * 2**20),
+            cost_estimate=pl.CostEstimate(flops=0, bytes_accessed=1, transcendentals=0),
+        )(self.inner.astype(jnp.int32)[None], *[one[0] for one in inputs])
+        results = dict(zip(given, results))
+        return results.get("part"), results.get("send")
 
 
 def place(shape, mine, other, rows, wide, blocks):
@@ -578,7 +678,7 @@
     turned_q = turned[:, :, :qw].transpose(1, 0, 2).reshape(share, parts * qw)
     turned_kv = turned[:, :, qw:].transpose(1, 0, 2).reshape(share, parts * 2 * kw)
     grad_gains, turned_q, turned_kv = slot(
-        (("rows", 0), grad_out, (0, 0)), grad_gains, turned_q, turned_kv
+        (("heads", 0), turned_q, (0, 0)), grad_gains, turned_q, turned_kv
     )
     if on_line:
         turned_kv = jnp.concatenate(
@@ -604,21 +704,13 @@
             )
 
         gate_turned = turn("gate")
-        turned_kv = slot((("heads", 0), turned_q, (0, 0)), turned_kv)
-        gate_turned = slot((("heads", 1), turned_kv, (0, 0)), gate_turned)
+        turned_kv = slot((("heads", 1), turned_kv, (0, 0)), turned_kv)
+        gate_turned = slot((("rows", 0), grad_out, (0, 0)), gate_turned)
         outs["gate"] = place_columns(gate_turned)
         up_turned = turn("up")
         outs, up_turned = slot(None, outs, up_turned)
         outs["up"] = place_columns(up_turned)
-        outs["out"] = place(
-            (qw * 2, width),
-            *both(line.stack("rows", 1)),
-            qw,
-            ff,
-            [((0, b, 0), lambda k, b=b: (k, b)) for b in range(2)],
-        )
         outs = slot(None, outs)
-        slot(None)
         mine, other = both(line.stack("heads", 2))
         grad_gains = sum(
             one[1, :2, parts * 2 * kw : parts * 2 * kw + share].astype(F32) for one in (mine, other)
@@ -639,6 +731,14 @@
         ).astype(F32)
         outs["key"] = narrow[..., :kw].reshape(share, team * kw)
         outs["value"] = narrow[..., kw:].reshape(share, team * kw)
+        outs = slot(None, outs)
+        outs["out"] = place(
+            (qw * 2, width),
+            *both(line.stack("rows", 1)),
+            qw,
+            ff,
+            [((0, b, 0), lambda k, b=b: (k, b)) for b in range(2)],
+        )
     else:
         def whole(value):
             value = lax.psum(value, "rest")[None]

time: 921 us -> 898 us (0.975)
  other arithmetic: 184 us -> 62.7 us
  Pallas kernels: 68.7 us -> 123 us
  starting transfers between devices: 149 us -> 177 us
  local copies, waits for them, and re-layouts: 104 us -> 117 us
    pallas_call x0 -> x22, Pallas kernels: none -> 56.4 us  [the longest x17 33.7 us: combine(): pl.pallas_call(kernel, grid_spec=pltpu.PrefetchScalarGridSpec(num_scalar_...]
    another operation x21 -> x2, other arithmetic: 49.2 us -> 0.36 us  [the longest x19 48.8 us: stack(): return jnp.stack([self.sums[name, k] for k in range(count)])]
    convert_element_type x17 -> x0, other arithmetic: 37.4 us -> none  [the longest x15 32.6 us: slot(): part = (self.piece(array, block).astype(F32) + came.astype(F32)).astype(BF)]
    select_n x13 -> x0, other arithmetic: 35.9 us -> none  [slot(): send = piece if send is None else jnp.where(self.inner, send, piece)]
    ppermute x17, starting transfers between devices: 35.6 us -> 68.7 us  [slot(): lax.ppermute(send, 'rest', [(0, 1), (1, 0), (2, 3), (3, 2)])]
    unnamed x194 -> x158, local copies, waits for them, and re-layouts: 16.2 us -> 32.3 us
    ppermute x17, waiting for transfers between devices: 199 us -> 187 us  [slot(): lax.ppermute(send, 'rest', [(0, 1), (1, 0), (2, 3), (3, 2)])]
  transfers between devices with their start and end apart: 69 -> 69, of which waited for: 30 -> 32; matrix products, arithmetic and copies ran while one was open for 33% -> 23% of each run, Pallas kernels for 6% -> 11%
where the time goes in v3:
time: 898 us; the launch traced here: 884 us
  waiting for transfers between devices  306 us (34%)
  starting transfers between devices  177 us (20%)
  Pallas kernels  123 us (14%)
  local copies, waits for them, and re-layouts  117 us (13%)
  matrix products  96.4 us (11%)
  other arithmetic  62.7 us (7%)
    ppermute x17, waiting for transfers between devices, slot(): lax.ppermute(send, 'rest', [(0, 1), (1, 0), (2, 3), (3, 2)])  187 us
    all_to_all x12, waiting for transfers between devices, exchange(): return lax.all_to_all(blocks, 'group', 0, 0, tiled=True)  68.7 us
    ppermute x17, starting transfers between devices, slot(): lax.ppermute(send, 'rest', [(0, 1), (1, 0), (2, 3), (3, 2)])  68.7 us
    all_to_all x12, starting transfers between devices, exchange(): return lax.all_to_all(blocks, 'group', 0, 0, tiled=True)  54 us
    ppermute x25, waiting for transfers between devices, step_to(): return lax.ppermute(value, axis, [(i, i ^ step) for i in range(size)])  49.6 us
    pallas_call x5, Pallas kernels, place(): pl.pallas_call(kernel, grid_spec=pltpu.PrefetchScalarGridSpec(num_scalar_...  44.7 us
    dot_general x5, matrix products, contract_last(): lax.dot_general(left, right, (((1,), (1,)), ((), ())), preferred_element_...  33.7 us
    pallas_call x17, Pallas kernels, combine(): pl.pallas_call(kernel, grid_spec=pltpu.PrefetchScalarGridSpec(num_scalar_...  33.7 us
  transfers between devices with their start and end apart: 69, of which 32 were waited for; matrix products, arithmetic and copies ran while one was open for 23% of the time, Pallas kernels for 11%

profile of v3, /device:TPU:1, one launch (start us, length us, event | category | flops | bytes accessed | tf_op | source)
XLA Modules:
  0.0 883.7 jit_solution(1722135460616573895)
XLA Ops:
  46.9 8.0 collective-permute-done.2
  70.5 9.8 %shard_map.248 = (bf16[1024,256]{1,0:T(8,128)(2,1)S(1)}, bf16[1024,384]{1,0:T(8,128)(2,1)S(1)}, f32[1024,128]{1,0:T(8,128)S(1)}) custom-call(f32[1024,384]{1,0:T(8,128)S(1)} %fusion.41.qkv_ref, f32[1024,128]{1,0:T(8,128)S(1)} %copy-done.17, f32[1024,128]{1,0:T(8,128)S(1)} %get-tuple-element.198.sin_ref, s32[2,512,2]{2,1,0:T(8,128)S(1)} %copy.55.column_ref, ...), custom_call_target="tpu_custom_call" | custom-call | bytes 1 | tf_op jit(solution)/shard_map/pallas_call | solution.py:195
  97.5 8.9 %collective-permute-done.6 = bf16[384,1024]{1,0:T(8,128)(2,1)} collective-permute-done((bf16[384,1024]{1,0:T(8,128)(2,1)S(1)}, bf16[384,1024]{1,0:T(8,128)(2,1)}, u32[]{:S(2)}, u32[]{:S(2)}) %collective-permute-start.6) | collective-permute-done | bytes 786464 | tf_op jit(solution)/shard_map/ppermute | solution.py:58
  106.4 16.9 %collective-permute-done.8 = bf16[384,1024]{1,0:T(8,128)(2,1)} collective-permute-done((bf16[384,1024]{1,0:T(8,128)(2,1)S(1)}, bf16[384,1024]{1,0:T(8,128)(2,1)}, u32[]{:S(2)}, u32[]{:S(2)}) %collective-permute-start.8) | collective-permute-done | bytes 786464 | tf_op jit(solution)/shard_map/ppermute | solution.py:58
  178.3 8.2 collective-permute-done.12
  208.2 18.8 %all-to-all-done.3 = bf16[4,128,2048]{2,1,0:T(8,128)(2,1)} async-done(((bf16[4,128,2048]{2,1,0:T(8,128)(2,1)}), bf16[4,128,2048]{2,1,0:T(8,128)(2,1)}, u32[]{:S(2)}, u32[]{:S(2)}) %all-to-all-start.3) | async-done | bytes 2097184 | tf_op jit(solution)/shard_map/all_to_all | solution.py:62
  236.9 7.8 fusion.47
  244.8 11.2 %multiply_convert_fusion.2 = (bf16[1024,1024]{1,0:T(8,128)(2,1)S(1)}, f32[1024,1024]{1,0:T(8,128)}, f32[1024,1024]{1,0:T(8,128)}) fusion(f32[1024,1024]{1,0:T(8,128)S(1)} %fusion.47, pred[]{:T(512)S(6)} %eq.74, bf16[1024,2048]{1,0:T(8,128)(2,1)S(1)} %constant_dynamic-update-slice_fusion.6, bf16[2048,1024]{1,0:T(8,128)(2,1)} %bitcast.72), kind=kOutput, calls=%fused_computation.24 | convolution fusion | flops 4303355904 | bytes 23068672 | tf_op jit(solution)/shard_map/dot_general | solution.py:32
  267.3 10.6 %multiply_convert_fusion = (bf16[1024,1024]{1,0:T(8,128)(2,1)S(1)}, bf16[1024,1024]{1,0:T(8,128)(2,1)}) fusion(f32[1024,1024]{1,0:T(8,128)} %get-tuple-element.424, f32[1024,1024]{1,0:T(8,128)} %get-tuple-element.487, f32[1024,1024]{1,0:T(8,128)} %copy-done.74, pred[]{:T(512)S(6)} %eq.74, bf16[1024,2048]{1,0:T(8,128)(2,1)S(1)} %pad_maximum_fusion.1, ...), kind=kOutput, calls=%fused_computation.22 | convolution fusion | flops 4309647360 | bytes 25165828 | tf_op jit(solution)/shard_map/dot_general | solution.py:36
  277.8 12.8 %collective-permute-done.16.refs_0_ = bf16[512,1024]{1,0:T(8,128)(2,1)S(1)} collective-permute-done((bf16[512,1024]{1,0:T(8,128)(2,1)S(1)}, bf16[512,1024]{1,0:T(8,128)(2,1)S(1)}, u32[]{:S(2)}, u32[]{:S(2)}) %collective-permute-start.16) | collective-permute-done | bytes 1048608 | tf_op jit(solution)/shard_map/ppermute | solution.py:252
  290.7 10.3 %fusion.11 = f32[1024,2048]{1,0:T(8,128)} fusion(bf16[2048,1024]{1,0:T(8,128)(2,1)} %bitcast.72, bf16[1024,1024]{1,0:T(8,128)(2,1)S(1)} %get-tuple-element.251, bf16[1024,1024]{1,0:T(8,128)(2,1)} %get-tuple-element.244, pred[]{:T(512)S(6)} %eq.74), kind=kOutput, calls=%fused_computation.40 | convolution fusion | flops 4296015872 | bytes 16777216 | tf_op jit(solution)/shard_map/dot_general | solution.py:36
  301.0 9.2 %convolution_add_fusion = f32[1024,2048]{1,0:T(8,128)S(1)} fusion(f32[1024,2048]{1,0:T(8,128)} %fusion.11, bf16[2048,1024]{1,0:T(8,128)(2,1)} %bitcast.71, bf16[1024,1024]{1,0:T(8,128)(2,1)S(1)} %copy-done.73, bf16[1024,1024]{1,0:T(8,128)(2,1)} %copy-done.71, pred[]{:T(512)S(6)} %eq.74), kind=kOutput, calls=%fused_computation.27 | convolution fusion | flops 4298113024 | bytes 25165824 | tf_op jit(solution)/shard_map/dot_general | solution.py:36
  320.4 20.7 %collective-permute-done.17.refs_0_ = bf16[512,1024]{1,0:T(8,128)(2,1)S(1)} collective-permute-done((bf16[512,1024]{1,0:T(8,128)(2,1)S(1)}, bf16[512,1024]{1,0:T(8,128)(2,1)S(1)}, u32[]{:S(2)}, u32[]{:S(2)}) %collective-permute-start.17) | collective-permute-done | bytes 1048608 | tf_op jit(solution)/shard_map/ppermute | solution.py:252
  354.0 9.6 %convolution_convert_fusion.1.refs_4_.refs_1_ = bf16[2048,1024]{1,0:T(8,128)(2,1)} fusion(bf16[1024,2048]{1,0:T(8,128)(2,1)} %copy-done.49, bf16[1024,1024]{1,0:T(8,128)(2,1)} %get-tuple-element.244), kind=kOutput, calls=%fused_computation.29 | convolution fusion | flops 4297064448 | bytes 10485760 | tf_op jit(solution)/shard_map/dot_general | solution.py:40
  363.6 7.0 collective-permute-done.20.refs_0_.refs_1_
  387.8 12.0 %collective-permute-done.22.refs_0_.refs_3_ = bf16[512,1024]{1,0:T(8,128)(2,1)} collective-permute-done((bf16[512,1024]{1,0:T(8,128)(2,1)}, bf16[512,1024]{1,0:T(8,128)(2,1)}, u32[]{:S(2)}, u32[]{:S(2)}) %collective-permute-start.22) | collective-permute-done | bytes 1048608 | tf_op jit(solution)/shard_map/ppermute | solution.py:252
  399.8 7.1 fusion.7
  453.2 15.0 %collective-permute-done.27.refs_0_.refs_7_ = bf16[512,1024]{1,0:T(8,128)(2,1)} collective-permute-done((bf16[512,1024]{1,0:T(8,128)(2,1)}, bf16[512,1024]{1,0:T(8,128)(2,1)}, u32[]{:S(2)}, u32[]{:S(2)}) %collective-permute-start.27) | collective-permute-done | bytes 1048608 | tf_op jit(solution)/shard_map/ppermute | solution.py:252
  491.4 10.7 %all-to-all-done.6 = bf16[4,128,2048]{2,1,0:T(8,128)(2,1)} async-done(((bf16[4,128,2048]{2,1,0:T(8,128)(2,1)}), bf16[4,128,2048]{2,1,0:T(8,128)(2,1)}, u32[]{:S(2)}, u32[]{:S(2)}) %all-to-all-start.6) | async-done | bytes 2097184 | tf_op jit(solution)/shard_map/all_to_all | solution.py:62
  509.7 11.7 %shard_map.256 = bf16[1024,384]{1,0:T(8,128)(2,1)S(1)} custom-call(bf16[1024,384]{1,0:T(8,128)(2,1)S(1)} %copy-done.26, f32[1024,128]{1,0:T(8,128)S(1)} %copy-done.30, bf16[1024,256]{1,0:T(8,128)(2,1)S(1)} %convolution_convert_fusion.5.grad_ref, f32[1024,128]{1,0:T(8,128)S(1)} %copy-done.18, f32[1024,128]{1,0:T(8,128)S(1)} %get-tuple-element.198.sin_ref, ...), custom_call_target="tpu_custom_call" | custom-call | bytes 1 | tf_op jit(solution)/shard_map/pallas_call | solution.py:195
  527.4 8.5 shard_map.259.mine_ref
  551.1 14.8 %collective-permute-done.32.refs_0_.refs_3_ = bf16[512,1024]{1,0:T(8,128)(2,1)S(1)} collective-permute-done((bf16[512,1024]{1,0:T(8,128)(2,1)S(1)}, bf16[512,1024]{1,0:T(8,128)(2,1)S(1)}, u32[]{:S(2)}, u32[]{:S(2)}) %collective-permute-start.32) | collective-permute-done | bytes 1048608 | tf_op jit(solution)/shard_map/ppermute | solution.py:252
  577.8 11.9 %shard_map.260 = f32[2048,2048]{1,0:T(8,128)} custom-call(s32[40]{0:T(128)S(1)} %reshape.323.table_ref, bf16[4,512,1024]{2,1,0:T(8,128)(2,1)} %shard_map.259.mine_ref, bf16[4,512,1024]{2,1,0:T(8,128)(2,1)} %collective-permute-done.37.other_ref), custom_call_target="tpu_custom_call" | custom-call | bytes 25165824 | tf_op jit(solution)/shard_map/pallas_call | solution.py:398
  607.5 18.3 %collective-permute-done.38.refs_0_.refs_7_ = bf16[512,1024]{1,0:T(8,128)(2,1)} collective-permute-done((bf16[512,1024]{1,0:T(8,128)(2,1)}, bf16[512,1024]{1,0:T(8,128)(2,1)}, u32[]{:S(2)}, u32[]{:S(2)}) %collective-permute-start.38) | collective-permute-done | bytes 1048608 | tf_op jit(solution)/shard_map/ppermute | solution.py:252
  699.2 19.2 %collective-permute-done.44.refs_0_.refs_5_ = bf16[512,1024]{1,0:T(8,128)(2,1)S(1)} collective-permute-done((bf16[512,1024]{1,0:T(8,128)(2,1)S(1)}, bf16[512,1024]{1,0:T(8,128)(2,1)S(1)}, u32[]{:S(2)}, u32[]{:S(2)}) %collective-permute-start.44) | collective-permute-done | bytes 1048608 | tf_op jit(solution)/shard_map/ppermute | solution.py:252
  731.5 11.3 %collective-permute-done.46.refs_0_.refs_7_ = bf16[512,1024]{1,0:T(8,128)(2,1)} collective-permute-done((bf16[512,1024]{1,0:T(8,128)(2,1)}, bf16[512,1024]{1,0:T(8,128)(2,1)}, u32[]{:S(2)}, u32[]{:S(2)}) %collective-permute-start.46) | collective-permute-done | bytes 1048608 | tf_op jit(solution)/shard_map/ppermute | solution.py:252
  771.6 11.6 %shard_map.268 = f32[512,8192]{1,0:T(8,128)} custom-call(s32[40]{0:T(128)S(1)} %reshape.327.table_ref, bf16[4,512,1024]{2,1,0:T(8,128)(2,1)} %all-to-all-done.10.mine_ref, bf16[4,512,1024]{2,1,0:T(8,128)(2,1)} %collective-permute-done.50.other_ref), custom_call_target="tpu_custom_call" | custom-call | bytes 25165824 | tf_op jit(solution)/shard_map/pallas_call | solution.py:398
  783.2 10.4 %collective-permute-done.48.refs_0_.refs_1_ = bf16[512,1024]{1,0:T(8,128)(2,1)} collective-permute-done((bf16[512,1024]{1,0:T(8,128)(2,1)}, bf16[512,1024]{1,0:T(8,128)(2,1)}, u32[]{:S(2)}, u32[]{:S(2)}) %collective-permute-start.48) | collective-permute-done | bytes 1048608 | tf_op jit(solution)/shard_map/ppermute | solution.py:252
  793.6 15.0 %all-to-all-done.11.mine_ref = bf16[4,512,1024]{2,1,0:T(8,128)(2,1)} async-done(((bf16[4,512,1024]{2,1,0:T(8,128)(2,1)}), bf16[4,512,1024]{2,1,0:T(8,128)(2,1)}, u32[]{:S(2)}, u32[]{:S(2)}) %all-to-all-start.11) | async-done | bytes 4194336 | tf_op jit(solution)/shard_map/all_to_all | solution.py:62
  816.6 9.5 %shard_map.271 = f32[512,8192]{1,0:T(8,128)} custom-call(s32[40]{0:T(128)S(1)} %reshape.327.table_ref, bf16[4,512,1024]{2,1,0:T(8,128)(2,1)} %all-to-all-done.11.mine_ref, bf16[4,512,1024]{2,1,0:T(8,128)(2,1)S(1)} %collective-permute-done.53.other_ref), custom_call_target="tpu_custom_call" | custom-call | bytes 25165824 | tf_op jit(solution)/shard_map/pallas_call | solution.py:398
  826.0 13.1 %collective-permute-done.51.refs_3_ = bf16[512,1024]{1,0:T(8,128)(2,1)S(1)} collective-permute-done((bf16[512,1024]{1,0:T(8,128)(2,1)S(1)}, bf16[512,1024]{1,0:T(8,128)(2,1)S(1)}, u32[]{:S(2)}, u32[]{:S(2)}) %collective-permute-start.51) | collective-permute-done | bytes 1048608 | tf_op jit(solution)/shard_map/ppermute | solution.py:252
  861.8 8.4 collective-permute-done.55.refs_1_
  (429 shorter events, 503.3 us)
Async XLA Ops:
  4.3 39.4 %all-to-all-start = ((bf16[4,144,2048]{2,1,0:T(8,128)(2,1)}), bf16[4,144,2048]{2,1,0:T(8,128)(2,1)}, u32[]{:S(2)}, u32[]{:S(2)}) async-start(bf16[4,144,2048]{2,1,0:T(8,128)(2,1)} %broadcast_in_dim.57), calls=%async_computation | async-start | bytes 4718592 | tf_op jit(solution)/shard_map/all_to_all | solution.py:62
  14.7 32.2 %collective-permute-start = (bf16[512,384]{1,0:T(8,128)(2,1)}, bf16[512,384]{1,0:T(8,128)(2,1)S(1)}, u32[]{:S(2)}, u32[]{:S(2)}) collective-permute-start(bf16[512,384]{1,0:T(8,128)(2,1)} %get-tuple-element.461), channel_id=1, source_target_pairs={{0,8},{8,0},{16,24},{24,16},{1,9},{9,1},{17,25},{25,17},{2,10},{10... | collective-permute-start | bytes 1179656 | tf_op jit(solution)/shard_map/ppermute | solution.py:58
  16.7 30.1 %collective-permute-start.1 = (bf16[512,384]{1,0:T(8,128)(2,1)}, bf16[512,384]{1,0:T(8,128)(2,1)S(1)}, u32[]{:S(2)}, u32[]{:S(2)}) collective-permute-start(bf16[512,384]{1,0:T(8,128)(2,1)} %get-tuple-element.460), channel_id=1, source_target_pairs={{0,16},{8,24},{16,0},{24,8},{1,17},{9,25},{17,1},{25,9},{2,18},{10... | collective-permute-start | bytes 1179656 | tf_op jit(solution)/shard_map/ppermute | solution.py:58
  17.9 36.9 %collective-permute-start.2 = (bf16[512,384]{1,0:T(8,128)(2,1)}, bf16[512,384]{1,0:T(8,128)(2,1)}, u32[]{:S(2)}, u32[]{:S(2)}) collective-permute-start(bf16[512,384]{1,0:T(8,128)(2,1)} %get-tuple-element.459), channel_id=1, source_target_pairs={{0,24},{8,16},{16,8},{24,0},{1,25},{9,17},{17,9},{25,1},{2,26},{10... | collective-permute-start | bytes 1179656 | tf_op jit(solution)/shard_map/ppermute | solution.py:58
  88.2 35.0 %collective-permute-start.8 = (bf16[384,1024]{1,0:T(8,128)(2,1)S(1)}, bf16[384,1024]{1,0:T(8,128)(2,1)}, u32[]{:S(2)}, u32[]{:S(2)}) collective-permute-start(bf16[384,1024]{1,0:T(8,128)(2,1)S(1)} %get-tuple-element.441), channel_id=1, source_target_pairs={{0,24},{8,16},{16,8},{24,0},{1,25},{9,17},{17,9},{25,1},{2,26},{10... | collective-permute-start | bytes 2359304 | tf_op jit(solution)/shard_map/ppermute | solution.py:58
  123.3 28.9 %all-to-all-start.1 = ((bf16[4,128,2048]{2,1,0:T(8,128)(2,1)}), bf16[4,128,2048]{2,1,0:T(8,128)(2,1)}, u32[]{:S(2)}, u32[]{:S(2)}) async-start(bf16[4,128,2048]{2,1,0:T(8,128)(2,1)} %bitcast.218), calls=%async_computation.1 | async-start | bytes 4194304 | tf_op jit(solution)/shard_map/all_to_all | solution.py:62
  129.7 27.0 %collective-permute-start.9 = (bf16[128,1024]{1,0:T(8,128)(2,1)}, bf16[128,1024]{1,0:T(8,128)(2,1)S(1)}, u32[]{:S(2)}, u32[]{:S(2)}) collective-permute-start(bf16[128,1024]{1,0:T(8,128)(2,1)} %get-tuple-element.466), channel_id=1, source_target_pairs={{0,8},{8,0},{16,24},{24,16},{1,9},{9,1},{17,25},{25,17},{2,10},{10... | collective-permute-start | bytes 786440 | tf_op jit(solution)/shard_map/ppermute | solution.py:58
  132.3 31.0 %collective-permute-start.11 = (bf16[128,1024]{1,0:T(8,128)(2,1)}, bf16[128,1024]{1,0:T(8,128)(2,1)}, u32[]{:S(2)}, u32[]{:S(2)}) collective-permute-start(bf16[128,1024]{1,0:T(8,128)(2,1)} %get-tuple-element.464), channel_id=1, source_target_pairs={{0,24},{8,16},{16,8},{24,0},{1,25},{9,17},{17,9},{25,1},{2,26},{10... | collective-permute-start | bytes 786440 | tf_op jit(solution)/shard_map/ppermute | solution.py:58
  135.8 50.8 %collective-permute-start.12 = (bf16[3,384,1024]{2,1,0:T(8,128)(2,1)}, bf16[3,384,1024]{2,1,0:T(8,128)(2,1)}, u32[]{:S(2)}, u32[]{:S(2)}) collective-permute-start(bf16[3,384,1024]{2,1,0:T(8,128)(2,1)} %pad_maximum_fusion.2), channel_id=1, source_target_pairs={{0,2},{2,0},{4,6},{6,4},{1,3},{3,1},{5,7},{7,5},{8,10},{10,8},{12,... | collective-permute-start | bytes 7077896 | tf_op jit(solution)/shard_map/ppermute | solution.py:58
  166.2 28.9 %all-to-all-start.2 = ((bf16[4,128,2048]{2,1,0:T(8,128)(2,1)}), bf16[4,128,2048]{2,1,0:T(8,128)(2,1)}, u32[]{:S(2)}, u32[]{:S(2)}) async-start(bf16[4,128,2048]{2,1,0:T(8,128)(2,1)} %broadcast_in_dim.71), calls=%async_computation.2 | async-start | bytes 4194304 | tf_op jit(solution)/shard_map/all_to_all | solution.py:62
  172.7 34.0 %collective-permute-start.13 = (bf16[3,128,1024]{2,1,0:T(8,128)(2,1)}, bf16[3,128,1024]{2,1,0:T(8,128)(2,1)}, u32[]{:S(2)}, u32[]{:S(2)}) collective-permute-start(bf16[3,128,1024]{2,1,0:T(8,128)(2,1)} %pad_maximum_fusion.4), channel_id=1, source_target_pairs={{0,2},{2,0},{4,6},{6,4},{1,3},{3,1},{5,7},{7,5},{8,10},{10,8},{12,... | collective-permute-start | bytes 2359304 | tf_op jit(solution)/shard_map/ppermute | solution.py:58
  197.7 29.3 %all-to-all-start.3 = ((bf16[4,128,2048]{2,1,0:T(8,128)(2,1)}), bf16[4,128,2048]{2,1,0:T(8,128)(2,1)}, u32[]{:S(2)}, u32[]{:S(2)}) async-start(bf16[4,128,2048]{2,1,0:T(8,128)(2,1)} %broadcast_in_dim.72), calls=%async_computation.3 | async-start | bytes 4194304 | tf_op jit(solution)/shard_map/all_to_all | solution.py:62
  206.7 28.5 %collective-permute-start.14 = (bf16[512,2048]{1,0:T(8,128)(2,1)}, bf16[512,2048]{1,0:T(8,128)(2,1)}, u32[]{:S(2)}, u32[]{:S(2)}) collective-permute-start(bf16[512,2048]{1,0:T(8,128)(2,1)} %bitcast.66), channel_id=1, source_target_pairs={{0,1},{1,0},{2,3},{3,2},{4,5},{5,4},{6,7},{7,6},{8,9},{9,8},{10,11... | collective-permute-start | bytes 6291464 | tf_op jit(solution)/shard_map/ppermute | solution.py:58
  227.0 29.0 %collective-permute-start.15 = (bf16[512,2048]{1,0:T(8,128)(2,1)}, bf16[512,2048]{1,0:T(8,128)(2,1)S(1)}, u32[]{:S(2)}, u32[]{:S(2)}) collective-permute-start(bf16[512,2048]{1,0:T(8,128)(2,1)} %bitcast.74), channel_id=1, source_target_pairs={{0,1},{1,0},{2,3},{3,2},{4,5},{5,4},{6,7},{7,6},{8,9},{9,8},{10,11... | collective-permute-start | bytes 6291464 | tf_op jit(solution)/shard_map/ppermute | solution.py:58
  343.1 27.5 %collective-permute-start.20 = (bf16[512,1024]{1,0:T(8,128)(2,1)}, bf16[512,1024]{1,0:T(8,128)(2,1)}, u32[]{:S(2)}, u32[]{:S(2)}) collective-permute-start(bf16[512,1024]{1,0:T(8,128)(2,1)} %get-tuple-element.242.refs_0_), channel_id=1, source_target_pairs={{0,2},{2,0},{4,6},{6,4},{1,3},{3,1},{5,7},{7,5},{8,10},{10,8},{12,... | collective-permute-start | bytes 3145736 | tf_op jit(solution)/shard_map/ppermute | solution.py:252
  349.3 36.4 %all-to-all-start.4 = ((bf16[4,128,2048]{2,1,0:T(8,128)(2,1)}), bf16[4,128,2048]{2,1,0:T(8,128)(2,1)}, u32[]{:S(2)}, u32[]{:S(2)}) async-start(bf16[4,128,2048]{2,1,0:T(8,128)(2,1)} %bitcast.220), calls=%async_computation.4 | async-start | bytes 4194304 | tf_op jit(solution)/shard_map/all_to_all | solution.py:62
  424.4 28.8 %all-to-all-start.5 = ((bf16[4,128,2048]{2,1,0:T(8,128)(2,1)}), bf16[4,128,2048]{2,1,0:T(8,128)(2,1)}, u32[]{:S(2)}, u32[]{:S(2)}) async-start(bf16[4,128,2048]{2,1,0:T(8,128)(2,1)} %broadcast_in_dim.75), calls=%async_computation.5 | async-start | bytes 4194304 | tf_op jit(solution)/shard_map/all_to_all | solution.py:62
  468.3 38.2 %collective-permute-start.31 = (bf16[512,2048]{1,0:T(8,128)(2,1)}, bf16[512,2048]{1,0:T(8,128)(2,1)}, u32[]{:S(2)}, u32[]{:S(2)}) collective-permute-start(bf16[512,2048]{1,0:T(8,128)(2,1)} %bitcast.79), channel_id=1, source_target_pairs={{0,1},{1,0},{2,3},{3,2},{4,5},{5,4},{6,7},{7,6},{8,9},{9,8},{10,11... | collective-permute-start | bytes 6291464 | tf_op jit(solution)/shard_map/ppermute | solution.py:58
  472.4 29.6 %all-to-all-start.6 = ((bf16[4,128,2048]{2,1,0:T(8,128)(2,1)}), bf16[4,128,2048]{2,1,0:T(8,128)(2,1)}, u32[]{:S(2)}, u32[]{:S(2)}) async-start(bf16[4,128,2048]{2,1,0:T(8,128)(2,1)} %bitcast.219), calls=%async_computation.6 | async-start | bytes 4194304 | tf_op jit(solution)/shard_map/all_to_all | solution.py:62
  482.0 41.8 %collective-permute-start.29 = (bf16[512,1024]{1,0:T(8,128)(2,1)}, bf16[512,1024]{1,0:T(8,128)(2,1)}, u32[]{:S(2)}, u32[]{:S(2)}) collective-permute-start(bf16[512,1024]{1,0:T(8,128)(2,1)} %get-tuple-element.275.refs_0_), channel_id=1, source_target_pairs={{0,2},{2,0},{4,6},{6,4},{1,3},{3,1},{5,7},{7,5},{8,10},{10,8},{12,... | collective-permute-start | bytes 3145736 | tf_op jit(solution)/shard_map/ppermute | solution.py:252
  486.6 37.3 %collective-permute-start.30 = (bf16[512,1024]{1,0:T(8,128)(2,1)}, bf16[512,1024]{1,0:T(8,128)(2,1)}, u32[]{:S(2)}, u32[]{:S(2)}) collective-permute-start(bf16[512,1024]{1,0:T(8,128)(2,1)} %get-tuple-element.276.refs_2_), channel_id=1, source_target_pairs={{2,4},{4,2},{3,5},{5,3},{10,12},{12,10},{11,13},{13,11},{18,20},{2... | collective-permute-start | bytes 3145736 | tf_op jit(solution)/shard_map/ppermute | solution.py:250
  537.3 28.6 %collective-permute-start.32 = (bf16[512,1024]{1,0:T(8,128)(2,1)S(1)}, bf16[512,1024]{1,0:T(8,128)(2,1)S(1)}, u32[]{:S(2)}, u32[]{:S(2)}) collective-permute-start(bf16[512,1024]{1,0:T(8,128)(2,1)S(1)} %get-tuple-element.288.refs_2_), channel_id=1, source_target_pairs={{0,2},{2,0},{4,6},{6,4},{1,3},{3,1},{5,7},{7,5},{8,10},{10,8},{12,... | collective-permute-start | bytes 3145736 | tf_op jit(solution)/shard_map/ppermute | solution.py:252
  568.0 27.4 %collective-permute-start.35 = (bf16[512,1024]{1,0:T(8,128)(2,1)}, bf16[512,1024]{1,0:T(8,128)(2,1)}, u32[]{:S(2)}, u32[]{:S(2)}) collective-permute-start(bf16[512,1024]{1,0:T(8,128)(2,1)} %get-tuple-element.296.refs_4_), channel_id=1, source_target_pairs={{0,2},{2,0},{4,6},{6,4},{1,3},{3,1},{5,7},{7,5},{8,10},{10,8},{12,... | collective-permute-start | bytes 3145736 | tf_op jit(solution)/shard_map/ppermute | solution.py:252
  573.3 31.3 %all-to-all-start.7 = ((bf16[4,128,2048]{2,1,0:T(8,128)(2,1)}), bf16[4,128,2048]{2,1,0:T(8,128)(2,1)}, u32[]{:S(2)}, u32[]{:S(2)}) async-start(bf16[4,128,2048]{2,1,0:T(8,128)(2,1)} %bitcast.217), calls=%async_computation.7 | async-start | bytes 4194304 | tf_op jit(solution)/shard_map/all_to_all | solution.py:62
  598.4 27.5 %collective-permute-start.38 = (bf16[512,1024]{1,0:T(8,128)(2,1)}, bf16[512,1024]{1,0:T(8,128)(2,1)}, u32[]{:S(2)}, u32[]{:S(2)}) collective-permute-start(bf16[512,1024]{1,0:T(8,128)(2,1)} %get-tuple-element.303.refs_6_), channel_id=1, source_target_pairs={{0,2},{2,0},{4,6},{6,4},{1,3},{3,1},{5,7},{7,5},{8,10},{10,8},{12,... | collective-permute-start | bytes 3145736 | tf_op jit(solution)/shard_map/ppermute | solution.py:252
  649.0 30.8 %all-to-all-start.9 = ((f32[4,2,512]{2,1,0:T(2,128)}), f32[4,2,512]{2,1,0:T(2,128)S(1)}, u32[]{:S(2)}, u32[]{:S(2)}) async-start(f32[4,2,512]{2,1,0:T(2,128)} %maximum_bitcast_fusion), calls=%async_computation.9 | async-start | bytes 32768 | tf_op jit(solution)/shard_map/all_to_all | solution.py:62
  679.8 51.7 %all-to-all-start.10 = ((bf16[4,512,1024]{2,1,0:T(8,128)(2,1)}), bf16[4,512,1024]{2,1,0:T(8,128)(2,1)}, u32[]{:S(2)}, u32[]{:S(2)}) async-start(bf16[4,512,1024]{2,1,0:T(8,128)(2,1)} %copy-done.13), calls=%async_computation.10 | async-start | bytes 8388608 | tf_op jit(solution)/shard_map/all_to_all | solution.py:62
  742.9 28.7 %collective-permute-start.50 = (bf16[4,512,1024]{2,1,0:T(8,128)(2,1)}, bf16[4,512,1024]{2,1,0:T(8,128)(2,1)}, u32[]{:S(2)}, u32[]{:S(2)}) collective-permute-start(bf16[4,512,1024]{2,1,0:T(8,128)(2,1)} %all-to-all-done.10.mine_ref), channel_id=1, source_target_pairs={{0,1},{1,0},{2,3},{3,2},{4,5},{5,4},{6,7},{7,6},{8,9},{9,8},{10,11... | collective-permute-start | bytes 12582920 | tf_op jit(solution)/shard_map/ppermute | solution.py:58
  756.1 52.5 %all-to-all-start.11 = ((bf16[4,512,1024]{2,1,0:T(8,128)(2,1)}), bf16[4,512,1024]{2,1,0:T(8,128)(2,1)}, u32[]{:S(2)}, u32[]{:S(2)}) async-start(bf16[4,512,1024]{2,1,0:T(8,128)(2,1)} %copy-done.14), calls=%async_computation.11 | async-start | bytes 8388608 | tf_op jit(solution)/shard_map/all_to_all | solution.py:62
  765.2 28.4 %collective-permute-start.48 = (bf16[512,1024]{1,0:T(8,128)(2,1)}, bf16[512,1024]{1,0:T(8,128)(2,1)}, u32[]{:S(2)}, u32[]{:S(2)}) collective-permute-start(bf16[512,1024]{1,0:T(8,128)(2,1)} %get-tuple-element.345.refs_0_), channel_id=1, source_target_pairs={{0,2},{2,0},{4,6},{6,4},{1,3},{3,1},{5,7},{7,5},{8,10},{10,8},{12,... | collective-permute-start | bytes 3145736 | tf_op jit(solution)/shard_map/ppermute | solution.py:252
  810.5 28.6 %collective-permute-start.51 = (bf16[512,1024]{1,0:T(8,128)(2,1)S(1)}, bf16[512,1024]{1,0:T(8,128)(2,1)S(1)}, u32[]{:S(2)}, u32[]{:S(2)}) collective-permute-start(bf16[512,1024]{1,0:T(8,128)(2,1)S(1)} %get-tuple-element.352.refs_2_), channel_id=1, source_target_pairs={{0,2},{2,0},{4,6},{6,4},{1,3},{3,1},{5,7},{7,5},{8,10},{10,8},{12,... | collective-permute-start | bytes 3145736 | tf_op jit(solution)/shard_map/ppermute | solution.py:252
  842.8 27.4 %collective-permute-start.55 = (bf16[512,1024]{1,0:T(8,128)(2,1)S(1)}, bf16[512,1024]{1,0:T(8,128)(2,1)}, u32[]{:S(2)}, u32[]{:S(2)}) collective-permute-start(bf16[512,1024]{1,0:T(8,128)(2,1)S(1)} %shard_map.273.refs_0_), channel_id=1, source_target_pairs={{0,2},{2,0},{4,6},{6,4},{1,3},{3,1},{5,7},{7,5},{8,10},{10,8},{12,... | collective-permute-start | bytes 3145736 | tf_op jit(solution)/shard_map/ppermute | solution.py:252
  (114 other events, 1553.6 us)

commit v4 on v3

--- a/solution.py
+++ b/solution.py
@@ -606,32 +606,30 @@
     grad_active = contract_last(cot_all, down_rows)
     grad_gate_pre = (grad_active * up * sigma * (1.0 + gate * (1.0 - sigma))).astype(BF)
     grad_up_pre = (grad_active * gate * sigma).astype(BF)
-    grad_gate_pre, grad_up_pre = slot(
-        (("down", 1), grad_down, (0, 1)), grad_gate_pre, grad_up_pre
-    )
     first_pre, second_pre = ordered(grad_gate_pre, grad_up_pre)
-    send = scatter_send(
-        contract_last(first_pre, first_full) + contract_last(second_pre, second_full)
-    )
-    send = slot((("down", 2), grad_down, (1, 0)), send)
-    grad_normed_two = scatter_sum(send)
-    grad_gate = contract_first(normed_two, clock.now(grad_gate_pre)).astype(BF)
-    grad_gate = slot((("down", 3), grad_down, (1, 1)), grad_gate)
+    partial = contract_last(first_pre, first_full) + contract_last(second_pre, second_full)
+    grad_gate_pre, grad_up_pre, partial = slot(
+        (("down", 1), grad_down, (0, 1)), grad_gate_pre, grad_up_pre, partial
+    )
+    grad_normed_two = scatter_sum(scatter_send(partial))
+    grad_gate = contract_first(normed_two, grad_gate_pre).astype(BF)
+    grad_gate = clock.tick(grad_gate) if not on_line else grad_gate
+    slot((("gate", 0), grad_gate, (0, 0)))
     grad_up = contract_first(normed_two, clock.now(grad_up_pre)).astype(BF)
-    grad_up, grad_normed_two = slot((("gate", 0), grad_gate, (0, 0)), grad_up, grad_normed_two)
+    grad_up, grad_normed_two = slot((("gate", 1), grad_gate, (1, 0)), grad_up, grad_normed_two)
     grad_y = cotangent[0].astype(F32)
     grad_gain_two = jnp.sum(grad_normed_two * unit_two, axis=0)
     grad_mid = grad_y + norm_back(grad_normed_two, unit_two, inverse_two, gain_two)
     grad_branch = spread(grad_mid.astype(BF))
-    send = scatter_send(matmul(clock.now(active), down_rows))
-    grad_mid, grad_gain_two, send = slot(
-        (("gate", 1), grad_gate, (1, 0)), grad_mid, grad_gain_two, send
-    )
-    grad_branch = slot((("gate", 2), grad_gate, (2, 0)), grad_branch)
-    result = mid + scatter_sum(clock.now(send))
+    grad_mid, grad_gain_two, grad_branch = slot(
+        (("gate", 2), grad_gate, (2, 0)), grad_mid, grad_gain_two, grad_branch
+    )
     grad_branch = with_core(grad_branch)
     grad_attended = contract_last(grad_branch, out_rows).astype(BF)
     grad_out = contract_first(attended, grad_branch).astype(BF)
+    grad_attended, grad_out = slot(
+        (("gate", 3), grad_gate, (3, 0)), grad_attended, grad_out
+    )
 
     def both(mine):
         mine = clock.now(mine)
@@ -645,14 +643,73 @@
         [jax.ShapeDtypeStruct((cores * total, qw + 2 * kw), BF)],
         [pltpu.VMEM((total, qw + 2 * kw), F32)],
     )
-    grad_qkv, grad_out, result = slot(
-        (("gate", 3), grad_gate, (3, 0)), grad_qkv, grad_out, result
-    )
+    grad_qkv = slot((("up", 0), grad_up, (0, 0)), grad_qkv)
     grad_weights = contract_first(normed_one, grad_qkv).astype(BF)
     send = scatter_send(contract_last(grad_qkv, qkv_full))
-    grad_weights, send = slot((("up", 0), grad_up, (0, 0)), grad_weights, send)
+    grad_weights, send = slot((("up", 1), grad_up, (1, 0)), grad_weights, send)
     grad_normed_one = scatter_sum(send)
+    grad_normed_one = slot((("up", 2), grad_up, (2, 0)), grad_normed_one)
+    inverse_one = lax.rsqrt(jnp.mean(x_own * x_own, axis=1, keepdims=True) + EPS)
+    unit_one = x_own * inverse_one
+    grad_gain_one = jnp.sum(grad_normed_one * unit_one, axis=0)
+    grad_x = grad_mid + norm_back(grad_normed_one, unit_one, inverse_one, gain_one)
+    each = qw + 2 * kw
+    grad_gains = jnp.stack([grad_gain_one, grad_gain_two]).reshape(2, parts, share)
+    grad_gains = grad_gains.transpose(1, 0, 2).reshape(parts, 2 * share).astype(BF)
+    grad_gains = jnp.pad(grad_gains, ((0, 0), (0, 16 * each - 2 * share)))
+    turned = exchange(
+        jnp.concatenate(
+            [grad_weights.reshape(parts, share, each), grad_gains.reshape(parts, 16, each)],
+            axis=1,
+        )
+    )
+    turned, grad_x = slot((("up", 3), grad_up, (3, 0)), turned, grad_x)
+    grad_gains = turned[:, share:].reshape(parts, 16 * each)[:, : 2 * share]
+    grad_gains = jnp.sum(grad_gains.reshape(parts, 2, share).astype(F32), axis=0)
+    turned = turned[:, :share]
+    turned_q = turned[:, :, :qw].transpose(1, 0, 2).reshape(share, parts * qw)
+    turned_kv = turned[:, :, qw:].transpose(1, 0, 2).reshape(share, parts * 2 * kw)
     if on_line:
+        turned_kv = jnp.concatenate(
+            [
+                turned_kv,
+                jnp.pad(
+                    grad_gains.astype(BF), ((0, share - 2), (0, ff - parts * 2 * kw - share))
+                ),
+            ],
+            axis=1,
+        )
+
+        def turn(name):
+            return exchange(line.stack(name, parts))
+
+        def place_columns(turned):
+            return place(
+                (share, ff * team),
+                *both(turned),
+                share,
+                ff,
+                [((j, 0, 0), lambda k, j=j: (0, j * 2 + k)) for j in range(parts)],
+            )
+
+        gate_turned = turn("gate")
+        grad_out = jnp.concatenate([grad_out[:, :ff], grad_out[:, ff:]], axis=0)
+        turned_q, turned_kv, grad_out = slot(
+            (("down", 2), grad_down, (1, 0)), turned_q, turned_kv, grad_out
+        )
+        result = matmul(clock.now(active), down_rows)
+        gate_turned, result = slot(
+            (("down", 3), grad_down, (1, 1)), gate_turned, result
+        )
+        outs["gate"] = place_columns(gate_turned)
+        outs = slot((("heads", 0), turned_q, (0, 0)), outs)
+        up_turned = turn("up")
+        slot((("heads", 1), turned_kv, (0, 0)))
+        result = scatter_send(clock.now(result))
+        up_turned, result = slot((("rows", 0), grad_out, (0, 0)), up_turned, result)
+        outs["up"] = place_columns(up_turned)
+        result = mid + scatter_sum(result)
+        outs, result = slot(None, outs, result)
         outs["down"] = place(
             (ff * 2, width),
             *both(line.stack("down", 4)),
@@ -664,52 +721,6 @@
                 for b in range(2)
             ],
         )
-        grad_out = jnp.concatenate([grad_out[:, :ff], grad_out[:, ff:]], axis=0)
-    outs = slot((("up", 1), grad_up, (1, 0)), outs)
-    grad_normed_one, outs = slot((("up", 2), grad_up, (2, 0)), grad_normed_one, outs)
-    turned = exchange(clock.now(grad_weights).reshape(parts, share, qw + 2 * kw))
-    inverse_one = lax.rsqrt(jnp.mean(x_own * x_own, axis=1, keepdims=True) + EPS)
-    unit_one = x_own * inverse_one
-    grad_gain_one = jnp.sum(grad_normed_one * unit_one, axis=0)
-    grad_x = grad_mid + norm_back(grad_normed_one, unit_one, inverse_one, gain_one)
-    grad_gains = jnp.stack([grad_gain_one, grad_gain_two]).reshape(2, parts, share)
-    grad_gains = jnp.sum(exchange(grad_gains.transpose(1, 0, 2)), axis=0)
-    turned, grad_x = slot((("up", 3), grad_up, (3, 0)), turned, grad_x)
-    turned_q = turned[:, :, :qw].transpose(1, 0, 2).reshape(share, parts * qw)
-    turned_kv = turned[:, :, qw:].transpose(1, 0, 2).reshape(share, parts * 2 * kw)
-    grad_gains, turned_q, turned_kv = slot(
-        (("heads", 0), turned_q, (0, 0)), grad_gains, turned_q, turned_kv
-    )
-    if on_line:
-        turned_kv = jnp.concatenate(
-            [
-                turned_kv,
-                jnp.pad(
-                    grad_gains.astype(BF), ((0, share - 2), (0, ff - parts * 2 * kw - share))
-                ),
-            ],
-            axis=1,
-        )
-
-        def turn(name):
-            return exchange(line.stack(name, parts))
-
-        def place_columns(turned):
-            return place(
-                (share, ff * team),
-                *both(turned),
-                share,
-                ff,
-                [((j, 0, 0), lambda k, j=j: (0, j * 2 + k)) for j in range(parts)],
-            )
-
-        gate_turned = turn("gate")
-        turned_kv = slot((("heads", 1), turned_kv, (0, 0)), turned_kv)
-        gate_turned = slot((("rows", 0), grad_out, (0, 0)), gate_turned)
-        outs["gate"] = place_columns(gate_turned)
-        up_turned = turn("up")
-        outs, up_turned = slot(None, outs, up_turned)
-        outs["up"] = place_columns(up_turned)
         outs = slot(None, outs)
         mine, other = both(line.stack("heads", 2))
         grad_gains = sum(
@@ -740,6 +751,8 @@
             [((0, b, 0), lambda k, b=b: (k, b)) for b in range(2)],
         )
     else:
+        result = mid + scatter_sum(scatter_send(matmul(active, down_rows)))
+
         def whole(value):
             value = lax.psum(value, "rest")[None]
             if cores == 2:

time: 898 us -> 872 us (0.971)
  waiting for transfers between devices: 306 us -> 263 us
  local copies, waits for them, and re-layouts: 117 us -> 143 us
  starting transfers between devices: 177 us -> 167 us
    ppermute x17, waiting for transfers between devices: 187 us -> 160 us  [slot(): lax.ppermute(send, 'rest', [(0, 1), (1, 0), (2, 3), (3, 2)])]
    unnamed x158 -> x227, local copies, waits for them, and re-layouts: 32.3 us -> 54.1 us
    all_to_all x12 -> x11, waiting for transfers between devices: 68.7 us -> 53.6 us  [exchange(): return lax.all_to_all(blocks, 'group', 0, 0, tiled=True)]
    all_to_all x12 -> x11, starting transfers between devices: 54 us -> 50.3 us  [exchange(): return lax.all_to_all(blocks, 'group', 0, 0, tiled=True)]
  transfers between devices with their start and end apart: 69 -> 68, of which waited for: 32 -> 30; matrix products, arithmetic and copies ran while one was open for 23% -> 26% of each run, Pallas kernels for 11% -> 11%
where the time goes in v4:
time: 872 us; the launch traced here: 858 us
  waiting for transfers between devices  263 us (30%)
  starting transfers between devices  167 us (19%)
  local copies, waits for them, and re-layouts  143 us (16%)
  Pallas kernels  118 us (14%)
  matrix products  98 us (11%)
  other arithmetic  66.3 us (8%)
    ppermute x17, waiting for transfers between devices, slot(): lax.ppermute(send, 'rest', [(0, 1), (1, 0), (2, 3), (3, 2)])  160 us
    ppermute x17, starting transfers between devices, slot(): lax.ppermute(send, 'rest', [(0, 1), (1, 0), (2, 3), (3, 2)])  62.4 us
    unnamed x227, local copies, waits for them, and re-layouts  54.1 us
    all_to_all x11, waiting for transfers between devices, exchange(): return lax.all_to_all(blocks, 'group', 0, 0, tiled=True)  53.6 us
    all_to_all x11, starting transfers between devices, exchange(): return lax.all_to_all(blocks, 'group', 0, 0, tiled=True)  50.3 us
    ppermute x25, waiting for transfers between devices, step_to(): return lax.ppermute(value, axis, [(i, i ^ step) for i in range(size)])  49.7 us
    pallas_call x5, Pallas kernels, place(): pl.pallas_call(kernel, grid_spec=pltpu.PrefetchScalarGridSpec(num_scalar_...  46.9 us
    dot_general x5, matrix products, contract_last(): lax.dot_general(left, right, (((1,), (1,)), ((), ())), preferred_element_...  35.6 us
  transfers between devices with their start and end apart: 68, of which 30 were waited for; matrix products, arithmetic and copies ran while one was open for 26% of the time, Pallas kernels for 11%

profile of v4, /device:TPU:1, one launch (start us, length us, event | category | flops | bytes accessed | tf_op | source)
XLA Modules:
  0.0 857.7 jit_solution(13567019440208079034)
XLA Ops:
  47.0 7.8 collective-permute-done.2
  70.5 9.8 %shard_map.248 = (bf16[1024,256]{1,0:T(8,128)(2,1)S(1)}, bf16[1024,384]{1,0:T(8,128)(2,1)S(1)}, f32[1024,128]{1,0:T(8,128)S(1)}) custom-call(f32[1024,384]{1,0:T(8,128)S(1)} %fusion.39.qkv_ref, f32[1024,128]{1,0:T(8,128)S(1)} %copy-done.21, f32[1024,128]{1,0:T(8,128)S(1)} %get-tuple-element.197.sin_ref, s32[2,512,2]{2,1,0:T(8,128)S(1)} %copy.63.column_ref, ...), custom_call_target="tpu_custom_call" | custom-call | bytes 1 | tf_op jit(solution)/shard_map/pallas_call | solution.py:195
  97.5 8.9 %collective-permute-done.6 = bf16[384,1024]{1,0:T(8,128)(2,1)} collective-permute-done((bf16[384,1024]{1,0:T(8,128)(2,1)S(1)}, bf16[384,1024]{1,0:T(8,128)(2,1)}, u32[]{:S(2)}, u32[]{:S(2)}) %collective-permute-start.6) | collective-permute-done | bytes 786464 | tf_op jit(solution)/shard_map/ppermute | solution.py:58
  106.4 16.8 %collective-permute-done.8 = bf16[384,1024]{1,0:T(8,128)(2,1)} collective-permute-done((bf16[384,1024]{1,0:T(8,128)(2,1)S(1)}, bf16[384,1024]{1,0:T(8,128)(2,1)}, u32[]{:S(2)}, u32[]{:S(2)}) %collective-permute-start.8) | collective-permute-done | bytes 786464 | tf_op jit(solution)/shard_map/ppermute | solution.py:58
  178.3 8.3 collective-permute-done.12
  208.1 18.8 %all-to-all-done.3 = bf16[4,128,2048]{2,1,0:T(8,128)(2,1)} async-done(((bf16[4,128,2048]{2,1,0:T(8,128)(2,1)}), bf16[4,128,2048]{2,1,0:T(8,128)(2,1)}, u32[]{:S(2)}, u32[]{:S(2)}) %all-to-all-start.3) | async-done | bytes 2097184 | tf_op jit(solution)/shard_map/all_to_all | solution.py:62
  236.9 7.8 fusion.45
  244.7 11.2 %multiply_convert_fusion.2 = (bf16[1024,1024]{1,0:T(8,128)(2,1)S(1)}, f32[1024,1024]{1,0:T(8,128)}, f32[1024,1024]{1,0:T(8,128)}) fusion(f32[1024,1024]{1,0:T(8,128)S(1)} %fusion.45, pred[]{:T(512)S(6)} %eq.74, bf16[1024,2048]{1,0:T(8,128)(2,1)S(1)} %constant_dynamic-update-slice_fusion.6, bf16[2048,1024]{1,0:T(8,128)(2,1)} %bitcast.72), kind=kOutput, calls=%fused_computation.22 | convolution fusion | flops 4303355904 | bytes 23068672 | tf_op jit(solution)/shard_map/dot_general | solution.py:32
  267.2 10.6 %multiply_convert_fusion = (bf16[1024,1024]{1,0:T(8,128)(2,1)S(1)}, bf16[1024,1024]{1,0:T(8,128)(2,1)}) fusion(f32[1024,1024]{1,0:T(8,128)} %get-tuple-element.433, f32[1024,1024]{1,0:T(8,128)} %get-tuple-element.496, f32[1024,1024]{1,0:T(8,128)} %copy-done.107, pred[]{:T(512)S(6)} %eq.74, bf16[1024,2048]{1,0:T(8,128)(2,1)S(1)} %pad_maximum_fusion.1, ...), kind=kOutput, calls=%fused_computation.20 | convolution fusion | flops 4309647360 | bytes 25165828 | tf_op jit(solution)/shard_map/dot_general | solution.py:36
  277.8 11.0 %fusion.9 = f32[1024,2048]{1,0:T(8,128)} fusion(bf16[2048,1024]{1,0:T(8,128)(2,1)} %bitcast.72, bf16[1024,1024]{1,0:T(8,128)(2,1)S(1)} %get-tuple-element.243, bf16[1024,1024]{1,0:T(8,128)(2,1)} %get-tuple-element.238, pred[]{:T(512)S(6)} %eq.74), kind=kOutput, calls=%fused_computation.38 | convolution fusion | flops 4296015872 | bytes 16777216 | tf_op jit(solution)/shard_map/dot_general | solution.py:36
  288.8 10.3 %convolution_add_fusion = f32[1024,2048]{1,0:T(8,128)} fusion(f32[1024,2048]{1,0:T(8,128)} %fusion.9, bf16[2048,1024]{1,0:T(8,128)(2,1)} %bitcast.71, bf16[1024,1024]{1,0:T(8,128)(2,1)S(1)} %copy-done.106, bf16[1024,1024]{1,0:T(8,128)(2,1)S(1)} %get-tuple-element.243, pred[]{:T(512)S(6)} %eq.74), kind=kOutput, calls=%fused_computation.25 | convolution fusion | flops 4298113024 | bytes 25165824 | tf_op jit(solution)/shard_map/dot_general | solution.py:36
  313.9 7.6 convolution_convert_fusion.1.refs_4_.refs_1_
  321.6 7.6 collective-permute-done.17.refs_0_
  347.6 12.2 %collective-permute-done.19.refs_0_.refs_1_ = bf16[512,1024]{1,0:T(8,128)(2,1)} collective-permute-done((bf16[512,1024]{1,0:T(8,128)(2,1)}, bf16[512,1024]{1,0:T(8,128)(2,1)}, u32[]{:S(2)}, u32[]{:S(2)}) %collective-permute-start.19) | collective-permute-done | bytes 1048608 | tf_op jit(solution)/shard_map/ppermute | solution.py:252
  379.5 18.6 %collective-permute-done.22.refs_0_.refs_3_ = bf16[512,1024]{1,0:T(8,128)(2,1)S(1)} collective-permute-done((bf16[512,1024]{1,0:T(8,128)(2,1)S(1)}, bf16[512,1024]{1,0:T(8,128)(2,1)S(1)}, u32[]{:S(2)}, u32[]{:S(2)}) %collective-permute-start.22) | collective-permute-done | bytes 1048608 | tf_op jit(solution)/shard_map/ppermute | solution.py:252
  419.3 17.0 %collective-permute-done.24.refs_0_.refs_1_ = bf16[512,1024]{1,0:T(8,128)(2,1)S(1)} collective-permute-done((bf16[512,1024]{1,0:T(8,128)(2,1)S(1)}, bf16[512,1024]{1,0:T(8,128)(2,1)S(1)}, u32[]{:S(2)}, u32[]{:S(2)}) %collective-permute-start.24) | collective-permute-done | bytes 1048608 | tf_op jit(solution)/shard_map/ppermute | solution.py:252
  441.3 11.8 %shard_map.255 = bf16[1024,384]{1,0:T(8,128)(2,1)S(1)} custom-call(bf16[1024,384]{1,0:T(8,128)(2,1)S(1)} %copy-done.64, f32[1024,128]{1,0:T(8,128)S(1)} %copy-done.68, bf16[1024,256]{1,0:T(8,128)(2,1)S(1)} %convolution_convert_fusion.5.grad_ref, f32[1024,128]{1,0:T(8,128)S(1)} %copy-done.22, f32[1024,128]{1,0:T(8,128)S(1)} %get-tuple-element.197.sin_ref, ...), custom_call_target="tpu_custom_call" | custom-call | bytes 1 | tf_op jit(solution)/shard_map/pallas_call | solution.py:195
  453.1 9.8 %collective-permute-done.27.refs_0_.refs_3_ = bf16[512,1024]{1,0:T(8,128)(2,1)S(1)} collective-permute-done((bf16[512,1024]{1,0:T(8,128)(2,1)S(1)}, bf16[512,1024]{1,0:T(8,128)(2,1)S(1)}, u32[]{:S(2)}, u32[]{:S(2)}) %collective-permute-start.27) | collective-permute-done | bytes 1048608 | tf_op jit(solution)/shard_map/ppermute | solution.py:252
  480.2 13.0 %collective-permute-done.29.refs_0_.refs_5_ = bf16[512,1024]{1,0:T(8,128)(2,1)S(1)} collective-permute-done((bf16[512,1024]{1,0:T(8,128)(2,1)S(1)}, bf16[512,1024]{1,0:T(8,128)(2,1)S(1)}, u32[]{:S(2)}, u32[]{:S(2)}) %collective-permute-start.29) | collective-permute-done | bytes 1048608 | tf_op jit(solution)/shard_map/ppermute | solution.py:252
  510.2 12.8 %all-to-all-done.6 = bf16[4,128,2048]{2,1,0:T(8,128)(2,1)} async-done(((bf16[4,128,2048]{2,1,0:T(8,128)(2,1)}), bf16[4,128,2048]{2,1,0:T(8,128)(2,1)}, u32[]{:S(2)}, u32[]{:S(2)}) %all-to-all-start.6) | async-done | bytes 2097184 | tf_op jit(solution)/shard_map/all_to_all | solution.py:62
  582.7 12.1 %collective-permute-done.36.refs_0_.refs_3_ = bf16[512,1024]{1,0:T(8,128)(2,1)} collective-permute-done((bf16[512,1024]{1,0:T(8,128)(2,1)}, bf16[512,1024]{1,0:T(8,128)(2,1)}, u32[]{:S(2)}, u32[]{:S(2)}) %collective-permute-start.36) | collective-permute-done | bytes 1048608 | tf_op jit(solution)/shard_map/ppermute | solution.py:252
  608.2 8.9 %fusion.5 = f32[1024,2048]{1,0:T(8,128)} fusion(bf16[1024,1024]{1,0:T(8,128)(2,1)S(1)} %copy-done.103, bf16[2048,2048]{1,0:T(8,128)(2,1)} %param.27, s32[]{:T(128)S(6)} %select_n.289), kind=kOutput, calls=%fused_computation.29 | convolution fusion | flops 4294967296 | bytes 14680068 | tf_op jit(solution)/shard_map/dot_general | solution.py:32
  617.2 7.8 collective-permute-done.38.refs_0_.refs_5_
  642.4 11.9 %shard_map.263 = f32[512,8192]{1,0:T(8,128)} custom-call(s32[40]{0:T(128)S(1)} %reshape.339.table_ref, bf16[4,512,1024]{2,1,0:T(8,128)(2,1)} %all-to-all-done.8.mine_ref, bf16[4,512,1024]{2,1,0:T(8,128)(2,1)} %collective-permute-done.42.other_ref), custom_call_target="tpu_custom_call" | custom-call | bytes 25165824 | tf_op jit(solution)/shard_map/pallas_call | solution.py:398
  654.3 10.2 %collective-permute-done.40.refs_0_.refs_7_ = bf16[512,1024]{1,0:T(8,128)(2,1)} collective-permute-done((bf16[512,1024]{1,0:T(8,128)(2,1)}, bf16[512,1024]{1,0:T(8,128)(2,1)}, u32[]{:S(2)}, u32[]{:S(2)}) %collective-permute-start.40) | collective-permute-done | bytes 1048608 | tf_op jit(solution)/shard_map/ppermute | solution.py:252
  686.2 8.6 %collective-permute-done.43.refs_0_.refs_5_ = bf16[512,1024]{1,0:T(8,128)(2,1)} collective-permute-done((bf16[512,1024]{1,0:T(8,128)(2,1)}, bf16[512,1024]{1,0:T(8,128)(2,1)}, u32[]{:S(2)}, u32[]{:S(2)}) %collective-permute-start.43) | collective-permute-done | bytes 1048608 | tf_op jit(solution)/shard_map/ppermute | solution.py:252
  710.0 18.6 %collective-permute-done.45.refs_0_.refs_7_ = bf16[512,1024]{1,0:T(8,128)(2,1)S(1)} collective-permute-done((bf16[512,1024]{1,0:T(8,128)(2,1)S(1)}, bf16[512,1024]{1,0:T(8,128)(2,1)S(1)}, u32[]{:S(2)}, u32[]{:S(2)}) %collective-permute-start.45) | collective-permute-done | bytes 1048608 | tf_op jit(solution)/shard_map/ppermute | solution.py:252
  754.9 9.2 %all-to-all-done.10 = bf16[4,128,2048]{2,1,0:T(8,128)(2,1)} async-done(((bf16[4,128,2048]{2,1,0:T(8,128)(2,1)}), bf16[4,128,2048]{2,1,0:T(8,128)(2,1)}, u32[]{:S(2)}, u32[]{:S(2)}) %all-to-all-start.10) | async-done | bytes 2097184 | tf_op jit(solution)/shard_map/all_to_all | solution.py:62
  768.4 11.6 %shard_map.268 = f32[512,8192]{1,0:T(8,128)} custom-call(s32[40]{0:T(128)S(1)} %reshape.339.table_ref, bf16[4,512,1024]{2,1,0:T(8,128)(2,1)} %all-to-all-done.9.mine_ref, bf16[4,512,1024]{2,1,0:T(8,128)(2,1)} %collective-permute-done.50.other_ref), custom_call_target="tpu_custom_call" | custom-call | bytes 25165824 | tf_op jit(solution)/shard_map/pallas_call | solution.py:398
  788.0 11.6 %shard_map.271 = f32[2048,2048]{1,0:T(8,128)} custom-call(s32[40]{0:T(128)S(1)} %reshape.342.table_ref, bf16[4,512,1024]{2,1,0:T(8,128)(2,1)} %shard_map.270.mine_ref, bf16[4,512,1024]{2,1,0:T(8,128)(2,1)} %collective-permute-done.53.other_ref), custom_call_target="tpu_custom_call" | custom-call | bytes 25165824 | tf_op jit(solution)/shard_map/pallas_call | solution.py:398
  799.7 10.0 %collective-permute-done.51.refs_3_ = bf16[512,1024]{1,0:T(8,128)(2,1)S(1)} collective-permute-done((bf16[512,1024]{1,0:T(8,128)(2,1)}, bf16[512,1024]{1,0:T(8,128)(2,1)S(1)}, u32[]{:S(2)}, u32[]{:S(2)}) %collective-permute-start.51) | collective-permute-done | bytes 1048608 | tf_op jit(solution)/shard_map/ppermute | solution.py:252
  835.5 8.7 %collective-permute-done.55.refs_1_ = bf16[512,1024]{1,0:T(8,128)(2,1)} collective-permute-done((bf16[512,1024]{1,0:T(8,128)(2,1)S(1)}, bf16[512,1024]{1,0:T(8,128)(2,1)}, u32[]{:S(2)}, u32[]{:S(2)}) %collective-permute-start.55) | collective-permute-done | bytes 1048608 | tf_op jit(solution)/shard_map/ppermute | solution.py:252
  (501 shorter events, 494.6 us)
Async XLA Ops:
  4.3 39.4 %all-to-all-start = ((bf16[4,144,2048]{2,1,0:T(8,128)(2,1)}), bf16[4,144,2048]{2,1,0:T(8,128)(2,1)}, u32[]{:S(2)}, u32[]{:S(2)}) async-start(bf16[4,144,2048]{2,1,0:T(8,128)(2,1)} %broadcast_in_dim.57), calls=%async_computation | async-start | bytes 4718592 | tf_op jit(solution)/shard_map/all_to_all | solution.py:62
  14.7 32.3 %collective-permute-start = (bf16[512,384]{1,0:T(8,128)(2,1)}, bf16[512,384]{1,0:T(8,128)(2,1)S(1)}, u32[]{:S(2)}, u32[]{:S(2)}) collective-permute-start(bf16[512,384]{1,0:T(8,128)(2,1)} %get-tuple-element.470), channel_id=1, source_target_pairs={{0,8},{8,0},{16,24},{24,16},{1,9},{9,1},{17,25},{25,17},{2,10},{10... | collective-permute-start | bytes 1179656 | tf_op jit(solution)/shard_map/ppermute | solution.py:58
  16.7 30.3 %collective-permute-start.1 = (bf16[512,384]{1,0:T(8,128)(2,1)}, bf16[512,384]{1,0:T(8,128)(2,1)S(1)}, u32[]{:S(2)}, u32[]{:S(2)}) collective-permute-start(bf16[512,384]{1,0:T(8,128)(2,1)} %get-tuple-element.469), channel_id=1, source_target_pairs={{0,16},{8,24},{16,0},{24,8},{1,17},{9,25},{17,1},{25,9},{2,18},{10... | collective-permute-start | bytes 1179656 | tf_op jit(solution)/shard_map/ppermute | solution.py:58
  18.0 36.8 %collective-permute-start.2 = (bf16[512,384]{1,0:T(8,128)(2,1)}, bf16[512,384]{1,0:T(8,128)(2,1)}, u32[]{:S(2)}, u32[]{:S(2)}) collective-permute-start(bf16[512,384]{1,0:T(8,128)(2,1)} %get-tuple-element.468), channel_id=1, source_target_pairs={{0,24},{8,16},{16,8},{24,0},{1,25},{9,17},{17,9},{25,1},{2,26},{10... | collective-permute-start | bytes 1179656 | tf_op jit(solution)/shard_map/ppermute | solution.py:58
  88.2 35.0 %collective-permute-start.8 = (bf16[384,1024]{1,0:T(8,128)(2,1)S(1)}, bf16[384,1024]{1,0:T(8,128)(2,1)}, u32[]{:S(2)}, u32[]{:S(2)}) collective-permute-start(bf16[384,1024]{1,0:T(8,128)(2,1)S(1)} %get-tuple-element.450), channel_id=1, source_target_pairs={{0,24},{8,16},{16,8},{24,0},{1,25},{9,17},{17,9},{25,1},{2,26},{10... | collective-permute-start | bytes 2359304 | tf_op jit(solution)/shard_map/ppermute | solution.py:58
  123.2 28.9 %all-to-all-start.1 = ((bf16[4,128,2048]{2,1,0:T(8,128)(2,1)}), bf16[4,128,2048]{2,1,0:T(8,128)(2,1)}, u32[]{:S(2)}, u32[]{:S(2)}) async-start(bf16[4,128,2048]{2,1,0:T(8,128)(2,1)} %bitcast.223), calls=%async_computation.1 | async-start | bytes 4194304 | tf_op jit(solution)/shard_map/all_to_all | solution.py:62
  129.8 26.9 %collective-permute-start.9 = (bf16[128,1024]{1,0:T(8,128)(2,1)}, bf16[128,1024]{1,0:T(8,128)(2,1)S(1)}, u32[]{:S(2)}, u32[]{:S(2)}) collective-permute-start(bf16[128,1024]{1,0:T(8,128)(2,1)} %get-tuple-element.475), channel_id=1, source_target_pairs={{0,8},{8,0},{16,24},{24,16},{1,9},{9,1},{17,25},{25,17},{2,10},{10... | collective-permute-start | bytes 786440 | tf_op jit(solution)/shard_map/ppermute | solution.py:58
  131.2 26.6 %collective-permute-start.10 = (bf16[128,1024]{1,0:T(8,128)(2,1)}, bf16[128,1024]{1,0:T(8,128)(2,1)}, u32[]{:S(2)}, u32[]{:S(2)}) collective-permute-start(bf16[128,1024]{1,0:T(8,128)(2,1)} %get-tuple-element.474), channel_id=1, source_target_pairs={{0,16},{8,24},{16,0},{24,8},{1,17},{9,25},{17,1},{25,9},{2,18},{10... | collective-permute-start | bytes 786440 | tf_op jit(solution)/shard_map/ppermute | solution.py:58
  132.4 30.9 %collective-permute-start.11 = (bf16[128,1024]{1,0:T(8,128)(2,1)}, bf16[128,1024]{1,0:T(8,128)(2,1)}, u32[]{:S(2)}, u32[]{:S(2)}) collective-permute-start(bf16[128,1024]{1,0:T(8,128)(2,1)} %get-tuple-element.473), channel_id=1, source_target_pairs={{0,24},{8,16},{16,8},{24,0},{1,25},{9,17},{17,9},{25,1},{2,26},{10... | collective-permute-start | bytes 786440 | tf_op jit(solution)/shard_map/ppermute | solution.py:58
  135.8 50.8 %collective-permute-start.12 = (bf16[3,384,1024]{2,1,0:T(8,128)(2,1)}, bf16[3,384,1024]{2,1,0:T(8,128)(2,1)}, u32[]{:S(2)}, u32[]{:S(2)}) collective-permute-start(bf16[3,384,1024]{2,1,0:T(8,128)(2,1)} %pad_maximum_fusion.2), channel_id=1, source_target_pairs={{0,2},{2,0},{4,6},{6,4},{1,3},{3,1},{5,7},{7,5},{8,10},{10,8},{12,... | collective-permute-start | bytes 7077896 | tf_op jit(solution)/shard_map/ppermute | solution.py:58
  166.1 28.9 %all-to-all-start.2 = ((bf16[4,128,2048]{2,1,0:T(8,128)(2,1)}), bf16[4,128,2048]{2,1,0:T(8,128)(2,1)}, u32[]{:S(2)}, u32[]{:S(2)}) async-start(bf16[4,128,2048]{2,1,0:T(8,128)(2,1)} %broadcast_in_dim.71), calls=%async_computation.2 | async-start | bytes 4194304 | tf_op jit(solution)/shard_map/all_to_all | solution.py:62
  172.6 34.0 %collective-permute-start.13 = (bf16[3,128,1024]{2,1,0:T(8,128)(2,1)}, bf16[3,128,1024]{2,1,0:T(8,128)(2,1)}, u32[]{:S(2)}, u32[]{:S(2)}) collective-permute-start(bf16[3,128,1024]{2,1,0:T(8,128)(2,1)} %pad_maximum_fusion.5), channel_id=1, source_target_pairs={{0,2},{2,0},{4,6},{6,4},{1,3},{3,1},{5,7},{7,5},{8,10},{10,8},{12,... | collective-permute-start | bytes 2359304 | tf_op jit(solution)/shard_map/ppermute | solution.py:58
  197.6 29.3 %all-to-all-start.3 = ((bf16[4,128,2048]{2,1,0:T(8,128)(2,1)}), bf16[4,128,2048]{2,1,0:T(8,128)(2,1)}, u32[]{:S(2)}, u32[]{:S(2)}) async-start(bf16[4,128,2048]{2,1,0:T(8,128)(2,1)} %broadcast_in_dim.72), calls=%async_computation.3 | async-start | bytes 4194304 | tf_op jit(solution)/shard_map/all_to_all | solution.py:62
  206.6 28.5 %collective-permute-start.14 = (bf16[512,2048]{1,0:T(8,128)(2,1)}, bf16[512,2048]{1,0:T(8,128)(2,1)}, u32[]{:S(2)}, u32[]{:S(2)}) collective-permute-start(bf16[512,2048]{1,0:T(8,128)(2,1)} %bitcast.66), channel_id=1, source_target_pairs={{0,1},{1,0},{2,3},{3,2},{4,5},{5,4},{6,7},{7,6},{8,9},{9,8},{10,11... | collective-permute-start | bytes 6291464 | tf_op jit(solution)/shard_map/ppermute | solution.py:58
  226.9 29.0 %collective-permute-start.15 = (bf16[512,2048]{1,0:T(8,128)(2,1)}, bf16[512,2048]{1,0:T(8,128)(2,1)S(1)}, u32[]{:S(2)}, u32[]{:S(2)}) collective-permute-start(bf16[512,2048]{1,0:T(8,128)(2,1)} %bitcast.74), channel_id=1, source_target_pairs={{0,1},{1,0},{2,3},{3,2},{4,5},{5,4},{6,7},{7,6},{8,9},{9,8},{10,11... | collective-permute-start | bytes 6291464 | tf_op jit(solution)/shard_map/ppermute | solution.py:58
  265.7 33.5 %collective-permute-start.16 = (bf16[512,1024]{1,0:T(8,128)(2,1)S(1)}, bf16[512,1024]{1,0:T(8,128)(2,1)S(1)}, u32[]{:S(2)}, u32[]{:S(2)}) collective-permute-start(bf16[512,1024]{1,0:T(8,128)(2,1)S(1)} %shard_map.249), channel_id=1, source_target_pairs={{0,2},{2,0},{4,6},{6,4},{1,3},{3,1},{5,7},{7,5},{8,10},{10,8},{12,... | collective-permute-start | bytes 3145736 | tf_op jit(solution)/shard_map/ppermute | solution.py:252
  309.5 35.9 %all-to-all-start.4 = ((bf16[4,128,2048]{2,1,0:T(8,128)(2,1)}), bf16[4,128,2048]{2,1,0:T(8,128)(2,1)}, u32[]{:S(2)}, u32[]{:S(2)}) async-start(bf16[4,128,2048]{2,1,0:T(8,128)(2,1)} %bitcast.225), calls=%async_computation.4 | async-start | bytes 4194304 | tf_op jit(solution)/shard_map/all_to_all | solution.py:62
  332.1 27.7 %collective-permute-start.19 = (bf16[512,1024]{1,0:T(8,128)(2,1)}, bf16[512,1024]{1,0:T(8,128)(2,1)}, u32[]{:S(2)}, u32[]{:S(2)}) collective-permute-start(bf16[512,1024]{1,0:T(8,128)(2,1)} %get-tuple-element.240.refs_0_), channel_id=1, source_target_pairs={{0,2},{2,0},{4,6},{6,4},{1,3},{3,1},{5,7},{7,5},{8,10},{10,8},{12,... | collective-permute-start | bytes 3145736 | tf_op jit(solution)/shard_map/ppermute | solution.py:252
  364.2 35.8 %all-to-all-start.5 = ((bf16[4,128,2048]{2,1,0:T(8,128)(2,1)}), bf16[4,128,2048]{2,1,0:T(8,128)(2,1)}, u32[]{:S(2)}, u32[]{:S(2)}) async-start(bf16[4,128,2048]{2,1,0:T(8,128)(2,1)} %broadcast_in_dim.75), calls=%async_computation.5 | async-start | bytes 4194304 | tf_op jit(solution)/shard_map/all_to_all | solution.py:62
  408.9 27.4 %collective-permute-start.24 = (bf16[512,1024]{1,0:T(8,128)(2,1)S(1)}, bf16[512,1024]{1,0:T(8,128)(2,1)S(1)}, u32[]{:S(2)}, u32[]{:S(2)}) collective-permute-start(bf16[512,1024]{1,0:T(8,128)(2,1)S(1)} %get-tuple-element.258.refs_0_), channel_id=1, source_target_pairs={{0,2},{2,0},{4,6},{6,4},{1,3},{3,1},{5,7},{7,5},{8,10},{10,8},{12,... | collective-permute-start | bytes 3145736 | tf_op jit(solution)/shard_map/ppermute | solution.py:252
  494.2 28.9 %all-to-all-start.6 = ((bf16[4,128,2048]{2,1,0:T(8,128)(2,1)}), bf16[4,128,2048]{2,1,0:T(8,128)(2,1)}, u32[]{:S(2)}, u32[]{:S(2)}) async-start(bf16[4,128,2048]{2,1,0:T(8,128)(2,1)} %bitcast.226), calls=%async_computation.6 | async-start | bytes 4194304 | tf_op jit(solution)/shard_map/all_to_all | solution.py:62
  557.7 59.4 %all-to-all-start.8 = ((bf16[4,512,1024]{2,1,0:T(8,128)(2,1)}), bf16[4,512,1024]{2,1,0:T(8,128)(2,1)}, u32[]{:S(2)}, u32[]{:S(2)}) async-start(bf16[4,512,1024]{2,1,0:T(8,128)(2,1)} %copy-done.15), calls=%async_computation.8 | async-start | bytes 8388608 | tf_op jit(solution)/shard_map/all_to_all | solution.py:62
  636.1 28.4 %collective-permute-start.40 = (bf16[512,1024]{1,0:T(8,128)(2,1)}, bf16[512,1024]{1,0:T(8,128)(2,1)}, u32[]{:S(2)}, u32[]{:S(2)}) collective-permute-start(bf16[512,1024]{1,0:T(8,128)(2,1)} %get-tuple-element.316.refs_6_), channel_id=1, source_target_pairs={{0,2},{2,0},{4,6},{6,4},{1,3},{3,1},{5,7},{7,5},{8,10},{10,8},{12,... | collective-permute-start | bytes 3145736 | tf_op jit(solution)/shard_map/ppermute | solution.py:252
  667.4 27.4 %collective-permute-start.43 = (bf16[512,1024]{1,0:T(8,128)(2,1)}, bf16[512,1024]{1,0:T(8,128)(2,1)}, u32[]{:S(2)}, u32[]{:S(2)}) collective-permute-start(bf16[512,1024]{1,0:T(8,128)(2,1)} %get-tuple-element.325.refs_4_), channel_id=1, source_target_pairs={{0,2},{2,0},{4,6},{6,4},{1,3},{3,1},{5,7},{7,5},{8,10},{10,8},{12,... | collective-permute-start | bytes 3145736 | tf_op jit(solution)/shard_map/ppermute | solution.py:252
  681.4 51.7 %all-to-all-start.9 = ((bf16[4,512,1024]{2,1,0:T(8,128)(2,1)}), bf16[4,512,1024]{2,1,0:T(8,128)(2,1)}, u32[]{:S(2)}, u32[]{:S(2)}) async-start(bf16[4,512,1024]{2,1,0:T(8,128)(2,1)} %copy-done.16), calls=%async_computation.9 | async-start | bytes 8388608 | tf_op jit(solution)/shard_map/all_to_all | solution.py:62
  700.1 28.5 %collective-permute-start.45 = (bf16[512,1024]{1,0:T(8,128)(2,1)S(1)}, bf16[512,1024]{1,0:T(8,128)(2,1)S(1)}, u32[]{:S(2)}, u32[]{:S(2)}) collective-permute-start(bf16[512,1024]{1,0:T(8,128)(2,1)S(1)} %get-tuple-element.332.refs_6_), channel_id=1, source_target_pairs={{0,2},{2,0},{4,6},{6,4},{1,3},{3,1},{5,7},{7,5},{8,10},{10,8},{12,... | collective-permute-start | bytes 3145736 | tf_op jit(solution)/shard_map/ppermute | solution.py:252
  733.0 35.3 %collective-permute-start.50 = (bf16[4,512,1024]{2,1,0:T(8,128)(2,1)}, bf16[4,512,1024]{2,1,0:T(8,128)(2,1)}, u32[]{:S(2)}, u32[]{:S(2)}) collective-permute-start(bf16[4,512,1024]{2,1,0:T(8,128)(2,1)} %all-to-all-done.9.mine_ref), channel_id=1, source_target_pairs={{0,1},{1,0},{2,3},{3,2},{4,5},{5,4},{6,7},{7,6},{8,9},{9,8},{10,11... | collective-permute-start | bytes 12582920 | tf_op jit(solution)/shard_map/ppermute | solution.py:58
  734.6 29.6 %all-to-all-start.10 = ((bf16[4,128,2048]{2,1,0:T(8,128)(2,1)}), bf16[4,128,2048]{2,1,0:T(8,128)(2,1)}, u32[]{:S(2)}, u32[]{:S(2)}) async-start(bf16[4,128,2048]{2,1,0:T(8,128)(2,1)} %bitcast.224), calls=%async_computation.10 | async-start | bytes 4194304 | tf_op jit(solution)/shard_map/all_to_all | solution.py:62
  745.8 34.3 %collective-permute-start.48 = (bf16[512,1024]{1,0:T(8,128)(2,1)}, bf16[512,1024]{1,0:T(8,128)(2,1)}, u32[]{:S(2)}, u32[]{:S(2)}) collective-permute-start(bf16[512,1024]{1,0:T(8,128)(2,1)} %get-tuple-element.341.refs_0_), channel_id=1, source_target_pairs={{0,2},{2,0},{4,6},{6,4},{1,3},{3,1},{5,7},{7,5},{8,10},{10,8},{12,... | collective-permute-start | bytes 3145736 | tf_op jit(solution)/shard_map/ppermute | solution.py:252
  747.0 33.1 %collective-permute-start.49 = (bf16[512,1024]{1,0:T(8,128)(2,1)}, bf16[512,1024]{1,0:T(8,128)(2,1)}, u32[]{:S(2)}, u32[]{:S(2)}) collective-permute-start(bf16[512,1024]{1,0:T(8,128)(2,1)} %get-tuple-element.342.refs_2_), channel_id=1, source_target_pairs={{2,4},{4,2},{3,5},{5,3},{10,12},{12,10},{11,13},{13,11},{18,20},{2... | collective-permute-start | bytes 3145736 | tf_op jit(solution)/shard_map/ppermute | solution.py:250
  783.8 25.9 %collective-permute-start.51 = (bf16[512,1024]{1,0:T(8,128)(2,1)}, bf16[512,1024]{1,0:T(8,128)(2,1)S(1)}, u32[]{:S(2)}, u32[]{:S(2)}) collective-permute-start(bf16[512,1024]{1,0:T(8,128)(2,1)} %get-tuple-element.351.refs_2_), channel_id=1, source_target_pairs={{0,2},{2,0},{4,6},{6,4},{1,3},{3,1},{5,7},{7,5},{8,10},{10,8},{12,... | collective-permute-start | bytes 3145736 | tf_op jit(solution)/shard_map/ppermute | solution.py:252
  814.6 29.6 %collective-permute-start.55 = (bf16[512,1024]{1,0:T(8,128)(2,1)S(1)}, bf16[512,1024]{1,0:T(8,128)(2,1)}, u32[]{:S(2)}, u32[]{:S(2)}) collective-permute-start(bf16[512,1024]{1,0:T(8,128)(2,1)S(1)} %shard_map.273.refs_0_), channel_id=1, source_target_pairs={{0,2},{2,0},{4,6},{6,4},{1,3},{3,1},{5,7},{7,5},{8,10},{10,8},{12,... | collective-permute-start | bytes 3145736 | tf_op jit(solution)/shard_map/ppermute | solution.py:252
  (146 other events, 1708.0 us)

commit v5 on v4

--- a/solution.py
+++ b/solution.py
@@ -292,7 +292,7 @@
 
     def combine(self, stream, came, moved, entering):
         rows, wide = self.shape
-        steps = 4
+        steps = 2
         tile = rows // steps
         last, across = stream.get("enter"), stream.get("across")
 

time: 872 us -> 862 us (0.989)
  starting transfers between devices: 167 us -> 157 us
    ppermute x17, starting transfers between devices: 62.4 us -> 53.1 us  [slot(): lax.ppermute(send, 'rest', [(0, 1), (1, 0), (2, 3), (3, 2)])]
  transfers between devices with their start and end apart: 68 -> 68, of which waited for: 30 -> 29; matrix products, arithmetic and copies ran while one was open for 26% -> 27% of each run, Pallas kernels for 11% -> 11%
where the time goes in v5:
time: 862 us; the launch traced here: 848 us
  waiting for transfers between devices  265 us (31%)
  starting transfers between devices  157 us (18%)
  local copies, waits for them, and re-layouts  143 us (17%)
  Pallas kernels  116 us (13%)
  matrix products  98 us (11%)
  other arithmetic  66.3 us (8%)
    ppermute x17, waiting for transfers between devices, slot(): lax.ppermute(send, 'rest', [(0, 1), (1, 0), (2, 3), (3, 2)])  157 us
    all_to_all x11, waiting for transfers between devices, exchange(): return lax.all_to_all(blocks, 'group', 0, 0, tiled=True)  57.3 us
    unnamed x227, local copies, waits for them, and re-layouts  54.2 us
    ppermute x17, starting transfers between devices, slot(): lax.ppermute(send, 'rest', [(0, 1), (1, 0), (2, 3), (3, 2)])  53.1 us
    ppermute x25, waiting for transfers between devices, step_to(): return lax.ppermute(value, axis, [(i, i ^ step) for i in range(size)])  51 us
    all_to_all x11, starting transfers between devices, exchange(): return lax.all_to_all(blocks, 'group', 0, 0, tiled=True)  50.5 us
    pallas_call x5, Pallas kernels, place(): pl.pallas_call(kernel, grid_spec=pltpu.PrefetchScalarGridSpec(num_scalar_...  46.9 us
    dot_general x5, matrix products, contract_last(): lax.dot_general(left, right, (((1,), (1,)), ((), ())), preferred_element_...  35.6 us
  transfers between devices with their start and end apart: 68, of which 29 were waited for; matrix products, arithmetic and copies ran while one was open for 27% of the time, Pallas kernels for 11%

profile of v5, /device:TPU:1, one launch (start us, length us, event | category | flops | bytes accessed | tf_op | source)
XLA Modules:
  0.0 848.1 jit_solution(14369181852281672052)
XLA Ops:
  47.0 7.8 collective-permute-done.2
  70.5 9.8 %shard_map.248 = (bf16[1024,256]{1,0:T(8,128)(2,1)S(1)}, bf16[1024,384]{1,0:T(8,128)(2,1)S(1)}, f32[1024,128]{1,0:T(8,128)S(1)}) custom-call(f32[1024,384]{1,0:T(8,128)S(1)} %fusion.39.qkv_ref, f32[1024,128]{1,0:T(8,128)S(1)} %copy-done.21, f32[1024,128]{1,0:T(8,128)S(1)} %get-tuple-element.197.sin_ref, s32[2,512,2]{2,1,0:T(8,128)S(1)} %copy.63.column_ref, ...), custom_call_target="tpu_custom_call" | custom-call | bytes 1 | tf_op jit(solution)/shard_map/pallas_call | solution.py:195
  97.5 8.9 %collective-permute-done.6 = bf16[384,1024]{1,0:T(8,128)(2,1)} collective-permute-done((bf16[384,1024]{1,0:T(8,128)(2,1)S(1)}, bf16[384,1024]{1,0:T(8,128)(2,1)}, u32[]{:S(2)}, u32[]{:S(2)}) %collective-permute-start.6) | collective-permute-done | bytes 786464 | tf_op jit(solution)/shard_map/ppermute | solution.py:58
  106.4 16.8 %collective-permute-done.8 = bf16[384,1024]{1,0:T(8,128)(2,1)} collective-permute-done((bf16[384,1024]{1,0:T(8,128)(2,1)S(1)}, bf16[384,1024]{1,0:T(8,128)(2,1)}, u32[]{:S(2)}, u32[]{:S(2)}) %collective-permute-start.8) | collective-permute-done | bytes 786464 | tf_op jit(solution)/shard_map/ppermute | solution.py:58
  178.3 8.3 collective-permute-done.12
  208.1 18.8 %all-to-all-done.3 = bf16[4,128,2048]{2,1,0:T(8,128)(2,1)} async-done(((bf16[4,128,2048]{2,1,0:T(8,128)(2,1)}), bf16[4,128,2048]{2,1,0:T(8,128)(2,1)}, u32[]{:S(2)}, u32[]{:S(2)}) %all-to-all-start.3) | async-done | bytes 2097184 | tf_op jit(solution)/shard_map/all_to_all | solution.py:62
  236.9 7.8 fusion.45
  244.7 11.2 %multiply_convert_fusion.2 = (bf16[1024,1024]{1,0:T(8,128)(2,1)S(1)}, f32[1024,1024]{1,0:T(8,128)}, f32[1024,1024]{1,0:T(8,128)}) fusion(f32[1024,1024]{1,0:T(8,128)S(1)} %fusion.45, pred[]{:T(512)S(6)} %eq.74, bf16[1024,2048]{1,0:T(8,128)(2,1)S(1)} %constant_dynamic-update-slice_fusion.6, bf16[2048,1024]{1,0:T(8,128)(2,1)} %bitcast.72), kind=kOutput, calls=%fused_computation.22 | convolution fusion | flops 4303355904 | bytes 23068672 | tf_op jit(solution)/shard_map/dot_general | solution.py:32
  267.2 10.6 %multiply_convert_fusion = (bf16[1024,1024]{1,0:T(8,128)(2,1)S(1)}, bf16[1024,1024]{1,0:T(8,128)(2,1)}) fusion(f32[1024,1024]{1,0:T(8,128)} %get-tuple-element.433, f32[1024,1024]{1,0:T(8,128)} %get-tuple-element.496, f32[1024,1024]{1,0:T(8,128)} %copy-done.107, pred[]{:T(512)S(6)} %eq.74, bf16[1024,2048]{1,0:T(8,128)(2,1)S(1)} %pad_maximum_fusion.1, ...), kind=kOutput, calls=%fused_computation.20 | convolution fusion | flops 4309647360 | bytes 25165828 | tf_op jit(solution)/shard_map/dot_general | solution.py:36
  277.8 11.0 %fusion.9 = f32[1024,2048]{1,0:T(8,128)} fusion(bf16[2048,1024]{1,0:T(8,128)(2,1)} %bitcast.72, bf16[1024,1024]{1,0:T(8,128)(2,1)S(1)} %get-tuple-element.243, bf16[1024,1024]{1,0:T(8,128)(2,1)} %get-tuple-element.238, pred[]{:T(512)S(6)} %eq.74), kind=kOutput, calls=%fused_computation.38 | convolution fusion | flops 4296015872 | bytes 16777216 | tf_op jit(solution)/shard_map/dot_general | solution.py:36
  288.8 10.3 %convolution_add_fusion = f32[1024,2048]{1,0:T(8,128)} fusion(f32[1024,2048]{1,0:T(8,128)} %fusion.9, bf16[2048,1024]{1,0:T(8,128)(2,1)} %bitcast.71, bf16[1024,1024]{1,0:T(8,128)(2,1)S(1)} %copy-done.106, bf16[1024,1024]{1,0:T(8,128)(2,1)S(1)} %get-tuple-element.243, pred[]{:T(512)S(6)} %eq.74), kind=kOutput, calls=%fused_computation.25 | convolution fusion | flops 4298113024 | bytes 25165824 | tf_op jit(solution)/shard_map/dot_general | solution.py:36
  313.7 7.6 convolution_convert_fusion.1.refs_4_.refs_1_
  321.4 7.3 collective-permute-done.17.refs_0_
  345.9 12.4 %collective-permute-done.19.refs_0_.refs_1_ = bf16[512,1024]{1,0:T(8,128)(2,1)} collective-permute-done((bf16[512,1024]{1,0:T(8,128)(2,1)}, bf16[512,1024]{1,0:T(8,128)(2,1)}, u32[]{:S(2)}, u32[]{:S(2)}) %collective-permute-start.19) | collective-permute-done | bytes 1048608 | tf_op jit(solution)/shard_map/ppermute | solution.py:252
  377.3 18.6 %collective-permute-done.22.refs_0_.refs_3_ = bf16[512,1024]{1,0:T(8,128)(2,1)S(1)} collective-permute-done((bf16[512,1024]{1,0:T(8,128)(2,1)S(1)}, bf16[512,1024]{1,0:T(8,128)(2,1)S(1)}, u32[]{:S(2)}, u32[]{:S(2)}) %collective-permute-start.22) | collective-permute-done | bytes 1048608 | tf_op jit(solution)/shard_map/ppermute | solution.py:252
  417.5 16.6 %collective-permute-done.24.refs_0_.refs_1_ = bf16[512,1024]{1,0:T(8,128)(2,1)S(1)} collective-permute-done((bf16[512,1024]{1,0:T(8,128)(2,1)S(1)}, bf16[512,1024]{1,0:T(8,128)(2,1)S(1)}, u32[]{:S(2)}, u32[]{:S(2)}) %collective-permute-start.24) | collective-permute-done | bytes 1048608 | tf_op jit(solution)/shard_map/ppermute | solution.py:252
  438.6 11.8 %shard_map.255 = bf16[1024,384]{1,0:T(8,128)(2,1)S(1)} custom-call(bf16[1024,384]{1,0:T(8,128)(2,1)S(1)} %copy-done.64, f32[1024,128]{1,0:T(8,128)S(1)} %copy-done.68, bf16[1024,256]{1,0:T(8,128)(2,1)S(1)} %convolution_convert_fusion.5.grad_ref, f32[1024,128]{1,0:T(8,128)S(1)} %copy-done.22, f32[1024,128]{1,0:T(8,128)S(1)} %get-tuple-element.197.sin_ref, ...), custom_call_target="tpu_custom_call" | custom-call | bytes 1 | tf_op jit(solution)/shard_map/pallas_call | solution.py:195
  450.4 10.2 %collective-permute-done.27.refs_0_.refs_3_ = bf16[512,1024]{1,0:T(8,128)(2,1)S(1)} collective-permute-done((bf16[512,1024]{1,0:T(8,128)(2,1)S(1)}, bf16[512,1024]{1,0:T(8,128)(2,1)S(1)}, u32[]{:S(2)}, u32[]{:S(2)}) %collective-permute-start.27) | collective-permute-done | bytes 1048608 | tf_op jit(solution)/shard_map/ppermute | solution.py:252
  478.0 12.8 %collective-permute-done.29.refs_0_.refs_5_ = bf16[512,1024]{1,0:T(8,128)(2,1)S(1)} collective-permute-done((bf16[512,1024]{1,0:T(8,128)(2,1)S(1)}, bf16[512,1024]{1,0:T(8,128)(2,1)S(1)}, u32[]{:S(2)}, u32[]{:S(2)}) %collective-permute-start.29) | collective-permute-done | bytes 1048608 | tf_op jit(solution)/shard_map/ppermute | solution.py:252
  507.2 13.5 %all-to-all-done.6 = bf16[4,128,2048]{2,1,0:T(8,128)(2,1)} async-done(((bf16[4,128,2048]{2,1,0:T(8,128)(2,1)}), bf16[4,128,2048]{2,1,0:T(8,128)(2,1)}, u32[]{:S(2)}, u32[]{:S(2)}) %all-to-all-start.6) | async-done | bytes 2097184 | tf_op jit(solution)/shard_map/all_to_all | solution.py:62
  577.5 12.3 %collective-permute-done.36.refs_0_.refs_3_ = bf16[512,1024]{1,0:T(8,128)(2,1)} collective-permute-done((bf16[512,1024]{1,0:T(8,128)(2,1)}, bf16[512,1024]{1,0:T(8,128)(2,1)}, u32[]{:S(2)}, u32[]{:S(2)}) %collective-permute-start.36) | collective-permute-done | bytes 1048608 | tf_op jit(solution)/shard_map/ppermute | solution.py:252
  602.2 8.9 %fusion.5 = f32[1024,2048]{1,0:T(8,128)} fusion(bf16[1024,1024]{1,0:T(8,128)(2,1)S(1)} %copy-done.103, bf16[2048,2048]{1,0:T(8,128)(2,1)} %param.27, s32[]{:T(128)S(6)} %select_n.289), kind=kOutput, calls=%fused_computation.29 | convolution fusion | flops 4294967296 | bytes 14680068 | tf_op jit(solution)/shard_map/dot_general | solution.py:32
  611.1 8.0 collective-permute-done.38.refs_0_.refs_5_
  635.3 11.9 %shard_map.263 = f32[512,8192]{1,0:T(8,128)} custom-call(s32[40]{0:T(128)S(1)} %reshape.339.table_ref, bf16[4,512,1024]{2,1,0:T(8,128)(2,1)} %all-to-all-done.8.mine_ref, bf16[4,512,1024]{2,1,0:T(8,128)(2,1)} %collective-permute-done.42.other_ref), custom_call_target="tpu_custom_call" | custom-call | bytes 25165824 | tf_op jit(solution)/shard_map/pallas_call | solution.py:398
  647.2 10.2 %collective-permute-done.40.refs_0_.refs_7_ = bf16[512,1024]{1,0:T(8,128)(2,1)} collective-permute-done((bf16[512,1024]{1,0:T(8,128)(2,1)}, bf16[512,1024]{1,0:T(8,128)(2,1)}, u32[]{:S(2)}, u32[]{:S(2)}) %collective-permute-start.40) | collective-permute-done | bytes 1048608 | tf_op jit(solution)/shard_map/ppermute | solution.py:252
  678.4 8.3 collective-permute-done.43.refs_0_.refs_5_
  701.2 18.6 %collective-permute-done.45.refs_0_.refs_7_ = bf16[512,1024]{1,0:T(8,128)(2,1)S(1)} collective-permute-done((bf16[512,1024]{1,0:T(8,128)(2,1)S(1)}, bf16[512,1024]{1,0:T(8,128)(2,1)S(1)}, u32[]{:S(2)}, u32[]{:S(2)}) %collective-permute-start.45) | collective-permute-done | bytes 1048608 | tf_op jit(solution)/shard_map/ppermute | solution.py:252
  746.6 9.7 %all-to-all-done.10 = bf16[4,128,2048]{2,1,0:T(8,128)(2,1)} async-done(((bf16[4,128,2048]{2,1,0:T(8,128)(2,1)}), bf16[4,128,2048]{2,1,0:T(8,128)(2,1)}, u32[]{:S(2)}, u32[]{:S(2)}) %all-to-all-start.10) | async-done | bytes 2097184 | tf_op jit(solution)/shard_map/all_to_all | solution.py:62
  760.5 11.6 %shard_map.268 = f32[512,8192]{1,0:T(8,128)} custom-call(s32[40]{0:T(128)S(1)} %reshape.339.table_ref, bf16[4,512,1024]{2,1,0:T(8,128)(2,1)} %all-to-all-done.9.mine_ref, bf16[4,512,1024]{2,1,0:T(8,128)(2,1)} %collective-permute-done.50.other_ref), custom_call_target="tpu_custom_call" | custom-call | bytes 25165824 | tf_op jit(solution)/shard_map/pallas_call | solution.py:398
  780.2 11.6 %shard_map.271 = f32[2048,2048]{1,0:T(8,128)} custom-call(s32[40]{0:T(128)S(1)} %reshape.342.table_ref, bf16[4,512,1024]{2,1,0:T(8,128)(2,1)} %shard_map.270.mine_ref, bf16[4,512,1024]{2,1,0:T(8,128)(2,1)} %collective-permute-done.53.other_ref), custom_call_target="tpu_custom_call" | custom-call | bytes 25165824 | tf_op jit(solution)/shard_map/pallas_call | solution.py:398
  791.8 8.9 %collective-permute-done.51.refs_3_ = bf16[512,1024]{1,0:T(8,128)(2,1)S(1)} collective-permute-done((bf16[512,1024]{1,0:T(8,128)(2,1)}, bf16[512,1024]{1,0:T(8,128)(2,1)S(1)}, u32[]{:S(2)}, u32[]{:S(2)}) %collective-permute-start.51) | collective-permute-done | bytes 1048608 | tf_op jit(solution)/shard_map/ppermute | solution.py:252
  825.9 8.7 %collective-permute-done.55.refs_1_ = bf16[512,1024]{1,0:T(8,128)(2,1)} collective-permute-done((bf16[512,1024]{1,0:T(8,128)(2,1)S(1)}, bf16[512,1024]{1,0:T(8,128)(2,1)}, u32[]{:S(2)}, u32[]{:S(2)}) %collective-permute-start.55) | collective-permute-done | bytes 1048608 | tf_op jit(solution)/shard_map/ppermute | solution.py:252
  (501 shorter events, 485.0 us)
Async XLA Ops:
  4.3 39.4 %all-to-all-start = ((bf16[4,144,2048]{2,1,0:T(8,128)(2,1)}), bf16[4,144,2048]{2,1,0:T(8,128)(2,1)}, u32[]{:S(2)}, u32[]{:S(2)}) async-start(bf16[4,144,2048]{2,1,0:T(8,128)(2,1)} %broadcast_in_dim.57), calls=%async_computation | async-start | bytes 4718592 | tf_op jit(solution)/shard_map/all_to_all | solution.py:62
  14.7 32.3 %collective-permute-start = (bf16[512,384]{1,0:T(8,128)(2,1)}, bf16[512,384]{1,0:T(8,128)(2,1)S(1)}, u32[]{:S(2)}, u32[]{:S(2)}) collective-permute-start(bf16[512,384]{1,0:T(8,128)(2,1)} %get-tuple-element.470), channel_id=1, source_target_pairs={{0,8},{8,0},{16,24},{24,16},{1,9},{9,1},{17,25},{25,17},{2,10},{10... | collective-permute-start | bytes 1179656 | tf_op jit(solution)/shard_map/ppermute | solution.py:58
  16.7 30.3 %collective-permute-start.1 = (bf16[512,384]{1,0:T(8,128)(2,1)}, bf16[512,384]{1,0:T(8,128)(2,1)S(1)}, u32[]{:S(2)}, u32[]{:S(2)}) collective-permute-start(bf16[512,384]{1,0:T(8,128)(2,1)} %get-tuple-element.469), channel_id=1, source_target_pairs={{0,16},{8,24},{16,0},{24,8},{1,17},{9,25},{17,1},{25,9},{2,18},{10... | collective-permute-start | bytes 1179656 | tf_op jit(solution)/shard_map/ppermute | solution.py:58
  18.0 36.8 %collective-permute-start.2 = (bf16[512,384]{1,0:T(8,128)(2,1)}, bf16[512,384]{1,0:T(8,128)(2,1)}, u32[]{:S(2)}, u32[]{:S(2)}) collective-permute-start(bf16[512,384]{1,0:T(8,128)(2,1)} %get-tuple-element.468), channel_id=1, source_target_pairs={{0,24},{8,16},{16,8},{24,0},{1,25},{9,17},{17,9},{25,1},{2,26},{10... | collective-permute-start | bytes 1179656 | tf_op jit(solution)/shard_map/ppermute | solution.py:58
  88.2 35.0 %collective-permute-start.8 = (bf16[384,1024]{1,0:T(8,128)(2,1)S(1)}, bf16[384,1024]{1,0:T(8,128)(2,1)}, u32[]{:S(2)}, u32[]{:S(2)}) collective-permute-start(bf16[384,1024]{1,0:T(8,128)(2,1)S(1)} %get-tuple-element.450), channel_id=1, source_target_pairs={{0,24},{8,16},{16,8},{24,0},{1,25},{9,17},{17,9},{25,1},{2,26},{10... | collective-permute-start | bytes 2359304 | tf_op jit(solution)/shard_map/ppermute | solution.py:58
  123.2 28.9 %all-to-all-start.1 = ((bf16[4,128,2048]{2,1,0:T(8,128)(2,1)}), bf16[4,128,2048]{2,1,0:T(8,128)(2,1)}, u32[]{:S(2)}, u32[]{:S(2)}) async-start(bf16[4,128,2048]{2,1,0:T(8,128)(2,1)} %bitcast.223), calls=%async_computation.1 | async-start | bytes 4194304 | tf_op jit(solution)/shard_map/all_to_all | solution.py:62
  129.8 26.9 %collective-permute-start.9 = (bf16[128,1024]{1,0:T(8,128)(2,1)}, bf16[128,1024]{1,0:T(8,128)(2,1)S(1)}, u32[]{:S(2)}, u32[]{:S(2)}) collective-permute-start(bf16[128,1024]{1,0:T(8,128)(2,1)} %get-tuple-element.475), channel_id=1, source_target_pairs={{0,8},{8,0},{16,24},{24,16},{1,9},{9,1},{17,25},{25,17},{2,10},{10... | collective-permute-start | bytes 786440 | tf_op jit(solution)/shard_map/ppermute | solution.py:58
  131.2 26.6 %collective-permute-start.10 = (bf16[128,1024]{1,0:T(8,128)(2,1)}, bf16[128,1024]{1,0:T(8,128)(2,1)}, u32[]{:S(2)}, u32[]{:S(2)}) collective-permute-start(bf16[128,1024]{1,0:T(8,128)(2,1)} %get-tuple-element.474), channel_id=1, source_target_pairs={{0,16},{8,24},{16,0},{24,8},{1,17},{9,25},{17,1},{25,9},{2,18},{10... | collective-permute-start | bytes 786440 | tf_op jit(solution)/shard_map/ppermute | solution.py:58
  132.4 30.9 %collective-permute-start.11 = (bf16[128,1024]{1,0:T(8,128)(2,1)}, bf16[128,1024]{1,0:T(8,128)(2,1)}, u32[]{:S(2)}, u32[]{:S(2)}) collective-permute-start(bf16[128,1024]{1,0:T(8,128)(2,1)} %get-tuple-element.473), channel_id=1, source_target_pairs={{0,24},{8,16},{16,8},{24,0},{1,25},{9,17},{17,9},{25,1},{2,26},{10... | collective-permute-start | bytes 786440 | tf_op jit(solution)/shard_map/ppermute | solution.py:58
  135.8 50.8 %collective-permute-start.12 = (bf16[3,384,1024]{2,1,0:T(8,128)(2,1)}, bf16[3,384,1024]{2,1,0:T(8,128)(2,1)}, u32[]{:S(2)}, u32[]{:S(2)}) collective-permute-start(bf16[3,384,1024]{2,1,0:T(8,128)(2,1)} %pad_maximum_fusion.2), channel_id=1, source_target_pairs={{0,2},{2,0},{4,6},{6,4},{1,3},{3,1},{5,7},{7,5},{8,10},{10,8},{12,... | collective-permute-start | bytes 7077896 | tf_op jit(solution)/shard_map/ppermute | solution.py:58
  166.1 28.9 %all-to-all-start.2 = ((bf16[4,128,2048]{2,1,0:T(8,128)(2,1)}), bf16[4,128,2048]{2,1,0:T(8,128)(2,1)}, u32[]{:S(2)}, u32[]{:S(2)}) async-start(bf16[4,128,2048]{2,1,0:T(8,128)(2,1)} %broadcast_in_dim.71), calls=%async_computation.2 | async-start | bytes 4194304 | tf_op jit(solution)/shard_map/all_to_all | solution.py:62
  172.6 34.0 %collective-permute-start.13 = (bf16[3,128,1024]{2,1,0:T(8,128)(2,1)}, bf16[3,128,1024]{2,1,0:T(8,128)(2,1)}, u32[]{:S(2)}, u32[]{:S(2)}) collective-permute-start(bf16[3,128,1024]{2,1,0:T(8,128)(2,1)} %pad_maximum_fusion.5), channel_id=1, source_target_pairs={{0,2},{2,0},{4,6},{6,4},{1,3},{3,1},{5,7},{7,5},{8,10},{10,8},{12,... | collective-permute-start | bytes 2359304 | tf_op jit(solution)/shard_map/ppermute | solution.py:58
  197.6 29.3 %all-to-all-start.3 = ((bf16[4,128,2048]{2,1,0:T(8,128)(2,1)}), bf16[4,128,2048]{2,1,0:T(8,128)(2,1)}, u32[]{:S(2)}, u32[]{:S(2)}) async-start(bf16[4,128,2048]{2,1,0:T(8,128)(2,1)} %broadcast_in_dim.72), calls=%async_computation.3 | async-start | bytes 4194304 | tf_op jit(solution)/shard_map/all_to_all | solution.py:62
  206.6 28.5 %collective-permute-start.14 = (bf16[512,2048]{1,0:T(8,128)(2,1)}, bf16[512,2048]{1,0:T(8,128)(2,1)}, u32[]{:S(2)}, u32[]{:S(2)}) collective-permute-start(bf16[512,2048]{1,0:T(8,128)(2,1)} %bitcast.66), channel_id=1, source_target_pairs={{0,1},{1,0},{2,3},{3,2},{4,5},{5,4},{6,7},{7,6},{8,9},{9,8},{10,11... | collective-permute-start | bytes 6291464 | tf_op jit(solution)/shard_map/ppermute | solution.py:58
  226.9 29.0 %collective-permute-start.15 = (bf16[512,2048]{1,0:T(8,128)(2,1)}, bf16[512,2048]{1,0:T(8,128)(2,1)S(1)}, u32[]{:S(2)}, u32[]{:S(2)}) collective-permute-start(bf16[512,2048]{1,0:T(8,128)(2,1)} %bitcast.74), channel_id=1, source_target_pairs={{0,1},{1,0},{2,3},{3,2},{4,5},{5,4},{6,7},{7,6},{8,9},{9,8},{10,11... | collective-permute-start | bytes 6291464 | tf_op jit(solution)/shard_map/ppermute | solution.py:58
  265.6 33.5 %collective-permute-start.16 = (bf16[512,1024]{1,0:T(8,128)(2,1)S(1)}, bf16[512,1024]{1,0:T(8,128)(2,1)S(1)}, u32[]{:S(2)}, u32[]{:S(2)}) collective-permute-start(bf16[512,1024]{1,0:T(8,128)(2,1)S(1)} %shard_map.249), channel_id=1, source_target_pairs={{0,2},{2,0},{4,6},{6,4},{1,3},{3,1},{5,7},{7,5},{8,10},{10,8},{12,... | collective-permute-start | bytes 3145736 | tf_op jit(solution)/shard_map/ppermute | solution.py:252
  309.1 34.7 %all-to-all-start.4 = ((bf16[4,128,2048]{2,1,0:T(8,128)(2,1)}), bf16[4,128,2048]{2,1,0:T(8,128)(2,1)}, u32[]{:S(2)}, u32[]{:S(2)}) async-start(bf16[4,128,2048]{2,1,0:T(8,128)(2,1)} %bitcast.225), calls=%async_computation.4 | async-start | bytes 4194304 | tf_op jit(solution)/shard_map/all_to_all | solution.py:62
  331.4 26.9 %collective-permute-start.19 = (bf16[512,1024]{1,0:T(8,128)(2,1)}, bf16[512,1024]{1,0:T(8,128)(2,1)}, u32[]{:S(2)}, u32[]{:S(2)}) collective-permute-start(bf16[512,1024]{1,0:T(8,128)(2,1)} %get-tuple-element.240.refs_0_), channel_id=1, source_target_pairs={{0,2},{2,0},{4,6},{6,4},{1,3},{3,1},{5,7},{7,5},{8,10},{10,8},{12,... | collective-permute-start | bytes 3145736 | tf_op jit(solution)/shard_map/ppermute | solution.py:252
  362.7 35.1 %all-to-all-start.5 = ((bf16[4,128,2048]{2,1,0:T(8,128)(2,1)}), bf16[4,128,2048]{2,1,0:T(8,128)(2,1)}, u32[]{:S(2)}, u32[]{:S(2)}) async-start(bf16[4,128,2048]{2,1,0:T(8,128)(2,1)} %broadcast_in_dim.75), calls=%async_computation.5 | async-start | bytes 4194304 | tf_op jit(solution)/shard_map/all_to_all | solution.py:62
  406.7 27.4 %collective-permute-start.24 = (bf16[512,1024]{1,0:T(8,128)(2,1)S(1)}, bf16[512,1024]{1,0:T(8,128)(2,1)S(1)}, u32[]{:S(2)}, u32[]{:S(2)}) collective-permute-start(bf16[512,1024]{1,0:T(8,128)(2,1)S(1)} %get-tuple-element.258.refs_0_), channel_id=1, source_target_pairs={{0,2},{2,0},{4,6},{6,4},{1,3},{3,1},{5,7},{7,5},{8,10},{10,8},{12,... | collective-permute-start | bytes 3145736 | tf_op jit(solution)/shard_map/ppermute | solution.py:252
  435.1 25.5 %collective-permute-start.27 = (bf16[512,1024]{1,0:T(8,128)(2,1)S(1)}, bf16[512,1024]{1,0:T(8,128)(2,1)S(1)}, u32[]{:S(2)}, u32[]{:S(2)}) collective-permute-start(bf16[512,1024]{1,0:T(8,128)(2,1)S(1)} %get-tuple-element.266.refs_2_), channel_id=1, source_target_pairs={{0,2},{2,0},{4,6},{6,4},{1,3},{3,1},{5,7},{7,5},{8,10},{10,8},{12,... | collective-permute-start | bytes 3145736 | tf_op jit(solution)/shard_map/ppermute | solution.py:252
  491.8 28.9 %all-to-all-start.6 = ((bf16[4,128,2048]{2,1,0:T(8,128)(2,1)}), bf16[4,128,2048]{2,1,0:T(8,128)(2,1)}, u32[]{:S(2)}, u32[]{:S(2)}) async-start(bf16[4,128,2048]{2,1,0:T(8,128)(2,1)} %bitcast.226), calls=%async_computation.6 | async-start | bytes 4194304 | tf_op jit(solution)/shard_map/all_to_all | solution.py:62
  554.9 56.2 %all-to-all-start.8 = ((bf16[4,512,1024]{2,1,0:T(8,128)(2,1)}), bf16[4,512,1024]{2,1,0:T(8,128)(2,1)}, u32[]{:S(2)}, u32[]{:S(2)}) async-start(bf16[4,512,1024]{2,1,0:T(8,128)(2,1)} %copy-done.15), calls=%async_computation.8 | async-start | bytes 8388608 | tf_op jit(solution)/shard_map/all_to_all | solution.py:62
  629.8 27.6 %collective-permute-start.40 = (bf16[512,1024]{1,0:T(8,128)(2,1)}, bf16[512,1024]{1,0:T(8,128)(2,1)}, u32[]{:S(2)}, u32[]{:S(2)}) collective-permute-start(bf16[512,1024]{1,0:T(8,128)(2,1)} %get-tuple-element.316.refs_6_), channel_id=1, source_target_pairs={{0,2},{2,0},{4,6},{6,4},{1,3},{3,1},{5,7},{7,5},{8,10},{10,8},{12,... | collective-permute-start | bytes 3145736 | tf_op jit(solution)/shard_map/ppermute | solution.py:252
  660.1 26.6 %collective-permute-start.43 = (bf16[512,1024]{1,0:T(8,128)(2,1)}, bf16[512,1024]{1,0:T(8,128)(2,1)}, u32[]{:S(2)}, u32[]{:S(2)}) collective-permute-start(bf16[512,1024]{1,0:T(8,128)(2,1)} %get-tuple-element.325.refs_4_), channel_id=1, source_target_pairs={{0,2},{2,0},{4,6},{6,4},{1,3},{3,1},{5,7},{7,5},{8,10},{10,8},{12,... | collective-permute-start | bytes 3145736 | tf_op jit(solution)/shard_map/ppermute | solution.py:252
  673.5 51.7 %all-to-all-start.9 = ((bf16[4,512,1024]{2,1,0:T(8,128)(2,1)}), bf16[4,512,1024]{2,1,0:T(8,128)(2,1)}, u32[]{:S(2)}, u32[]{:S(2)}) async-start(bf16[4,512,1024]{2,1,0:T(8,128)(2,1)} %copy-done.16), calls=%async_computation.9 | async-start | bytes 8388608 | tf_op jit(solution)/shard_map/all_to_all | solution.py:62
  692.2 27.6 %collective-permute-start.45 = (bf16[512,1024]{1,0:T(8,128)(2,1)S(1)}, bf16[512,1024]{1,0:T(8,128)(2,1)S(1)}, u32[]{:S(2)}, u32[]{:S(2)}) collective-permute-start(bf16[512,1024]{1,0:T(8,128)(2,1)S(1)} %get-tuple-element.332.refs_6_), channel_id=1, source_target_pairs={{0,2},{2,0},{4,6},{6,4},{1,3},{3,1},{5,7},{7,5},{8,10},{10,8},{12,... | collective-permute-start | bytes 3145736 | tf_op jit(solution)/shard_map/ppermute | solution.py:252
  725.2 35.3 %collective-permute-start.50 = (bf16[4,512,1024]{2,1,0:T(8,128)(2,1)}, bf16[4,512,1024]{2,1,0:T(8,128)(2,1)}, u32[]{:S(2)}, u32[]{:S(2)}) collective-permute-start(bf16[4,512,1024]{2,1,0:T(8,128)(2,1)} %all-to-all-done.9.mine_ref), channel_id=1, source_target_pairs={{0,1},{1,0},{2,3},{3,2},{4,5},{5,4},{6,7},{7,6},{8,9},{9,8},{10,11... | collective-permute-start | bytes 12582920 | tf_op jit(solution)/shard_map/ppermute | solution.py:58
  726.7 29.6 %all-to-all-start.10 = ((bf16[4,128,2048]{2,1,0:T(8,128)(2,1)}), bf16[4,128,2048]{2,1,0:T(8,128)(2,1)}, u32[]{:S(2)}, u32[]{:S(2)}) async-start(bf16[4,128,2048]{2,1,0:T(8,128)(2,1)} %bitcast.224), calls=%async_computation.10 | async-start | bytes 4194304 | tf_op jit(solution)/shard_map/all_to_all | solution.py:62
  737.5 34.7 %collective-permute-start.48 = (bf16[512,1024]{1,0:T(8,128)(2,1)}, bf16[512,1024]{1,0:T(8,128)(2,1)}, u32[]{:S(2)}, u32[]{:S(2)}) collective-permute-start(bf16[512,1024]{1,0:T(8,128)(2,1)} %get-tuple-element.341.refs_0_), channel_id=1, source_target_pairs={{0,2},{2,0},{4,6},{6,4},{1,3},{3,1},{5,7},{7,5},{8,10},{10,8},{12,... | collective-permute-start | bytes 3145736 | tf_op jit(solution)/shard_map/ppermute | solution.py:252
  738.7 33.5 %collective-permute-start.49 = (bf16[512,1024]{1,0:T(8,128)(2,1)}, bf16[512,1024]{1,0:T(8,128)(2,1)}, u32[]{:S(2)}, u32[]{:S(2)}) collective-permute-start(bf16[512,1024]{1,0:T(8,128)(2,1)} %get-tuple-element.342.refs_2_), channel_id=1, source_target_pairs={{2,4},{4,2},{3,5},{5,3},{10,12},{12,10},{11,13},{13,11},{18,20},{2... | collective-permute-start | bytes 3145736 | tf_op jit(solution)/shard_map/ppermute | solution.py:250
  805.9 28.7 %collective-permute-start.55 = (bf16[512,1024]{1,0:T(8,128)(2,1)S(1)}, bf16[512,1024]{1,0:T(8,128)(2,1)}, u32[]{:S(2)}, u32[]{:S(2)}) collective-permute-start(bf16[512,1024]{1,0:T(8,128)(2,1)S(1)} %shard_map.273.refs_0_), channel_id=1, source_target_pairs={{0,2},{2,0},{4,6},{6,4},{1,3},{3,1},{5,7},{7,5},{8,10},{10,8},{12,... | collective-permute-start | bytes 3145736 | tf_op jit(solution)/shard_map/ppermute | solution.py:252
  (146 other events, 1669.5 us)

commit v6 on v5

--- a/solution.py
+++ b/solution.py
@@ -306,6 +306,8 @@
         inputs, names = [], []
 
         def take(name, array, block, used):
+            if name == "last":
+                array = pltpu.with_memory_space_constraint(array, pltpu.HBM)
             inputs.append((array, spec(block, used)))
             names.append(name)
 

time: 862 us -> 856 us (level)
  local copies, waits for them, and re-layouts: 143 us -> 126 us
  Pallas kernels: 116 us -> 126 us
    unnamed x227 -> x203, local copies, waits for them, and re-layouts: 54.2 us -> 39.1 us
    pallas_call x17, Pallas kernels: 28.6 us -> 38 us  [combine(): pl.pallas_call(kernel, grid_spec=pltpu.PrefetchScalarGridSpec(num_scalar_...]
  transfers between devices with their start and end apart: 68 -> 68, of which waited for: 29 -> 29; matrix products, arithmetic and copies ran while one was open for 27% -> 27% of each run, Pallas kernels for 11% -> 12%
where the time goes in v6:
time: 856 us; the launch traced here: 842 us
  waiting for transfers between devices  270 us (32%)
  starting transfers between devices  156 us (18%)
  local copies, waits for them, and re-layouts  126 us (15%)
  Pallas kernels  126 us (15%)
  matrix products  95.9 us (11%)
  other arithmetic  66.2 us (8%)
    ppermute x17, waiting for transfers between devices, slot(): lax.ppermute(send, 'rest', [(0, 1), (1, 0), (2, 3), (3, 2)])  159 us
    all_to_all x11, waiting for transfers between devices, exchange(): return lax.all_to_all(blocks, 'group', 0, 0, tiled=True)  59.9 us
    ppermute x17, starting transfers between devices, slot(): lax.ppermute(send, 'rest', [(0, 1), (1, 0), (2, 3), (3, 2)])  53.5 us
    ppermute x25, waiting for transfers between devices, step_to(): return lax.ppermute(value, axis, [(i, i ^ step) for i in range(size)])  51.2 us
    all_to_all x11, starting transfers between devices, exchange(): return lax.all_to_all(blocks, 'group', 0, 0, tiled=True)  50.5 us
    pallas_call x5, Pallas kernels, place(): pl.pallas_call(kernel, grid_spec=pltpu.PrefetchScalarGridSpec(num_scalar_...  46.6 us
    unnamed x203, local copies, waits for them, and re-layouts  39.1 us
    pallas_call x17, Pallas kernels, combine(): pl.pallas_call(kernel, grid_spec=pltpu.PrefetchScalarGridSpec(num_scalar_...  38 us
  transfers between devices with their start and end apart: 68, of which 29 were waited for; matrix products, arithmetic and copies ran while one was open for 27% of the time, Pallas kernels for 12%

profile of v6, /device:TPU:1, one launch (start us, length us, event | category | flops | bytes accessed | tf_op | source)
XLA Modules:
  0.0 842.2 jit_solution(2772162172620499465)
XLA Ops:
  46.9 7.9 collective-permute-done.2
  70.4 9.8 %shard_map.248 = (bf16[1024,256]{1,0:T(8,128)(2,1)S(1)}, bf16[1024,384]{1,0:T(8,128)(2,1)S(1)}, f32[1024,128]{1,0:T(8,128)S(1)}) custom-call(f32[1024,384]{1,0:T(8,128)S(1)} %fusion.39.qkv_ref, f32[1024,128]{1,0:T(8,128)S(1)} %copy-done.10, f32[1024,128]{1,0:T(8,128)S(1)} %get-tuple-element.197.sin_ref, s32[2,512,2]{2,1,0:T(8,128)S(1)} %copy.63.column_ref, ...), custom_call_target="tpu_custom_call" | custom-call | bytes 1 | tf_op jit(solution)/shard_map/pallas_call | solution.py:195
  97.4 8.9 %collective-permute-done.6 = bf16[384,1024]{1,0:T(8,128)(2,1)} collective-permute-done((bf16[384,1024]{1,0:T(8,128)(2,1)S(1)}, bf16[384,1024]{1,0:T(8,128)(2,1)}, u32[]{:S(2)}, u32[]{:S(2)}) %collective-permute-start.6) | collective-permute-done | bytes 786464 | tf_op jit(solution)/shard_map/ppermute | solution.py:58
  106.3 16.9 %collective-permute-done.8 = bf16[384,1024]{1,0:T(8,128)(2,1)} collective-permute-done((bf16[384,1024]{1,0:T(8,128)(2,1)S(1)}, bf16[384,1024]{1,0:T(8,128)(2,1)}, u32[]{:S(2)}, u32[]{:S(2)}) %collective-permute-start.8) | collective-permute-done | bytes 786464 | tf_op jit(solution)/shard_map/ppermute | solution.py:58
  178.1 8.3 collective-permute-done.12
  208.0 18.8 %all-to-all-done.3 = bf16[4,128,2048]{2,1,0:T(8,128)(2,1)} async-done(((bf16[4,128,2048]{2,1,0:T(8,128)(2,1)}), bf16[4,128,2048]{2,1,0:T(8,128)(2,1)}, u32[]{:S(2)}, u32[]{:S(2)}) %all-to-all-start.3) | async-done | bytes 2097184 | tf_op jit(solution)/shard_map/all_to_all | solution.py:62
  236.7 7.8 fusion.45
  244.6 11.1 %multiply_convert_fusion.2 = (bf16[1024,1024]{1,0:T(8,128)(2,1)S(1)}, f32[1024,1024]{1,0:T(8,128)}, f32[1024,1024]{1,0:T(8,128)}) fusion(f32[1024,1024]{1,0:T(8,128)S(1)} %fusion.45, pred[]{:T(512)S(6)} %eq.74, bf16[1024,2048]{1,0:T(8,128)(2,1)S(1)} %constant_dynamic-update-slice_fusion.6, bf16[2048,1024]{1,0:T(8,128)(2,1)} %bitcast.72), kind=kOutput, calls=%fused_computation.22 | convolution fusion | flops 4303355904 | bytes 23068672 | tf_op jit(solution)/shard_map/dot_general | solution.py:32
  266.9 10.8 %multiply_convert_fusion = (bf16[1024,1024]{1,0:T(8,128)(2,1)S(1)}, bf16[1024,1024]{1,0:T(8,128)(2,1)}) fusion(f32[1024,1024]{1,0:T(8,128)} %get-tuple-element.433, f32[1024,1024]{1,0:T(8,128)} %get-tuple-element.496, f32[1024,1024]{1,0:T(8,128)} %copy-done.95, pred[]{:T(512)S(6)} %eq.74, bf16[1024,2048]{1,0:T(8,128)(2,1)S(1)} %pad_maximum_fusion.1, ...), kind=kOutput, calls=%fused_computation.20 | convolution fusion | flops 4309647360 | bytes 25165828 | tf_op jit(solution)/shard_map/dot_general | solution.py:36
  277.7 10.9 %fusion.9 = f32[1024,2048]{1,0:T(8,128)} fusion(bf16[2048,1024]{1,0:T(8,128)(2,1)} %bitcast.72, bf16[1024,1024]{1,0:T(8,128)(2,1)S(1)} %get-tuple-element.243, bf16[1024,1024]{1,0:T(8,128)(2,1)} %get-tuple-element.238, pred[]{:T(512)S(6)} %eq.74), kind=kOutput, calls=%fused_computation.38 | convolution fusion | flops 4296015872 | bytes 16777216 | tf_op jit(solution)/shard_map/dot_general | solution.py:36
  288.6 8.4 convolution_add_fusion
  310.5 7.4 convolution_convert_fusion.1.refs_4_.refs_1_
  317.9 7.5 collective-permute-done.17.refs_0_
  343.0 12.4 %collective-permute-done.19.refs_0_.refs_1_ = bf16[512,1024]{1,0:T(8,128)(2,1)} collective-permute-done((bf16[512,1024]{1,0:T(8,128)(2,1)}, bf16[512,1024]{1,0:T(8,128)(2,1)}, u32[]{:S(2)}, u32[]{:S(2)}) %collective-permute-start.19) | collective-permute-done | bytes 1048608 | tf_op jit(solution)/shard_map/ppermute | solution.py:252
  372.7 18.6 %collective-permute-done.22.refs_0_.refs_3_ = bf16[512,1024]{1,0:T(8,128)(2,1)S(1)} collective-permute-done((bf16[512,1024]{1,0:T(8,128)(2,1)S(1)}, bf16[512,1024]{1,0:T(8,128)(2,1)S(1)}, u32[]{:S(2)}, u32[]{:S(2)}) %collective-permute-start.22) | collective-permute-done | bytes 1048608 | tf_op jit(solution)/shard_map/ppermute | solution.py:252
  411.7 16.8 %collective-permute-done.24.refs_0_.refs_1_ = bf16[512,1024]{1,0:T(8,128)(2,1)S(1)} collective-permute-done((bf16[512,1024]{1,0:T(8,128)(2,1)S(1)}, bf16[512,1024]{1,0:T(8,128)(2,1)S(1)}, u32[]{:S(2)}, u32[]{:S(2)}) %collective-permute-start.24) | collective-permute-done | bytes 1048608 | tf_op jit(solution)/shard_map/ppermute | solution.py:252
  434.3 11.8 %shard_map.255 = bf16[1024,384]{1,0:T(8,128)(2,1)S(1)} custom-call(bf16[1024,384]{1,0:T(8,128)(2,1)S(1)} %copy-done.53, f32[1024,128]{1,0:T(8,128)S(1)} %copy-done.57, bf16[1024,256]{1,0:T(8,128)(2,1)S(1)} %convolution_convert_fusion.5.grad_ref, f32[1024,128]{1,0:T(8,128)S(1)} %copy-done.11, f32[1024,128]{1,0:T(8,128)S(1)} %get-tuple-element.197.sin_ref, ...), custom_call_target="tpu_custom_call" | custom-call | bytes 1 | tf_op jit(solution)/shard_map/pallas_call | solution.py:195
  446.1 10.2 %collective-permute-done.27.refs_0_.refs_3_ = bf16[512,1024]{1,0:T(8,128)(2,1)S(1)} collective-permute-done((bf16[512,1024]{1,0:T(8,128)(2,1)S(1)}, bf16[512,1024]{1,0:T(8,128)(2,1)S(1)}, u32[]{:S(2)}, u32[]{:S(2)}) %collective-permute-start.27) | collective-permute-done | bytes 1048608 | tf_op jit(solution)/shard_map/ppermute | solution.py:252
  474.8 12.8 %collective-permute-done.29.refs_0_.refs_5_ = bf16[512,1024]{1,0:T(8,128)(2,1)S(1)} collective-permute-done((bf16[512,1024]{1,0:T(8,128)(2,1)S(1)}, bf16[512,1024]{1,0:T(8,128)(2,1)S(1)}, u32[]{:S(2)}, u32[]{:S(2)}) %collective-permute-start.29) | collective-permute-done | bytes 1048608 | tf_op jit(solution)/shard_map/ppermute | solution.py:252
  503.0 14.4 %all-to-all-done.6 = bf16[4,128,2048]{2,1,0:T(8,128)(2,1)} async-done(((bf16[4,128,2048]{2,1,0:T(8,128)(2,1)}), bf16[4,128,2048]{2,1,0:T(8,128)(2,1)}, u32[]{:S(2)}, u32[]{:S(2)}) %all-to-all-start.6) | async-done | bytes 2097184 | tf_op jit(solution)/shard_map/all_to_all | solution.py:62
  573.9 13.3 %collective-permute-done.36.refs_0_.refs_3_ = bf16[512,1024]{1,0:T(8,128)(2,1)} collective-permute-done((bf16[512,1024]{1,0:T(8,128)(2,1)}, bf16[512,1024]{1,0:T(8,128)(2,1)}, u32[]{:S(2)}, u32[]{:S(2)}) %collective-permute-start.36) | collective-permute-done | bytes 1048608 | tf_op jit(solution)/shard_map/ppermute | solution.py:252
  597.6 8.9 %fusion.5 = f32[1024,2048]{1,0:T(8,128)} fusion(bf16[1024,1024]{1,0:T(8,128)(2,1)S(1)} %copy-done.91, bf16[2048,2048]{1,0:T(8,128)(2,1)} %param.27, s32[]{:T(128)S(6)} %select_n.289), kind=kOutput, calls=%fused_computation.29 | convolution fusion | flops 4294967296 | bytes 14680068 | tf_op jit(solution)/shard_map/dot_general | solution.py:32
  606.5 9.5 %collective-permute-done.38.refs_0_.refs_5_ = bf16[512,1024]{1,0:T(8,128)(2,1)} collective-permute-done((bf16[512,1024]{1,0:T(8,128)(2,1)}, bf16[512,1024]{1,0:T(8,128)(2,1)}, u32[]{:S(2)}, u32[]{:S(2)}) %collective-permute-start.38) | collective-permute-done | bytes 1048608 | tf_op jit(solution)/shard_map/ppermute | solution.py:252
  629.0 11.6 %shard_map.263 = f32[512,8192]{1,0:T(8,128)} custom-call(s32[40]{0:T(128)S(1)} %reshape.339.table_ref, bf16[4,512,1024]{2,1,0:T(8,128)(2,1)} %all-to-all-done.8.mine_ref, bf16[4,512,1024]{2,1,0:T(8,128)(2,1)} %collective-permute-done.42.other_ref), custom_call_target="tpu_custom_call" | custom-call | bytes 25165824 | tf_op jit(solution)/shard_map/pallas_call | solution.py:400
  640.6 10.4 %collective-permute-done.40.refs_0_.refs_7_ = bf16[512,1024]{1,0:T(8,128)(2,1)} collective-permute-done((bf16[512,1024]{1,0:T(8,128)(2,1)}, bf16[512,1024]{1,0:T(8,128)(2,1)}, u32[]{:S(2)}, u32[]{:S(2)}) %collective-permute-start.40) | collective-permute-done | bytes 1048608 | tf_op jit(solution)/shard_map/ppermute | solution.py:252
  672.4 8.3 collective-permute-done.43.refs_0_.refs_5_
  695.5 18.6 %collective-permute-done.45.refs_0_.refs_7_ = bf16[512,1024]{1,0:T(8,128)(2,1)S(1)} collective-permute-done((bf16[512,1024]{1,0:T(8,128)(2,1)S(1)}, bf16[512,1024]{1,0:T(8,128)(2,1)S(1)}, u32[]{:S(2)}, u32[]{:S(2)}) %collective-permute-start.45) | collective-permute-done | bytes 1048608 | tf_op jit(solution)/shard_map/ppermute | solution.py:252
  740.5 9.7 %all-to-all-done.10 = bf16[4,128,2048]{2,1,0:T(8,128)(2,1)} async-done(((bf16[4,128,2048]{2,1,0:T(8,128)(2,1)}), bf16[4,128,2048]{2,1,0:T(8,128)(2,1)}, u32[]{:S(2)}, u32[]{:S(2)}) %all-to-all-start.10) | async-done | bytes 2097184 | tf_op jit(solution)/shard_map/all_to_all | solution.py:62
  754.6 11.6 %shard_map.268 = f32[512,8192]{1,0:T(8,128)} custom-call(s32[40]{0:T(128)S(1)} %reshape.339.table_ref, bf16[4,512,1024]{2,1,0:T(8,128)(2,1)} %all-to-all-done.9.mine_ref, bf16[4,512,1024]{2,1,0:T(8,128)(2,1)} %collective-permute-done.50.other_ref), custom_call_target="tpu_custom_call" | custom-call | bytes 25165824 | tf_op jit(solution)/shard_map/pallas_call | solution.py:400
  774.2 11.6 %shard_map.271 = f32[2048,2048]{1,0:T(8,128)} custom-call(s32[40]{0:T(128)S(1)} %reshape.342.table_ref, bf16[4,512,1024]{2,1,0:T(8,128)(2,1)} %shard_map.270.mine_ref, bf16[4,512,1024]{2,1,0:T(8,128)(2,1)} %collective-permute-done.53.other_ref), custom_call_target="tpu_custom_call" | custom-call | bytes 25165824 | tf_op jit(solution)/shard_map/pallas_call | solution.py:400
  785.8 9.0 %collective-permute-done.51.refs_3_ = bf16[512,1024]{1,0:T(8,128)(2,1)} collective-permute-done((bf16[512,1024]{1,0:T(8,128)(2,1)}, bf16[512,1024]{1,0:T(8,128)(2,1)}, u32[]{:S(2)}, u32[]{:S(2)}) %collective-permute-start.51) | collective-permute-done | bytes 1048608 | tf_op jit(solution)/shard_map/ppermute | solution.py:252
  819.9 8.7 %collective-permute-done.55.refs_1_ = bf16[512,1024]{1,0:T(8,128)(2,1)} collective-permute-done((bf16[512,1024]{1,0:T(8,128)(2,1)S(1)}, bf16[512,1024]{1,0:T(8,128)(2,1)}, u32[]{:S(2)}, u32[]{:S(2)}) %collective-permute-start.55) | collective-permute-done | bytes 1048608 | tf_op jit(solution)/shard_map/ppermute | solution.py:252
  (477 shorter events, 477.2 us)
Async XLA Ops:
  4.3 39.4 %all-to-all-start = ((bf16[4,144,2048]{2,1,0:T(8,128)(2,1)}), bf16[4,144,2048]{2,1,0:T(8,128)(2,1)}, u32[]{:S(2)}, u32[]{:S(2)}) async-start(bf16[4,144,2048]{2,1,0:T(8,128)(2,1)} %broadcast_in_dim.57), calls=%async_computation | async-start | bytes 4718592 | tf_op jit(solution)/shard_map/all_to_all | solution.py:62
  14.7 32.2 %collective-permute-start = (bf16[512,384]{1,0:T(8,128)(2,1)}, bf16[512,384]{1,0:T(8,128)(2,1)S(1)}, u32[]{:S(2)}, u32[]{:S(2)}) collective-permute-start(bf16[512,384]{1,0:T(8,128)(2,1)} %get-tuple-element.470), channel_id=1, source_target_pairs={{0,8},{8,0},{16,24},{24,16},{1,9},{9,1},{17,25},{25,17},{2,10},{10... | collective-permute-start | bytes 1179656 | tf_op jit(solution)/shard_map/ppermute | solution.py:58
  16.7 30.2 %collective-permute-start.1 = (bf16[512,384]{1,0:T(8,128)(2,1)}, bf16[512,384]{1,0:T(8,128)(2,1)S(1)}, u32[]{:S(2)}, u32[]{:S(2)}) collective-permute-start(bf16[512,384]{1,0:T(8,128)(2,1)} %get-tuple-element.469), channel_id=1, source_target_pairs={{0,16},{8,24},{16,0},{24,8},{1,17},{9,25},{17,1},{25,9},{2,18},{10... | collective-permute-start | bytes 1179656 | tf_op jit(solution)/shard_map/ppermute | solution.py:58
  17.9 36.9 %collective-permute-start.2 = (bf16[512,384]{1,0:T(8,128)(2,1)}, bf16[512,384]{1,0:T(8,128)(2,1)}, u32[]{:S(2)}, u32[]{:S(2)}) collective-permute-start(bf16[512,384]{1,0:T(8,128)(2,1)} %get-tuple-element.468), channel_id=1, source_target_pairs={{0,24},{8,16},{16,8},{24,0},{1,25},{9,17},{17,9},{25,1},{2,26},{10... | collective-permute-start | bytes 1179656 | tf_op jit(solution)/shard_map/ppermute | solution.py:58
  88.2 35.0 %collective-permute-start.8 = (bf16[384,1024]{1,0:T(8,128)(2,1)S(1)}, bf16[384,1024]{1,0:T(8,128)(2,1)}, u32[]{:S(2)}, u32[]{:S(2)}) collective-permute-start(bf16[384,1024]{1,0:T(8,128)(2,1)S(1)} %get-tuple-element.450), channel_id=1, source_target_pairs={{0,24},{8,16},{16,8},{24,0},{1,25},{9,17},{17,9},{25,1},{2,26},{10... | collective-permute-start | bytes 2359304 | tf_op jit(solution)/shard_map/ppermute | solution.py:58
  123.2 28.8 %all-to-all-start.1 = ((bf16[4,128,2048]{2,1,0:T(8,128)(2,1)}), bf16[4,128,2048]{2,1,0:T(8,128)(2,1)}, u32[]{:S(2)}, u32[]{:S(2)}) async-start(bf16[4,128,2048]{2,1,0:T(8,128)(2,1)} %bitcast.223), calls=%async_computation.1 | async-start | bytes 4194304 | tf_op jit(solution)/shard_map/all_to_all | solution.py:62
  129.7 27.0 %collective-permute-start.9 = (bf16[128,1024]{1,0:T(8,128)(2,1)}, bf16[128,1024]{1,0:T(8,128)(2,1)S(1)}, u32[]{:S(2)}, u32[]{:S(2)}) collective-permute-start(bf16[128,1024]{1,0:T(8,128)(2,1)} %get-tuple-element.475), channel_id=1, source_target_pairs={{0,8},{8,0},{16,24},{24,16},{1,9},{9,1},{17,25},{25,17},{2,10},{10... | collective-permute-start | bytes 786440 | tf_op jit(solution)/shard_map/ppermute | solution.py:58
  131.1 26.7 %collective-permute-start.10 = (bf16[128,1024]{1,0:T(8,128)(2,1)}, bf16[128,1024]{1,0:T(8,128)(2,1)}, u32[]{:S(2)}, u32[]{:S(2)}) collective-permute-start(bf16[128,1024]{1,0:T(8,128)(2,1)} %get-tuple-element.474), channel_id=1, source_target_pairs={{0,16},{8,24},{16,0},{24,8},{1,17},{9,25},{17,1},{25,9},{2,18},{10... | collective-permute-start | bytes 786440 | tf_op jit(solution)/shard_map/ppermute | solution.py:58
  132.3 30.9 %collective-permute-start.11 = (bf16[128,1024]{1,0:T(8,128)(2,1)}, bf16[128,1024]{1,0:T(8,128)(2,1)}, u32[]{:S(2)}, u32[]{:S(2)}) collective-permute-start(bf16[128,1024]{1,0:T(8,128)(2,1)} %get-tuple-element.473), channel_id=1, source_target_pairs={{0,24},{8,16},{16,8},{24,0},{1,25},{9,17},{17,9},{25,1},{2,26},{10... | collective-permute-start | bytes 786440 | tf_op jit(solution)/shard_map/ppermute | solution.py:58
  135.7 50.7 %collective-permute-start.12 = (bf16[3,384,1024]{2,1,0:T(8,128)(2,1)}, bf16[3,384,1024]{2,1,0:T(8,128)(2,1)}, u32[]{:S(2)}, u32[]{:S(2)}) collective-permute-start(bf16[3,384,1024]{2,1,0:T(8,128)(2,1)} %pad_maximum_fusion.2), channel_id=1, source_target_pairs={{0,2},{2,0},{4,6},{6,4},{1,3},{3,1},{5,7},{7,5},{8,10},{10,8},{12,... | collective-permute-start | bytes 7077896 | tf_op jit(solution)/shard_map/ppermute | solution.py:58
  166.1 28.8 %all-to-all-start.2 = ((bf16[4,128,2048]{2,1,0:T(8,128)(2,1)}), bf16[4,128,2048]{2,1,0:T(8,128)(2,1)}, u32[]{:S(2)}, u32[]{:S(2)}) async-start(bf16[4,128,2048]{2,1,0:T(8,128)(2,1)} %broadcast_in_dim.71), calls=%async_computation.2 | async-start | bytes 4194304 | tf_op jit(solution)/shard_map/all_to_all | solution.py:62
  172.5 34.0 %collective-permute-start.13 = (bf16[3,128,1024]{2,1,0:T(8,128)(2,1)}, bf16[3,128,1024]{2,1,0:T(8,128)(2,1)}, u32[]{:S(2)}, u32[]{:S(2)}) collective-permute-start(bf16[3,128,1024]{2,1,0:T(8,128)(2,1)} %pad_maximum_fusion.5), channel_id=1, source_target_pairs={{0,2},{2,0},{4,6},{6,4},{1,3},{3,1},{5,7},{7,5},{8,10},{10,8},{12,... | collective-permute-start | bytes 2359304 | tf_op jit(solution)/shard_map/ppermute | solution.py:58
  197.5 29.3 %all-to-all-start.3 = ((bf16[4,128,2048]{2,1,0:T(8,128)(2,1)}), bf16[4,128,2048]{2,1,0:T(8,128)(2,1)}, u32[]{:S(2)}, u32[]{:S(2)}) async-start(bf16[4,128,2048]{2,1,0:T(8,128)(2,1)} %broadcast_in_dim.72), calls=%async_computation.3 | async-start | bytes 4194304 | tf_op jit(solution)/shard_map/all_to_all | solution.py:62
  206.5 28.5 %collective-permute-start.14 = (bf16[512,2048]{1,0:T(8,128)(2,1)}, bf16[512,2048]{1,0:T(8,128)(2,1)}, u32[]{:S(2)}, u32[]{:S(2)}) collective-permute-start(bf16[512,2048]{1,0:T(8,128)(2,1)} %bitcast.66), channel_id=1, source_target_pairs={{0,1},{1,0},{2,3},{3,2},{4,5},{5,4},{6,7},{7,6},{8,9},{9,8},{10,11... | collective-permute-start | bytes 6291464 | tf_op jit(solution)/shard_map/ppermute | solution.py:58
  226.8 28.9 %collective-permute-start.15 = (bf16[512,2048]{1,0:T(8,128)(2,1)}, bf16[512,2048]{1,0:T(8,128)(2,1)S(1)}, u32[]{:S(2)}, u32[]{:S(2)}) collective-permute-start(bf16[512,2048]{1,0:T(8,128)(2,1)} %bitcast.74), channel_id=1, source_target_pairs={{0,1},{1,0},{2,3},{3,2},{4,5},{5,4},{6,7},{7,6},{8,9},{9,8},{10,11... | collective-permute-start | bytes 6291464 | tf_op jit(solution)/shard_map/ppermute | solution.py:58
  265.4 31.7 %collective-permute-start.16 = (bf16[512,1024]{1,0:T(8,128)(2,1)S(1)}, bf16[512,1024]{1,0:T(8,128)(2,1)S(1)}, u32[]{:S(2)}, u32[]{:S(2)}) collective-permute-start(bf16[512,1024]{1,0:T(8,128)(2,1)S(1)} %shard_map.249), channel_id=1, source_target_pairs={{0,2},{2,0},{4,6},{6,4},{1,3},{3,1},{5,7},{7,5},{8,10},{10,8},{12,... | collective-permute-start | bytes 3145736 | tf_op jit(solution)/shard_map/ppermute | solution.py:252
  305.8 35.0 %all-to-all-start.4 = ((bf16[4,128,2048]{2,1,0:T(8,128)(2,1)}), bf16[4,128,2048]{2,1,0:T(8,128)(2,1)}, u32[]{:S(2)}, u32[]{:S(2)}) async-start(bf16[4,128,2048]{2,1,0:T(8,128)(2,1)} %bitcast.225), calls=%async_computation.4 | async-start | bytes 4194304 | tf_op jit(solution)/shard_map/all_to_all | solution.py:62
  328.3 27.1 %collective-permute-start.19 = (bf16[512,1024]{1,0:T(8,128)(2,1)}, bf16[512,1024]{1,0:T(8,128)(2,1)}, u32[]{:S(2)}, u32[]{:S(2)}) collective-permute-start(bf16[512,1024]{1,0:T(8,128)(2,1)} %get-tuple-element.240.refs_0_), channel_id=1, source_target_pairs={{0,2},{2,0},{4,6},{6,4},{1,3},{3,1},{5,7},{7,5},{8,10},{10,8},{12,... | collective-permute-start | bytes 3145736 | tf_op jit(solution)/shard_map/ppermute | solution.py:252
  359.8 33.5 %all-to-all-start.5 = ((bf16[4,128,2048]{2,1,0:T(8,128)(2,1)}), bf16[4,128,2048]{2,1,0:T(8,128)(2,1)}, u32[]{:S(2)}, u32[]{:S(2)}) async-start(bf16[4,128,2048]{2,1,0:T(8,128)(2,1)} %broadcast_in_dim.75), calls=%async_computation.5 | async-start | bytes 4194304 | tf_op jit(solution)/shard_map/all_to_all | solution.py:62
  401.3 27.3 %collective-permute-start.24 = (bf16[512,1024]{1,0:T(8,128)(2,1)S(1)}, bf16[512,1024]{1,0:T(8,128)(2,1)S(1)}, u32[]{:S(2)}, u32[]{:S(2)}) collective-permute-start(bf16[512,1024]{1,0:T(8,128)(2,1)S(1)} %get-tuple-element.258.refs_0_), channel_id=1, source_target_pairs={{0,2},{2,0},{4,6},{6,4},{1,3},{3,1},{5,7},{7,5},{8,10},{10,8},{12,... | collective-permute-start | bytes 3145736 | tf_op jit(solution)/shard_map/ppermute | solution.py:252
  430.4 25.9 %collective-permute-start.27 = (bf16[512,1024]{1,0:T(8,128)(2,1)S(1)}, bf16[512,1024]{1,0:T(8,128)(2,1)S(1)}, u32[]{:S(2)}, u32[]{:S(2)}) collective-permute-start(bf16[512,1024]{1,0:T(8,128)(2,1)S(1)} %get-tuple-element.266.refs_2_), channel_id=1, source_target_pairs={{0,2},{2,0},{4,6},{6,4},{1,3},{3,1},{5,7},{7,5},{8,10},{10,8},{12,... | collective-permute-start | bytes 3145736 | tf_op jit(solution)/shard_map/ppermute | solution.py:252
  488.6 28.8 %all-to-all-start.6 = ((bf16[4,128,2048]{2,1,0:T(8,128)(2,1)}), bf16[4,128,2048]{2,1,0:T(8,128)(2,1)}, u32[]{:S(2)}, u32[]{:S(2)}) async-start(bf16[4,128,2048]{2,1,0:T(8,128)(2,1)} %bitcast.226), calls=%async_computation.6 | async-start | bytes 4194304 | tf_op jit(solution)/shard_map/all_to_all | solution.py:62
  550.7 55.8 %all-to-all-start.8 = ((bf16[4,512,1024]{2,1,0:T(8,128)(2,1)}), bf16[4,512,1024]{2,1,0:T(8,128)(2,1)}, u32[]{:S(2)}, u32[]{:S(2)}) async-start(bf16[4,512,1024]{2,1,0:T(8,128)(2,1)} %copy-done.5), calls=%async_computation.8 | async-start | bytes 8388608 | tf_op jit(solution)/shard_map/all_to_all | solution.py:62
  623.4 27.7 %collective-permute-start.40 = (bf16[512,1024]{1,0:T(8,128)(2,1)}, bf16[512,1024]{1,0:T(8,128)(2,1)}, u32[]{:S(2)}, u32[]{:S(2)}) collective-permute-start(bf16[512,1024]{1,0:T(8,128)(2,1)} %get-tuple-element.316.refs_6_), channel_id=1, source_target_pairs={{0,2},{2,0},{4,6},{6,4},{1,3},{3,1},{5,7},{7,5},{8,10},{10,8},{12,... | collective-permute-start | bytes 3145736 | tf_op jit(solution)/shard_map/ppermute | solution.py:252
  654.0 26.7 %collective-permute-start.43 = (bf16[512,1024]{1,0:T(8,128)(2,1)}, bf16[512,1024]{1,0:T(8,128)(2,1)}, u32[]{:S(2)}, u32[]{:S(2)}) collective-permute-start(bf16[512,1024]{1,0:T(8,128)(2,1)} %get-tuple-element.325.refs_4_), channel_id=1, source_target_pairs={{0,2},{2,0},{4,6},{6,4},{1,3},{3,1},{5,7},{7,5},{8,10},{10,8},{12,... | collective-permute-start | bytes 3145736 | tf_op jit(solution)/shard_map/ppermute | solution.py:252
  667.5 51.8 %all-to-all-start.9 = ((bf16[4,512,1024]{2,1,0:T(8,128)(2,1)}), bf16[4,512,1024]{2,1,0:T(8,128)(2,1)}, u32[]{:S(2)}, u32[]{:S(2)}) async-start(bf16[4,512,1024]{2,1,0:T(8,128)(2,1)} %copy-done.6), calls=%async_computation.9 | async-start | bytes 8388608 | tf_op jit(solution)/shard_map/all_to_all | solution.py:62
  686.3 27.8 %collective-permute-start.45 = (bf16[512,1024]{1,0:T(8,128)(2,1)S(1)}, bf16[512,1024]{1,0:T(8,128)(2,1)S(1)}, u32[]{:S(2)}, u32[]{:S(2)}) collective-permute-start(bf16[512,1024]{1,0:T(8,128)(2,1)S(1)} %get-tuple-element.332.refs_6_), channel_id=1, source_target_pairs={{0,2},{2,0},{4,6},{6,4},{1,3},{3,1},{5,7},{7,5},{8,10},{10,8},{12,... | collective-permute-start | bytes 3145736 | tf_op jit(solution)/shard_map/ppermute | solution.py:252
  719.3 35.3 %collective-permute-start.50 = (bf16[4,512,1024]{2,1,0:T(8,128)(2,1)}, bf16[4,512,1024]{2,1,0:T(8,128)(2,1)}, u32[]{:S(2)}, u32[]{:S(2)}) collective-permute-start(bf16[4,512,1024]{2,1,0:T(8,128)(2,1)} %all-to-all-done.9.mine_ref), channel_id=1, source_target_pairs={{0,1},{1,0},{2,3},{3,2},{4,5},{5,4},{6,7},{7,6},{8,9},{9,8},{10,11... | collective-permute-start | bytes 12582920 | tf_op jit(solution)/shard_map/ppermute | solution.py:58
  720.7 29.6 %all-to-all-start.10 = ((bf16[4,128,2048]{2,1,0:T(8,128)(2,1)}), bf16[4,128,2048]{2,1,0:T(8,128)(2,1)}, u32[]{:S(2)}, u32[]{:S(2)}) async-start(bf16[4,128,2048]{2,1,0:T(8,128)(2,1)} %bitcast.224), calls=%async_computation.10 | async-start | bytes 4194304 | tf_op jit(solution)/shard_map/all_to_all | solution.py:62
  731.5 34.7 %collective-permute-start.48 = (bf16[512,1024]{1,0:T(8,128)(2,1)}, bf16[512,1024]{1,0:T(8,128)(2,1)S(1)}, u32[]{:S(2)}, u32[]{:S(2)}) collective-permute-start(bf16[512,1024]{1,0:T(8,128)(2,1)} %get-tuple-element.341.refs_0_), channel_id=1, source_target_pairs={{0,2},{2,0},{4,6},{6,4},{1,3},{3,1},{5,7},{7,5},{8,10},{10,8},{12,... | collective-permute-start | bytes 3145736 | tf_op jit(solution)/shard_map/ppermute | solution.py:252
  732.6 33.6 %collective-permute-start.49 = (bf16[512,1024]{1,0:T(8,128)(2,1)}, bf16[512,1024]{1,0:T(8,128)(2,1)}, u32[]{:S(2)}, u32[]{:S(2)}) collective-permute-start(bf16[512,1024]{1,0:T(8,128)(2,1)} %get-tuple-element.342.refs_2_), channel_id=1, source_target_pairs={{2,4},{4,2},{3,5},{5,3},{10,12},{12,10},{11,13},{13,11},{18,20},{2... | collective-permute-start | bytes 3145736 | tf_op jit(solution)/shard_map/ppermute | solution.py:250
  801.1 27.5 %collective-permute-start.55 = (bf16[512,1024]{1,0:T(8,128)(2,1)S(1)}, bf16[512,1024]{1,0:T(8,128)(2,1)}, u32[]{:S(2)}, u32[]{:S(2)}) collective-permute-start(bf16[512,1024]{1,0:T(8,128)(2,1)S(1)} %shard_map.273.refs_0_), channel_id=1, source_target_pairs={{0,2},{2,0},{4,6},{6,4},{1,3},{3,1},{5,7},{7,5},{8,10},{10,8},{12,... | collective-permute-start | bytes 3145736 | tf_op jit(solution)/shard_map/ppermute | solution.py:252
  (134 other events, 1707.7 us)
